TPU v7x, 128 devices: a whole 4x4x4 slice. The times are simulated.
128 devices in a mesh: lon: 8 (over z, x_lo), lat: 16 (over x_hi, y, core).
Axes of the slice: x: 4 (x_hi: 2, x_lo: 2; x = x_hi * 2 + x_lo), y: 4, z: 4, core: 2. Of those that a mesh axis runs over, the one named last changes fastest.
Arguments:
- flux_probes: float32 [192, 288, 64], P('lat', 'lon'), may hold values from -6 to 6
- conc_start: float32 [192, 288, 47, 64], P('lat', 'lon'), may hold values from -6 to 6
- u_courant: float32 [192, 288, 47], P('lat', 'lon'), may hold values from -0.45 to 0.45
- v_courant: float32 [192, 288, 47], P('lat', 'lon'), may hold values from -0.45 to 0.45
- vert_mix: float32 [192, 288, 47], P('lat', 'lon'), may hold values from 0.02 to 0.24
- obs_cell: int32 [131072], P(('lon', 'lat')), may hold values from 0 to 20303
- obs_weight: float32 [131072], P(('lon', 'lat')), may hold values from 0.3 to 3
- obs_count: int32 [128], P(('lon', 'lat')), may hold values from 341 to 1024, as said below
Outputs:
- basis: float32 [131072, 64], P(('lon', 'lat'))
- factor: float32 [64, 64], replicated
Inputs may be any that keep to these rules, and one draw needn't show every extreme that they name: `obs_count`: each device's number of live slots; some device has exactly 1024.
All inputs are finite; a program needn't handle non-finite values.
Results may differ from a plain program's by a relative error of at most 0.0003.
Values sent between devices are 32-bit elements; how exact they have to be, the bound alone decides.
No kernel may reach another device: no remote copies, remote signals or barrier semaphores. Data moves between devices by JAX's collectives and lax.ppermute only.
A program may use at most 192 MiB of HBM per device.

v0:
```python
import jax
import jax.numpy as jnp
from jax import lax
from jax.sharding import PartitionSpec as P

STEPS = 4


def padded_2(x, sides, width, wrap):
    for axis, dim in sides:
        size, length = (lax.axis_size(axis), x.shape[dim])
        up = [(i, (i + 1) % size) for i in range(size if wrap else size - 1)]
        down = [(j, i) for i, j in up]
        last = lax.slice_in_dim(x, length - width, length, axis=dim)
        leading = lax.slice_in_dim(x, 0, width, axis=dim)
        before = lax.ppermute(last, axis, up)
        after = lax.ppermute(leading, axis, down)
        x = jnp.concatenate([before, x, after], axis=dim)
    return x


def shifted(block, axis, distance):
    devices = range(lax.axis_size(axis))
    route = [((i - distance) % len(devices), i) for i in devices]
    return lax.ppermute(block, axis, route)


def from_behind(value, axis, steps):
    count = lax.axis_size(axis)
    leading, last = (max(0, -steps), min(count, count - steps))
    return lax.ppermute(value, axis, [(source, source + steps) for source in range(leading, last)])


def advance(padded, u_pad, v_pad, mix_pad):
    conc = padded[1:-1, 1:-1]
    west = padded[1:-1, :-2]
    east = padded[1:-1, 2:]
    south = padded[:-2, 1:-1]
    north = padded[2:, 1:-1]
    u_face = u_pad[1:-1, 1:-1]
    u_east = u_pad[1:-1, 2:]
    v_face = v_pad[1:-1, 1:-1]
    v_north = v_pad[2:, 1:-1]
    mixing = mix_pad[1:-1, 1:-1]
    flux_w = jnp.maximum(u_face, 0.0) * west + jnp.minimum(u_face, 0.0) * conc
    flux_e = jnp.maximum(u_east, 0.0) * conc + jnp.minimum(u_east, 0.0) * east
    flux_s = jnp.maximum(v_face, 0.0) * south + jnp.minimum(v_face, 0.0) * conc
    flux_n = jnp.maximum(v_north, 0.0) * conc + jnp.minimum(v_north, 0.0) * north
    advected = conc + flux_w - flux_e + flux_s - flux_n
    mixed = mixing[:, :, :-1] * (advected[:, :, 1:] - advected[:, :, :-1])
    zero_lev = jnp.zeros_like(mixed[:, :, :1])
    return (
        advected
        + jnp.concatenate([mixed, zero_lev], axis=2)
        - jnp.concatenate([zero_lev, mixed], axis=2)
    )


def pad_field(conc):
    beside_all = padded_2(conc, (("lon", 1),), 1, True)
    return padded_2(beside_all, (("lat", 0),), 1, False)


def highest_dot(left, right):
    return jnp.dot(left, right, precision=lax.Precision.HIGHEST, preferred_element_type=jnp.float32)


def on_device(
    flux_probes, conc_start, u_courant, v_courant, vert_mix, obs_cell, obs_weight, obs_count
):
    lat_rows, lon_cols, levels = u_courant.shape
    probes = flux_probes.shape[2]
    steps = STEPS
    east_col = shifted(u_courant[:, :1, :], "lon", -1)
    north_row = from_behind(v_courant[:1, :, :], "lat", -1)
    u_wide = jnp.concatenate([u_courant, east_col], axis=1)
    u_pad = jnp.pad(u_wide, ((1, 1), (1, 0), (0, 0)))[:, :, :, None]
    v_tall = jnp.concatenate([v_courant, north_row], axis=0)
    v_pad = jnp.pad(v_tall, ((1, 0), (1, 1), (0, 0)))[:, :, :, None]
    mix_pad = jnp.pad(vert_mix, ((1, 1), (1, 1), (0, 0)))[:, :, :, None]
    conc = conc_start
    for step in range(steps):
        conc = conc.at[:, :, 0, :].add(flux_probes)
        conc = advance(pad_field(conc), u_pad, v_pad, mix_pad)
    band_cells = lon_cols * levels
    banded = conc.reshape(lat_rows, band_cells, probes)
    slots = obs_cell.shape[0]
    cell_ids = jnp.arange(band_cells, dtype=jnp.int32)

    def pick_band(band, total):
        local = obs_cell - band * band_cells
        onehot = (local[:, None] == cell_ids[None, :]).astype(jnp.float32)
        piece = lax.dynamic_index_in_dim(banded, band, 0, keepdims=False)
        return total + highest_dot(onehot, piece)

    picked = lax.fori_loop(0, lat_rows, pick_band, jnp.zeros((slots, probes), jnp.float32))
    live = jnp.arange(slots, dtype=jnp.int32) < obs_count[0]
    scale = jnp.where(live, obs_weight, 0.0)
    images = picked * scale[:, None]
    partial_gram = highest_dot(images.T, images)
    gram = lax.psum(partial_gram, ("lon", "lat"))
    column_ids = jnp.arange(probes, dtype=jnp.int32)
    remaining = gram
    upper = jnp.zeros((probes, probes), jnp.float32)
    for column in range(probes):
        pivot = jnp.sqrt(remaining[column, column])
        row_vals = jnp.where(column_ids >= column, remaining[column, :] / pivot, 0.0)
        upper = upper.at[column].set(row_vals)
        remaining = remaining - row_vals[:, None] * row_vals[None, :]
    inverse = jnp.zeros((probes, probes), jnp.float32)
    identity = jnp.eye(probes, dtype=jnp.float32)
    for row in range(probes - 1, -1, -1):
        rhs = identity[row] - highest_dot(upper[row][None, :], inverse)[0]
        inverse = inverse.at[row].set(rhs / upper[row, row])
    total_rows = slots * lax.axis_size("lon") * lax.axis_size("lat")
    root = jnp.sqrt(jnp.float32(total_rows))
    return (highest_dot(images, inverse) * root, upper / root)


def solution(mesh):
    in_specs = (
        P("lat", "lon", None),
        P("lat", "lon", None, None),
        P("lat", "lon", None),
        P("lat", "lon", None),
        P("lat", "lon", None),
        P(("lon", "lat")),
        P(("lon", "lat")),
        P(("lon", "lat")),
    )
    out_specs = (P(("lon", "lat"), None), P())
    return jax.shard_map(
        on_device, mesh=mesh, in_specs=in_specs, out_specs=out_specs, check_vma=False
    )
```

profile of v0, /device:TPU:0, one launch (start us, length us, event | category | flops | bytes accessed | tf_op | source)
XLA Modules:
  0.0 802.7 jit_solution(15084779175674584533)
XLA Ops:
  0.7 7.5 copy.23
  8.2 4.3 copy-done.1
  14.7 3.6 collective-permute-start.2
  23.3 6.1 collective-permute-done
  29.5 2.0 pad_maximum_fusion.43
  33.5 2.2 collective-permute-start.4
  46.0 33.2 %fusion.46 = f32[12,36,47,64]{3,1,0,2:T(8,128)S(1)} fusion(f32[1,38,47,64]{3,1,0,2:T(8,128)S(1)} %copy.35, f32[12,1,47,64]{3,1,0,2:T(1,128)} %copy-done.15, f32[12,36,47,64]{3,1,0,2:T(8,128)} %copy-done.1, f32[12,1,47,64]{3,1,0,2:T(1,128)} %copy-done.13, f32[1,38,47,64]{3,1,0,2:T(8,128)S(1)} %copy.30, f32[12,36,47]{1,0,2:T(8,128)S(1)} %copy.33, ...), kind=kLoop, calls=%fused_computation.72 | loop fusion | flops 31186944 | bytes 12248576 | tf_op jit(solution)/shard_map/sub | solution.py:49
  79.2 6.8 fusion.59
  86.1 30.8 %pad_subtract_fusion.3 = f32[12,36,47,64]{3,1,0,2:T(8,128)S(1)} fusion(f32[12,36,46,64]{3,1,0,2:T(8,128)} %fusion.59, f32[1,38,47,64]{3,1,0,2:T(8,128)S(1)} %copy.35, f32[12,1,47,64]{3,1,0,2:T(1,128)S(1)} %copy-done.16, f32[12,36,47,64]{3,1,0,2:T(8,128)S(1)} %bitcast.1636, f32[12,1,47,64]{3,1,0,2:T(1,128)S(1)} %copy-done.14, f32[12,36,47]{1,0,2:T(8,128)S(1)} %copy.33, ...), kind=kLoop, calls=%fused_computation.92 | loop fusion | flops 33785856 | bytes 17335808 | tf_op jit(solution)/shard_map/sub | solution.py:53
  119.1 2.6 collective-permute-start.7
  121.7 4.6 collective-permute-done.6
  126.3 2.3 collective-permute-done.7
  130.0 10.0 %collective-permute-start.8 = (f32[1,38,47,64]{3,0,2,1:T(1,128)S(1)}, f32[1,38,47,64]{3,0,2,1:T(1,128)S(1)}, u32[]{:S(2)}, u32[]{:S(2)}) collective-permute-start(f32[1,38,47,64]{3,0,2,1:T(1,128)S(1)} %copy.37), channel_id=1, source_target_pairs={{0,1},{1,2},{2,3},{3,4},{4,5},{5,6},{6,7},{7,8},{8,9},{9,10},{10,1... | collective-permute-start | bytes 1371656 | tf_op jit(solution)/shard_map/ppermute | solution.py:16
  142.3 8.7 %collective-permute-done.9 = f32[1,38,47,64]{3,0,2,1:T(1,128)S(1)} collective-permute-done((f32[1,38,47,64]{3,0,2,1:T(1,128)S(1)}, f32[1,38,47,64]{3,0,2,1:T(1,128)S(1)}, u32[]{:S(2)}, u32[]{:S(2)}) %collective-permute-start.9) | collective-permute-done | bytes 457248 | tf_op jit(solution)/shard_map/ppermute | solution.py:17
  151.1 28.2 %fusion.34 = f32[12,36,47,64]{3,1,0,2:T(8,128)S(1)} fusion(f32[1,38,47,64]{3,1,0,2:T(8,128)S(1)} %copy.40, f32[12,1,47,64]{3,1,0,2:T(1,128)S(1)} %collective-permute-done.7, f32[12,36,47,64]{3,1,0,2:T(8,128)S(1)} %fusion.267, f32[12,1,47,64]{3,1,0,2:T(1,128)S(1)} %collective-permute-done.6, f32[1,38,47,64]{3,1,0,2:T(8,128)S(1)} %copy.38, ...), kind=kLoop, calls=%fused_computation.52 | loop fusion | flops 31186944 | bytes 12248576 | tf_op jit(solution)/shard_map/sub | solution.py:49
  179.4 6.9 fusion.58
  186.3 30.8 %pad_subtract_fusion.2 = f32[12,36,47,64]{3,1,0,2:T(8,128)S(1)} fusion(f32[12,36,46,64]{3,1,0,2:T(8,128)} %fusion.58, f32[1,38,47,64]{3,1,0,2:T(8,128)S(1)} %copy.40, f32[12,1,47,64]{3,1,0,2:T(1,128)S(1)} %collective-permute-done.7, f32[12,36,47,64]{3,1,0,2:T(8,128)S(1)} %fusion.267, f32[12,1,47,64]{3,1,0,2:T(1,128)S(1)} %collective-permute-done.6, ...), kind=kLoop, calls=%fused_computation.91 | loop fusion | flops 33785856 | bytes 17335808 | tf_op jit(solution)/shard_map/sub | solution.py:53
  219.2 3.0 collective-permute-start.11
  222.2 4.2 collective-permute-done.10
  226.5 2.0 collective-permute-done.11
  229.8 11.6 %collective-permute-start.12 = (f32[1,38,47,64]{3,0,2,1:T(1,128)S(1)}, f32[1,38,47,64]{3,0,2,1:T(1,128)S(1)}, u32[]{:S(2)}, u32[]{:S(2)}) collective-permute-start(f32[1,38,47,64]{3,0,2,1:T(1,128)S(1)} %copy.41), channel_id=1, source_target_pairs={{0,1},{1,2},{2,3},{3,4},{4,5},{5,6},{6,7},{7,8},{8,9},{9,10},{10,1... | collective-permute-start | bytes 1371656 | tf_op jit(solution)/shard_map/ppermute | solution.py:16
  243.8 8.3 %collective-permute-done.13 = f32[1,38,47,64]{3,0,2,1:T(1,128)S(1)} collective-permute-done((f32[1,38,47,64]{3,0,2,1:T(1,128)S(1)}, f32[1,38,47,64]{3,0,2,1:T(1,128)S(1)}, u32[]{:S(2)}, u32[]{:S(2)}) %collective-permute-start.13) | collective-permute-done | bytes 457248 | tf_op jit(solution)/shard_map/ppermute | solution.py:17
  252.3 28.2 %fusion.22 = f32[12,36,47,64]{3,1,0,2:T(8,128)S(1)} fusion(f32[1,38,47,64]{3,1,0,2:T(8,128)S(1)} %copy.44, f32[12,1,47,64]{3,1,0,2:T(1,128)S(1)} %collective-permute-done.11, f32[12,36,47,64]{3,1,0,2:T(8,128)S(1)} %fusion.266, f32[12,1,47,64]{3,1,0,2:T(1,128)S(1)} %collective-permute-done.10, f32[1,38,47,64]{3,1,0,2:T(8,128)S(1)} %copy.42, ...), kind=kLoop, calls=%fused_computation.32 | loop fusion | flops 31186944 | bytes 12248576 | tf_op jit(solution)/shard_map/sub | solution.py:49
  280.5 6.9 fusion.57
  287.3 30.8 %pad_subtract_fusion.1 = f32[12,36,47,64]{3,1,0,2:T(8,128)S(1)} fusion(f32[12,36,46,64]{3,1,0,2:T(8,128)} %fusion.57, f32[1,38,47,64]{3,1,0,2:T(8,128)S(1)} %copy.44, f32[12,1,47,64]{3,1,0,2:T(1,128)S(1)} %collective-permute-done.11, f32[12,36,47,64]{3,1,0,2:T(8,128)S(1)} %fusion.266, f32[12,1,47,64]{3,1,0,2:T(1,128)S(1)} %collective-permute-done.10, ...), kind=kLoop, calls=%fused_computation.90 | loop fusion | flops 33785856 | bytes 17335808 | tf_op jit(solution)/shard_map/sub | solution.py:53
  320.3 2.6 collective-permute-start.15
  323.0 4.6 collective-permute-done.14
  330.6 12.5 %collective-permute-start.16 = (f32[1,38,47,64]{3,0,2,1:T(1,128)}, f32[1,38,47,64]{3,0,2,1:T(1,128)}, u32[]{:S(2)}, u32[]{:S(2)}) collective-permute-start(f32[1,38,47,64]{3,0,2,1:T(1,128)} %copy.45), channel_id=1, source_target_pairs={{0,1},{1,2},{2,3},{3,4},{4,5},{5,6},{6,7},{7,8},{8,9},{9,10},{10,1... | collective-permute-start | bytes 1371656 | tf_op jit(solution)/shard_map/ppermute | solution.py:16
  348.2 5.1 collective-permute-done.17
  355.6 32.8 %fusion.10 = f32[12,36,47,64]{3,1,0,2:T(8,128)S(1)} fusion(f32[1,38,47,64]{3,1,0,2:T(8,128)S(1)} %copy.48, f32[12,1,47,64]{3,1,0,2:T(1,128)} %copy-done.17, f32[12,36,47,64]{3,1,0,2:T(8,128)} %copy-done, f32[12,1,47,64]{3,1,0,2:T(1,128)S(1)} %collective-permute-done.14, f32[1,38,47,64]{3,1,0,2:T(8,128)S(1)} %copy.46, f32[12,36,47]{1,0,2:T(8,128)S(1)} %copy.33, ...), kind=kLoop, calls=%fused_computation.12 | loop fusion | flops 31186944 | bytes 12248576 | tf_op jit(solution)/shard_map/sub | solution.py:49
  388.4 6.9 fusion.56
  395.3 33.1 %pad_subtract_fusion = f32[12,36,47,64]{3,1,0,2:T(8,128)S(1)} fusion(f32[12,36,46,64]{3,1,0,2:T(8,128)} %fusion.56, f32[1,38,47,64]{3,1,0,2:T(8,128)} %copy-done.10, f32[12,1,47,64]{3,1,0,2:T(1,128)} %copy-done.17, f32[12,36,47,64]{3,1,0,2:T(8,128)S(1)} %bitcast.1634, f32[12,1,47,64]{3,1,0,2:T(1,128)S(1)} %collective-permute-done.14, ...), kind=kLoop, calls=%fused_computation.89 | loop fusion | flops 33785856 | bytes 17335808 | tf_op jit(solution)/shard_map/sub | solution.py:53
  428.4 10.0 %copy.49 = f32[12,36,47,64]{3,2,1,0:T(8,128)} copy(f32[12,36,47,64]{3,1,0,2:T(8,128)S(1)} %pad_subtract_fusion) | data formatting | bytes 10395648 | tf_op jit(solution)/shard_map/sub | solution.py:53
  438.4 9.3 %reshape.4725 = f32[12,1692,64]{2,1,0:T(8,128)} reshape(f32[12,36,47,64]{3,2,1,0:T(8,128)} %copy.49) | data formatting | bytes 10395648 | tf_op jit(solution)/shard_map/reshape | solution.py:86
  447.7 62.8 %while.146 = (s32[]{:T(128)}, f32[1024,64]{0,1:T(8,128)S(1)}, s32[1024]{0:T(1024)S(1)}, f32[12,1692,64]{2,1,0:T(8,128)}, s32[]{:T(128)}, /*index=5*/s32[]{:T(128)}, s32[]{:T(128)}) while((s32[]{:T(128)}, f32[1024,64]{0,1:T(8,128)S(1)}, s32[1024]{0:T(1024)S(1)}, f32[12,1692,64]{2,1,0:T(8,128)}, s32[]{:T(128)}, /*index=5*/s32[]{:T(128)}, ...), condition=%wide.region_1.2_spmd.clone, body=%wide.region_0.1_spmd.clone.sunk | while | flops 1332507648 | bytes 1405543 | solution.py:96
  447.7 5.2 fusion.421
  453.0 5.2 fusion.421
  458.2 5.2 fusion.421
  463.4 5.2 fusion.421
  468.7 5.2 fusion.421
  473.9 5.2 fusion.421
  479.1 5.2 fusion.421
  484.4 5.2 fusion.421
  489.6 5.2 fusion.421
  494.9 5.2 fusion.421
  500.1 5.2 fusion.421
  505.3 5.2 fusion.421
  510.9 84.3 %psum.7 = f32[64,64]{1,0:T(8,128)S(1)} all-reduce(f32[64,64]{1,0:T(8,128)S(1)} %fusion.263), channel_id=1, replica_groups=mesh['lon'=8,'lat'=16] {'lon','lat'}, use_global_device_ids=true, to_apply=%region_2.3 | all-reduce | flops 4096 | bytes 32768 | tf_op jit(solution)/shard_map/psum | solution.py:101
  (657 shorter events, 204.0 us)
Async XLA Ops:
  0.6 7.5 copy-start.11
  0.6 19.6 %copy-start.21 = (f32[12,36,47]{2,1,0:T(8,128)S(1)}, f32[12,36,47]{2,1,0:T(8,128)}, u32[]{:S(2)}) copy-start(f32[12,36,47]{2,1,0:T(8,128)} %param.276) | copy-start | bytes 243652
  0.7 21.6 %copy-start.22 = (f32[12,36,47]{2,1,0:T(8,128)S(1)}, f32[12,36,47]{2,1,0:T(8,128)}, u32[]{:S(2)}) copy-start(f32[12,36,47]{2,1,0:T(8,128)} %param.278) | copy-start | bytes 243652
  8.2 4.3 copy-start.1
  13.0 16.5 %collective-permute-start.1 = (f32[12,1,47,64]{3,1,0,2:T(1,128)S(1)}, f32[12,1,47,64]{3,1,0,2:T(1,128)S(1)}, u32[]{:S(2)}, u32[]{:S(2)}) collective-permute-start(f32[12,1,47,64]{3,1,0,2:T(1,128)S(1)} %get-tuple-element.1846), channel_id=1, source_target_pairs={{0,16},{16,32},{32,48},{48,64},{64,80},{80,96},{96,112},{112,0},{1... | collective-permute-start | bytes 433160 | tf_op jit(solution)/shard_map/ppermute | solution.py:16
  14.7 14.9 %collective-permute-start.2 = (f32[12,1,47,64]{3,1,0,2:T(1,128)S(1)}, f32[12,1,47,64]{3,1,0,2:T(1,128)S(1)}, u32[]{:S(2)}, u32[]{:S(2)}) collective-permute-start(f32[12,1,47,64]{3,1,0,2:T(1,128)S(1)} %get-tuple-element.1847), channel_id=1, source_target_pairs={{16,0},{32,16},{48,32},{64,48},{80,64},{96,80},{112,96},{0,112},{1... | collective-permute-start | bytes 433160 | tf_op jit(solution)/shard_map/ppermute | solution.py:17
  18.9 21.3 %collective-permute-start.3 = (f32[1,36,47]{2,1,0:T(8,128)S(1)}, f32[1,36,47]{2,1,0:T(8,128)S(1)}, u32[]{:S(2)}, u32[]{:S(2)}) collective-permute-start(f32[1,36,47]{2,1,0:T(8,128)S(1)} %slice.3170), channel_id=1, source_target_pairs={{1,0},{2,1},{3,2},{4,3},{5,4},{6,5},{7,6},{8,7},{9,8},{10,9},{11,1... | collective-permute-start | bytes 20312 | tf_op jit(solution)/shard_map/ppermute | solution.py:31
  20.2 9.2 %collective-permute-start = (f32[12,1,47]{2,1,0:T(1,128)S(1)}, f32[12,1,47]{2,1,0:T(1,128)S(1)}, u32[]{:S(2)}, u32[]{:S(2)}) collective-permute-start(f32[12,1,47]{2,1,0:T(1,128)S(1)} %slice.3163), channel_id=1, source_target_pairs={{16,0},{32,16},{48,32},{64,48},{80,64},{96,80},{112,96},{0,112},{1... | collective-permute-start | bytes 6776 | tf_op jit(solution)/shard_map/ppermute | solution.py:25
  22.3 17.9 %copy-start.20 = (f32[12,36,47]{2,1,0:T(8,128)S(1)}, f32[12,36,47]{2,1,0:T(8,128)}, u32[]{:S(2)}) copy-start(f32[12,36,47]{2,1,0:T(8,128)} %param.277) | copy-start | bytes 243652
  29.5 10.5 %copy-start.13 = (f32[12,1,47,64]{3,1,0,2:T(1,128)}, f32[12,1,47,64]{3,1,0,2:T(1,128)S(1)}, u32[]{:S(2)}) copy-start(f32[12,1,47,64]{3,1,0,2:T(1,128)S(1)} %collective-permute-done.1) | copy-start | bytes 433156
  29.5 10.4 %copy-start.15 = (f32[12,1,47,64]{3,1,0,2:T(1,128)}, f32[12,1,47,64]{3,1,0,2:T(1,128)S(1)}, u32[]{:S(2)}) copy-start(f32[12,1,47,64]{3,1,0,2:T(1,128)S(1)} %collective-permute-done.2) | copy-start | bytes 433156
  33.5 9.8 %collective-permute-start.4 = (f32[1,38,47,64]{3,0,2,1:T(1,128)}, f32[1,38,47,64]{3,0,2,1:T(1,128)}, u32[]{:S(2)}, u32[]{:S(2)}) collective-permute-start(f32[1,38,47,64]{3,0,2,1:T(1,128)} %copy.29), channel_id=1, source_target_pairs={{0,1},{1,2},{2,3},{3,4},{4,5},{5,6},{6,7},{7,8},{8,9},{9,10},{10,1... | collective-permute-start | bytes 1371656 | tf_op jit(solution)/shard_map/ppermute | solution.py:16
  37.6 7.2 collective-permute-start.5
  40.3 314.3 %copy-start.2 = (f32[12,36,47]{1,0,2:T(8,128)}, f32[12,36,47]{1,0,2:T(8,128)S(1)}, u32[]{:S(2)}) copy-start(f32[12,36,47]{1,0,2:T(8,128)S(1)} %copy.27) | copy-start | bytes 243652
  41.4 313.2 %copy-start.3 = (f32[12,36,47]{1,0,2:T(8,128)}, f32[12,36,47]{1,0,2:T(8,128)S(1)}, u32[]{:S(2)}) copy-start(f32[12,36,47]{1,0,2:T(8,128)S(1)} %copy.28) | copy-start | bytes 243652
  41.6 312.9 %copy-start.4 = (f32[12,36,47]{1,0,2:T(8,128)}, f32[12,36,47]{1,0,2:T(8,128)S(1)}, u32[]{:S(2)}) copy-start(f32[12,36,47]{1,0,2:T(8,128)S(1)} %copy.31) | copy-start | bytes 243652
  41.9 312.6 %copy-start.5 = (f32[12,36,47]{1,0,2:T(8,128)}, f32[12,36,47]{1,0,2:T(8,128)S(1)}, u32[]{:S(2)}) copy-start(f32[12,36,47]{1,0,2:T(8,128)S(1)} %copy.32) | copy-start | bytes 243652
  43.3 311.3 %copy-start.6 = (f32[12,36,47]{1,0,2:T(8,128)}, f32[12,36,47]{1,0,2:T(8,128)S(1)}, u32[]{:S(2)}) copy-start(f32[12,36,47]{1,0,2:T(8,128)S(1)} %copy.33) | copy-start | bytes 243652
  46.0 33.2 %copy-start.7 = (f32[12,36,46]{1,0,2:T(8,128)S(1)}, f32[12,36,46]{1,0,2:T(8,128)}, u32[]{:S(2)}) copy-start(f32[12,36,46]{1,0,2:T(8,128)} %copy.36) | copy-start | bytes 238468
  46.0 40.1 %slice-start.3 = ((s8[11550720]{0:T(1024)(128)(4,1)}), s8[4194304]{0:T(1024)(128)(4,1)S(1)}, s32[]{:S(2)}) async-start(s8[11550720]{0:T(1024)(128)(4,1)} %bitcast.1635), calls=%async_computation.3 | async-start | bytes 8388608
  46.0 40.0 %slice-start.4 = ((s8[11550720]{0:T(1024)(128)(4,1)}), s8[4194304]{0:T(1024)(128)(4,1)S(1)}, s32[]{:S(2)}) async-start(s8[11550720]{0:T(1024)(128)(4,1)} %bitcast.1635), calls=%async_computation.4 | async-start | bytes 8388608
  79.2 6.9 slice-start.5
  79.2 6.9 copy-start.14
  79.2 6.9 copy-start.16
  117.5 8.8 %collective-permute-start.6 = (f32[12,1,47,64]{3,1,0,2:T(1,128)S(1)}, f32[12,1,47,64]{3,1,0,2:T(1,128)S(1)}, u32[]{:S(2)}, u32[]{:S(2)}) collective-permute-start(f32[12,1,47,64]{3,1,0,2:T(1,128)S(1)} %get-tuple-element.1844), channel_id=1, source_target_pairs={{0,16},{16,32},{32,48},{48,64},{64,80},{80,96},{96,112},{112,0},{1... | collective-permute-start | bytes 433160 | tf_op jit(solution)/shard_map/ppermute | solution.py:16
  119.1 9.6 %collective-permute-start.7 = (f32[12,1,47,64]{3,1,0,2:T(1,128)S(1)}, f32[12,1,47,64]{3,1,0,2:T(1,128)S(1)}, u32[]{:S(2)}, u32[]{:S(2)}) collective-permute-start(f32[12,1,47,64]{3,1,0,2:T(1,128)S(1)} %get-tuple-element.1845), channel_id=1, source_target_pairs={{16,0},{32,16},{48,32},{64,48},{80,64},{96,80},{112,96},{0,112},{1... | collective-permute-start | bytes 433160 | tf_op jit(solution)/shard_map/ppermute | solution.py:17
  130.0 12.3 %collective-permute-start.8 = (f32[1,38,47,64]{3,0,2,1:T(1,128)S(1)}, f32[1,38,47,64]{3,0,2,1:T(1,128)S(1)}, u32[]{:S(2)}, u32[]{:S(2)}) collective-permute-start(f32[1,38,47,64]{3,0,2,1:T(1,128)S(1)} %copy.37), channel_id=1, source_target_pairs={{0,1},{1,2},{2,3},{3,4},{4,5},{5,6},{6,7},{7,8},{8,9},{9,10},{10,1... | collective-permute-start | bytes 1371656 | tf_op jit(solution)/shard_map/ppermute | solution.py:16
  140.9 10.1 %collective-permute-start.9 = (f32[1,38,47,64]{3,0,2,1:T(1,128)S(1)}, f32[1,38,47,64]{3,0,2,1:T(1,128)S(1)}, u32[]{:S(2)}, u32[]{:S(2)}) collective-permute-start(f32[1,38,47,64]{3,0,2,1:T(1,128)S(1)} %copy.39), channel_id=1, source_target_pairs={{1,0},{2,1},{3,2},{4,3},{5,4},{6,5},{7,6},{8,7},{9,8},{10,9},{11,1... | collective-permute-start | bytes 1371656 | tf_op jit(solution)/shard_map/ppermute | solution.py:17
  217.7 8.8 %collective-permute-start.10 = (f32[12,1,47,64]{3,1,0,2:T(1,128)S(1)}, f32[12,1,47,64]{3,1,0,2:T(1,128)S(1)}, u32[]{:S(2)}, u32[]{:S(2)}) collective-permute-start(f32[12,1,47,64]{3,1,0,2:T(1,128)S(1)} %get-tuple-element.1842), channel_id=1, source_target_pairs={{0,16},{16,32},{32,48},{48,64},{64,80},{80,96},{96,112},{112,0},{1... | collective-permute-start | bytes 433160 | tf_op jit(solution)/shard_map/ppermute | solution.py:16
  219.2 9.3 %collective-permute-start.11 = (f32[12,1,47,64]{3,1,0,2:T(1,128)S(1)}, f32[12,1,47,64]{3,1,0,2:T(1,128)S(1)}, u32[]{:S(2)}, u32[]{:S(2)}) collective-permute-start(f32[12,1,47,64]{3,1,0,2:T(1,128)S(1)} %get-tuple-element.1843), channel_id=1, source_target_pairs={{16,0},{32,16},{48,32},{64,48},{80,64},{96,80},{112,96},{0,112},{1... | collective-permute-start | bytes 433160 | tf_op jit(solution)/shard_map/ppermute | solution.py:17
  229.8 13.9 %collective-permute-start.12 = (f32[1,38,47,64]{3,0,2,1:T(1,128)S(1)}, f32[1,38,47,64]{3,0,2,1:T(1,128)S(1)}, u32[]{:S(2)}, u32[]{:S(2)}) collective-permute-start(f32[1,38,47,64]{3,0,2,1:T(1,128)S(1)} %copy.41), channel_id=1, source_target_pairs={{0,1},{1,2},{2,3},{3,4},{4,5},{5,6},{6,7},{7,8},{8,9},{9,10},{10,1... | collective-permute-start | bytes 1371656 | tf_op jit(solution)/shard_map/ppermute | solution.py:16
  242.4 9.7 %collective-permute-start.13 = (f32[1,38,47,64]{3,0,2,1:T(1,128)S(1)}, f32[1,38,47,64]{3,0,2,1:T(1,128)S(1)}, u32[]{:S(2)}, u32[]{:S(2)}) collective-permute-start(f32[1,38,47,64]{3,0,2,1:T(1,128)S(1)} %copy.43), channel_id=1, source_target_pairs={{1,0},{2,1},{3,2},{4,3},{5,4},{6,5},{7,6},{8,7},{9,8},{10,9},{11,1... | collective-permute-start | bytes 1371656 | tf_op jit(solution)/shard_map/ppermute | solution.py:17
  318.2 28.8 %copy-start.24 = (f32[1024]{0:T(1024)S(1)}, f32[1024]{0:T(1024)}, u32[]{:S(2)}) copy-start(f32[1024]{0:T(1024)} %param.280) | copy-start | bytes 12292
  318.2 10.1 %copy-start = (f32[12,36,47,64]{3,1,0,2:T(8,128)}, f32[12,36,47,64]{3,1,0,2:T(8,128)S(1)}, u32[]{:S(2)}) copy-start(f32[12,36,47,64]{3,1,0,2:T(8,128)S(1)} %fusion.265) | copy-start | bytes 15593476
  318.8 8.8 %collective-permute-start.14 = (f32[12,1,47,64]{3,1,0,2:T(1,128)S(1)}, f32[12,1,47,64]{3,1,0,2:T(1,128)S(1)}, u32[]{:S(2)}, u32[]{:S(2)}) collective-permute-start(f32[12,1,47,64]{3,1,0,2:T(1,128)S(1)} %get-tuple-element.1840), channel_id=1, source_target_pairs={{0,16},{16,32},{32,48},{48,64},{64,80},{80,96},{96,112},{112,0},{1... | collective-permute-start | bytes 433160 | tf_op jit(solution)/shard_map/ppermute | solution.py:16
  320.3 8.0 collective-permute-start.15
  328.3 16.6 %copy-start.17 = (f32[12,1,47,64]{3,1,0,2:T(1,128)}, f32[12,1,47,64]{3,1,0,2:T(1,128)S(1)}, u32[]{:S(2)}) copy-start(f32[12,1,47,64]{3,1,0,2:T(1,128)S(1)} %collective-permute-done.15) | copy-start | bytes 433156
  330.6 16.4 %collective-permute-start.16 = (f32[1,38,47,64]{3,0,2,1:T(1,128)}, f32[1,38,47,64]{3,0,2,1:T(1,128)}, u32[]{:S(2)}, u32[]{:S(2)}) collective-permute-start(f32[1,38,47,64]{3,0,2,1:T(1,128)} %copy.45), channel_id=1, source_target_pairs={{0,1},{1,2},{2,3},{3,4},{4,5},{5,6},{6,7},{7,8},{8,9},{9,10},{10,1... | collective-permute-start | bytes 1371656 | tf_op jit(solution)/shard_map/ppermute | solution.py:16
  344.9 8.3 %collective-permute-start.17 = (f32[1,38,47,64]{3,0,2,1:T(1,128)}, f32[1,38,47,64]{3,0,2,1:T(1,128)}, u32[]{:S(2)}, u32[]{:S(2)}) collective-permute-start(f32[1,38,47,64]{3,0,2,1:T(1,128)} %copy.47), channel_id=1, source_target_pairs={{1,0},{2,1},{3,2},{4,3},{5,4},{6,5},{7,6},{8,7},{9,8},{10,9},{11,1... | collective-permute-start | bytes 1371656 | tf_op jit(solution)/shard_map/ppermute | solution.py:17
  346.9 367.1 %copy-start.18 = (f32[64,64]{1,0:T(8,128)}, f32[64,64]{1,0:T(8,128)S(1)}, u32[]{:S(2)}) copy-start(f32[64,64]{1,0:T(8,128)S(1)} %fusion.271) | copy-start | bytes 49156
  348.2 6.4 copy-start.9
  355.5 32.9 %copy-start.8 = (f32[12,36,46]{1,0,2:T(8,128)S(1)}, f32[12,36,46]{1,0,2:T(8,128)}, u32[]{:S(2)}) copy-start(f32[12,36,46]{1,0,2:T(8,128)} %copy.36) | copy-start | bytes 238468
  355.5 39.8 %slice-start = ((s8[11550720]{0:T(1024)(128)(4,1)}), s8[4194304]{0:T(1024)(128)(4,1)S(1)}, s32[]{:S(2)}) async-start(s8[11550720]{0:T(1024)(128)(4,1)} %bitcast.1633), calls=%async_computation | async-start | bytes 8388608
  355.5 39.8 %slice-start.1 = ((s8[11550720]{0:T(1024)(128)(4,1)}), s8[4194304]{0:T(1024)(128)(4,1)S(1)}, s32[]{:S(2)}) async-start(s8[11550720]{0:T(1024)(128)(4,1)} %bitcast.1633), calls=%async_computation.1 | async-start | bytes 8388608
  388.4 6.9 slice-start.2
  438.4 9.3 %copy-start.19 = (f32[1024,64]{0,1:T(8,128)S(1)}, f32[1024,64]{0,1:T(8,128)}, u32[]{:S(2)}) copy-start(f32[1024,64]{0,1:T(8,128)} %custom-call) | copy-start | bytes 786436
  438.4 9.3 %copy-start.23 = (s32[1024]{0:T(1024)S(1)}, s32[1024]{0:T(1024)}, u32[]{:S(2)}) copy-start(s32[1024]{0:T(1024)} %param.279) | copy-start | bytes 12292
  706.5 8.3 %copy-start.12 = (f32[64,64]{1,0:T(8,128)}, f32[64,64]{1,0:T(8,128)S(1)}, u32[]{:S(2)}) copy-start(f32[64,64]{1,0:T(8,128)S(1)} %scatter.534) | copy-start | bytes 49156
  (1 other events, 0.9 us)
where the time goes:
time: 816 us; the launch traced here: 803 us
  other arithmetic  305 us (37%)
  matrix products  153 us (19%)
  local copies, waits for them, and re-layouts  100 us (12%)
  blocking collectives  84.3 us (10%)
  starting transfers between devices  63.2 us (8%)
  between operations  48.7 us (6%)
  waiting for transfers between devices  46.9 us (6%)
    dot_general x78, matrix products, highest_dot(): jnp.dot(left, right, precision=lax.Precision.HIGHEST, preferred_element_t...  153 us
    sub x4, other arithmetic, advance(): advected + jnp.concatenate([mixed, zero_lev], axis=2)  126 us
    sub x4, other arithmetic, advance(): advected = conc + flux_w - flux_e + flux_s - flux_n  122 us
    psum x1, blocking collectives, on_device(): gram = lax.psum(partial_gram, ('lon', 'lat'))  84.3 us
    ppermute x8, starting transfers between devices, padded_2(): before = lax.ppermute(last, axis, up)  42.7 us
    slice x64, local copies, waits for them, and re-layouts, on_device(): pivot = jnp.sqrt(remaining[column, column])  37.2 us
    mul x4, other arithmetic, advance(): mixed = mixing[:, :, :-1] * (advected[:, :, 1:] - advected[:, :, :-1])  27.5 us
    ppermute x8, waiting for transfers between devices, padded_2(): after = lax.ppermute(leading, axis, down)  27.3 us
  transfers between devices with their start and end apart: 18, of which 10 were waited for; matrix products, arithmetic and copies ran while one was open for 2% of the time, Pallas kernels for 0%

commit v1 on v0

v1 whole, which is shorter than its diff:
```python
import jax
import jax.numpy as jnp
from jax import lax
from jax.experimental import pallas as pl
from jax.experimental.pallas import tpu as pltpu
from jax.sharding import PartitionSpec as P

STEPS = 4
BANDS, COLS, LEVS, PROBES = 12, 36, 47, 64
HALO = STEPS
TALL = BANDS + 2 * HALO
WIDE = COLS + 2 * HALO
LEVP = 48
HALF = COLS // 2
PAIRS = HALF + 2 * HALO
SLOTS = 1024
FIELD_ROWS = TALL * HALF * LEVP
ZERO_ROW = 2 * FIELD_ROWS
F32 = jnp.float32
HIGHEST = lax.Precision.HIGHEST
VMEM_BYTES = 62 * 1024 * 1024


def params():
    return pltpu.CompilerParams(vmem_limit_bytes=VMEM_BYTES)


def whole(space=pltpu.VMEM):
    return pl.BlockSpec(memory_space=space)


def along(x, axis, step, wrap):
    size = lax.axis_size(axis)
    pairs = [(i, (i + step) % size) for i in range(size) if wrap or 0 <= i + step < size]
    return lax.ppermute(x, axis, pairs)


def all_sum(x):
    for axis, bits in (("lat", (1,)), ("lat", (2, 4)), ("lon", (2, 4)), ("lon", (1,)), ("lat", (8,))):
        size = lax.axis_size(axis)
        masks = [bits[0]] if len(bits) == 1 else [bits[0], bits[1], bits[0] | bits[1]]
        terms = [lax.ppermute(x, axis, [(i, i ^ mask) for i in range(size)]) for mask in masks]
        for term in terms:
            x = x + term
    return x


def edges_kernel(west, east, flux_west, flux_east, to_west, to_east):
    half = BANDS // 2
    for band in range(half):
        for col in range(HALO):
            for src, flux, dst in ((west, flux_west, to_west), (east, flux_east, to_east)):
                dst[band, col, 0:LEVS, 0:PROBES] = src[band, col]
                dst[band, col, 0:LEVS, PROBES:] = src[band + half, col]
                dst[band, col, LEVS:LEVP, 0:PROBES] = flux[band, col : col + 1]
                dst[band, col, LEVS:LEVP, PROBES:] = flux[band + half, col : col + 1]


def pack_edges(conc, flux):
    last = COLS // HALO - 1
    field = lambda at: pl.BlockSpec((BANDS, HALO, LEVS, PROBES), lambda i: (0, at, 0, 0))
    out = jax.ShapeDtypeStruct((BANDS // 2, HALO, LEVP, 2 * PROBES), F32)
    spec = pl.BlockSpec(out.shape, lambda i: (0, 0, 0, 0))
    return pl.pallas_call(
        edges_kernel,
        grid=(1,),
        in_specs=[field(0), field(last), whole(), whole()],
        out_specs=[spec, spec],
        out_shape=[out, out],
        compiler_params=params(),
        name="pack_edges",
    )(conc, conc, flux[:, :HALO], flux[:, -HALO:])


def split_terms(x):
    doubled = x + pltpu.roll(x, 64, 1)
    high = doubled.astype(jnp.bfloat16).astype(F32)
    lane = lax.broadcasted_iota(jnp.int32, x.shape, 1)
    return jnp.where(lane < 64, high, doubled - high).astype(jnp.bfloat16)


def spread(split_ref, refs, tile, source, sign=None):
    shape = (128, 256)
    row = lax.broadcasted_iota(jnp.int32, shape, 0) & 63
    col = lax.broadcasted_iota(jnp.int32, shape, 1)
    pair = 2 * tile + (col >> 7)
    upper = ((col >> 6) & 1) == 1
    for which, ref in enumerate(refs):
        low, high, high_sign = source(which, pair)
        weight = jnp.where(upper, high_sign, 1.0)
        chosen = jnp.where(row == jnp.where(upper, high, low), weight, 0.0).astype(jnp.bfloat16)
        out = jnp.dot(split_ref[which], chosen, preferred_element_type=F32)
        out = out.reshape(TALL, 1, LEVP, 256)
        ref[:, pl.ds(2 * tile, 1)] = out[..., :128]
        ref[:, pl.ds(2 * tile + 1, 1)] = out[..., 128:]


def face_flux(speed, behind, ahead):
    return speed * jnp.where(speed > 0.0, behind, ahead)


def mix_levels(advected, mixing):
    moved = mixing * (pltpu.roll(advected, LEVP - 1, 0) - advected)
    return advected + moved - pltpu.roll(moved, 1, 0)


def transport_kernel(conc, flux, coef, out, c, u, v, m, fs, split, stage, in_sem, out_sem):
    def fetch(band, slot):
        return pltpu.make_async_copy(conc.at[band], stage.at[slot], in_sem.at[slot])

    fetch(0, 0).start()
    fetch(1, 1).start()
    for which in range(3):
        split[which] = split_terms(coef[which].reshape(TALL * LEVP, 128))

    def expand(tile, carry):
        spread(split, (u, v, m), tile, lambda which, pair: (pair, pair + HALF, 1.0))
        return carry

    lax.fori_loop(0, PAIRS // 2, expand, 0)

    def clear(band, carry):
        c[band] = jnp.zeros((PAIRS, LEVP, 128), F32)
        return carry

    lax.fori_loop(0, TALL, clear, 0)

    def load(band, carry):
        slot = lax.rem(band, 2)
        fetch(band, slot).wait()
        for pair in range(PAIRS):
            low, high = pair - HALO, pair - HALO + HALF
            if low >= 0:
                c[band + HALO, pair, 0:LEVS, 0:PROBES] = stage[slot, low]
            if high < COLS:
                c[band + HALO, pair, 0:LEVS, PROBES:] = stage[slot, high]

        @pl.when(band + 2 < BANDS)
        def _():
            fetch(band + 2, slot).start()

        return carry

    lax.fori_loop(0, BANDS, load, 0)

    def save(band):
        return pltpu.make_async_copy(c.at[band, pl.ds(HALO, HALF)], out.at[band], out_sem.at[band])

    for step in range(1, STEPS + 1):
        first, last = step, PAIRS - step
        chunk = {24: 6, 22: 11, 20: 5, 18: 6}[last - first]

        def gain(band, carry):
            for pair in range(PAIRS):
                c[band + HALO, pair, 0:1] = c[band + HALO, pair, 0:1] + flux[band, pair : pair + 1]
            return carry

        lax.fori_loop(0, BANDS, gain, 0)
        fs[first:last] = jnp.zeros((last - first, LEVP, 128), F32)

        def row(band, carry):
            north = jnp.minimum(band + 1, TALL - 1)
            here = c[band, first]
            west = face_flux(u[band, first], c[band, first - 1], here)

            def some(at, state):
                here, west = state
                for k in range(chunk):
                    pair = first + at * chunk + k
                    ahead = c[band, pair + 1]
                    east = face_flux(u[band, pair + 1], here, ahead)
                    top = face_flux(v[north, pair], here, c[north, pair])
                    advected = here + (west - east) + (fs[pair] - top)
                    fs[pair] = top
                    c[band, pair] = mix_levels(advected, m[band, pair])
                    here, west = ahead, east
                return here, west

            lax.fori_loop(0, (last - first) // chunk, some, (here, west))
            if step == STEPS:
                save(band).start()
            return carry

        lax.fori_loop(HALO - step, TALL - HALO + step, row, 0)

    def drain(band, carry):
        save(band).wait()
        return carry

    lax.fori_loop(0, TALL, drain, 0)


def transport(conc, flux, coef):
    field = pltpu.VMEM((TALL, PAIRS, LEVP, 128), F32)
    return pl.pallas_call(
        transport_kernel,
        in_specs=[whole(pl.ANY), whole(), whole()],
        out_specs=whole(pl.ANY),
        out_shape=jax.ShapeDtypeStruct((TALL, HALF, LEVP, 128), F32),
        scratch_shapes=[
            field,
            field,
            field,
            field,
            pltpu.VMEM((PAIRS, LEVP, 128), F32),
            pltpu.VMEM((3, TALL * LEVP, 128), jnp.bfloat16),
            pltpu.VMEM((2, COLS, LEVS, PROBES), F32),
            pltpu.SemaphoreType.DMA((2,)),
            pltpu.SemaphoreType.DMA((TALL,)),
        ],
        compiler_params=params(),
        name="transport",
    )(conc, flux, coef)


def strips_kernel(index, west, east, coef, field, out, c, u, v, m, fs, gain, split, full, sem):
    fetch = pltpu.make_async_copy(field, full.at[pl.ds(0, FIELD_ROWS)], sem)
    fetch.start()
    for which in range(3):
        split[which] = split_terms(coef[which].reshape(TALL * LEVP, 128))

    def source(which, pair):
        if which == 0:
            return pair, WIDE - pair, -1.0
        return pair, WIDE - 1 - pair, 1.0

    def expand(tile, carry):
        spread(split, (u, v, m), tile, source)
        return carry

    lax.fori_loop(0, HALO, expand, 0)

    def clear(band, carry):
        c[band] = jnp.zeros((2 * HALO, LEVP, 128), F32)
        return carry

    lax.fori_loop(0, TALL, clear, 0)
    lane = lax.broadcasted_iota(jnp.int32, (LEVP, 128), 1)
    lower = lane < PROBES
    inside = lax.broadcasted_iota(jnp.int32, (LEVP, 128), 0) < LEVS

    def place(band, carry):
        for k in range(HALO):
            left, right = west[band, k], east[band, HALO - 1 - k]
            for at, value in (
                (band, jnp.where(lower, left, pltpu.roll(right, PROBES, 1))),
                (band + BANDS // 2, jnp.where(lower, pltpu.roll(left, PROBES, 1), right)),
            ):
                c[at + HALO, k] = jnp.where(inside, value, 0.0)
                gain[at, k, 0:1] = value[LEVS:LEVP]
        return carry

    lax.fori_loop(0, BANDS // 2, place, 0)

    for step in range(1, STEPS + 1):
        region = range(step, step + HALO)

        def add(band, carry):
            for k in range(step - 1, HALO):
                c[band + HALO, k, 0:1] = c[band + HALO, k, 0:1] + gain[band, k, 0:1]
            return carry

        lax.fori_loop(0, BANDS, add, 0)
        for k in region:
            fs[k] = jnp.zeros((LEVP, 128), F32)

        def row(band, carry):
            north = jnp.minimum(band + 1, TALL - 1)
            here = c[band, step]
            behind = face_flux(u[band, step], c[band, step - 1], here)
            for k in region:
                if k < step + HALO - 1:
                    ahead = c[band, k + 1]
                    front = face_flux(u[band, k + 1], here, ahead)
                    net = behind - front
                else:
                    net = behind
                top = face_flux(v[north, k], here, c[north, k])
                advected = here + net + (fs[k] - top)
                fs[k] = top
                c[band, k] = mix_levels(advected, m[band, k])
                here, behind = ahead, front
            return carry

        lax.fori_loop(HALO - step, TALL - HALO + step, row, 0)

    fetch.wait()

    def merge(band, carry):
        base = band * (HALF * LEVP)
        for k in range(HALO):
            share = c[band, HALO + k]
            for pair, keep in ((k, lower), (HALF - 1 - k, ~lower)):
                rows = pl.ds(pl.multiple_of(base + pair * LEVP, LEVP), LEVP)
                full[rows] = full[rows] + jnp.where(keep, share, 0.0)
        for pair in range(HALF):
            at = pl.multiple_of(base + pair * LEVP, LEVP)
            full[pl.ds(FIELD_ROWS + at, LEVP)] = pltpu.roll(full[pl.ds(at, LEVP)], PROBES, 1)
        return carry

    lax.fori_loop(0, TALL, merge, 0)
    full[ZERO_ROW : ZERO_ROW + 8] = jnp.zeros((8, 128), F32)

    half = SLOTS // 2
    low_lanes = lax.broadcasted_iota(jnp.int32, (1, 128), 1) < PROBES
    unroll = 16
    for group in range(3):

        def pick(at, carry):
            for k in range(unroll):
                slot = at * unroll + k
                one = full[pl.ds(index[group, slot], 1)]
                two = full[pl.ds(index[group, slot + half], 1)]
                out[group, pl.ds(slot, 1)] = jnp.where(low_lanes, one, two)
            return carry

        lax.fori_loop(0, half // unroll, pick, 0)


def strips(index, west, east, coef, field):
    strip = pltpu.VMEM((TALL, 2 * HALO, LEVP, 128), F32)
    return pl.pallas_call(
        strips_kernel,
        in_specs=[whole(pltpu.SMEM), whole(), whole(), whole(), whole(pl.ANY)],
        out_specs=whole(),
        out_shape=jax.ShapeDtypeStruct((3, SLOTS // 2, 128), F32),
        scratch_shapes=[
            strip,
            strip,
            strip,
            strip,
            pltpu.VMEM((2 * HALO, LEVP, 128), F32),
            pltpu.VMEM((BANDS, HALO, 8, 128), F32),
            pltpu.VMEM((3, TALL * LEVP, 128), jnp.bfloat16),
            pltpu.VMEM((ZERO_ROW + 8, 128), F32),
            pltpu.SemaphoreType.DMA,
        ],
        compiler_params=params(),
        name="strips",
    )(index, west, east, coef, field)


def row_index(cells, shift, wanted):
    level = cells % LEVS
    rest = cells // LEVS
    col = rest % COLS
    band = rest // COLS + HALO + shift
    held = (band >= 0) & (band < TALL)
    upper = (col >= HALF).astype(jnp.int32)
    row = (band * HALF + col - HALF * upper) * LEVP + level + FIELD_ROWS * (upper ^ wanted)
    return jnp.where(held, row, ZERO_ROW)


def gram_kernel(own, from_south, from_north, weight, images, gram):
    rows = (own[...] + from_south[...] + from_north[...]) * weight[...]
    images[...] = rows
    both = lax.dot_general(
        rows, rows, (((0,), (0,)), ((), ())), precision=HIGHEST, preferred_element_type=F32
    )
    total = both[:PROBES, :PROBES] + both[PROBES:, PROBES:]
    gram[:, 0:PROBES] = total[: PROBES // 2]
    gram[:, PROBES:] = total[PROBES // 2 :]


def gram_of(own, from_south, from_north, weight):
    return pl.pallas_call(
        gram_kernel,
        in_specs=[whole()] * 4,
        out_specs=[whole()] * 2,
        out_shape=[
            jax.ShapeDtypeStruct((SLOTS // 2, 128), F32),
            jax.ShapeDtypeStruct((PROBES // 2, 128), F32),
        ],
        compiler_params=params(),
        name="gram",
    )(own, from_south, from_north, weight)


def factor_kernel(root, gram, images, basis_t, factor, work):
    half = PROBES // 2
    work[0:half, 0:PROBES] = gram[:, 0:PROBES]
    work[half:, 0:PROBES] = gram[:, PROBES:]
    diagonal = (
        lax.broadcasted_iota(jnp.int32, (PROBES, PROBES), 0)
        == lax.broadcasted_iota(jnp.int32, (PROBES, PROBES), 1)
    )
    work[:, PROBES:] = diagonal.astype(F32)
    state = work[...]
    below = lax.broadcasted_iota(jnp.int32, (PROBES, 128), 0)
    done = []
    for k in range(PROBES):
        column = jnp.broadcast_to(state[:, k : k + 1], (PROBES, 128))
        scale = 1.0 / jnp.sqrt(column[k : k + 1])
        pivot = state[k : k + 1] * scale
        work[k : k + 1] = pivot
        state = state - jnp.where(below > k, column * scale, 0.0) * pivot
    both = work[...]
    row = lax.broadcasted_iota(jnp.int32, (PROBES, PROBES), 0)
    col = lax.broadcasted_iota(jnp.int32, (PROBES, PROBES), 1)
    factor[...] = jnp.where(col >= row, both[:, :PROBES], 0.0) * (1.0 / root)
    inverse_t = jnp.where(col <= row, both[:, PROBES:], 0.0) * root
    zero = jnp.zeros((PROBES, PROBES), F32)
    twice = jnp.concatenate(
        [
            jnp.concatenate([inverse_t, zero], axis=1),
            jnp.concatenate([zero, inverse_t], axis=1),
        ],
        axis=0,
    )
    basis = lax.dot_general(
        twice, images[...], (((1,), (1,)), ((), ())), precision=HIGHEST, preferred_element_type=F32
    )
    basis_t[:, 0 : SLOTS // 2] = basis[:PROBES]
    basis_t[:, SLOTS // 2 :] = basis[PROBES:]


def factor_of(gram, images, root):
    return pl.pallas_call(
        lambda *refs: factor_kernel(root, *refs),
        in_specs=[whole()] * 2,
        out_specs=[whole()] * 2,
        out_shape=[
            jax.ShapeDtypeStruct((PROBES, SLOTS), F32),
            jax.ShapeDtypeStruct((PROBES, PROBES), F32),
        ],
        scratch_shapes=[pltpu.VMEM((PROBES, 128), F32)],
        compiler_params=params(),
        name="factor",
    )(gram, images)


def on_device(
    flux_probes, conc_start, u_courant, v_courant, vert_mix, obs_cell, obs_weight, obs_count
):
    coef = jnp.stack([u_courant, v_courant, vert_mix.at[:, :, LEVS - 1].set(0.0)])
    from_south = along(coef[:, -HALO:], "lat", 1, False)
    from_north = along(coef[:, :HALO], "lat", -1, False)
    to_west, to_east = pack_edges(conc_start, flux_probes)
    west_field = along(to_east, "lon", 1, True)
    east_field = along(to_west, "lon", -1, True)
    north_cells = along(obs_cell, "lat", -1, False)
    south_cells = along(obs_cell, "lat", 1, False)
    tall = jnp.concatenate([from_south, coef, from_north], axis=1)
    from_west = along(tall[:, :, -HALO:], "lon", 1, True)
    from_east = along(tall[:, :, :HALO], "lon", -1, True)
    wide = jnp.concatenate([from_west, tall, from_east], axis=2)
    wide = jnp.pad(wide.transpose(0, 1, 3, 2), ((0, 0), (0, 0), (0, LEVP - LEVS), (0, 128 - WIDE)))
    flux_wide = jnp.pad(flux_probes, ((0, 0), (HALO, HALO), (0, 0)))
    flux_pairs = jnp.concatenate([flux_wide[:, :PAIRS], flux_wide[:, HALF:]], axis=2)
    field = transport(conc_start, flux_pairs, wide)

    wanted = (jnp.arange(SLOTS, dtype=jnp.int32) >= SLOTS // 2).astype(jnp.int32)
    index = jnp.stack(
        [
            row_index(obs_cell, 0, wanted),
            row_index(north_cells, BANDS, wanted),
            row_index(south_cells, -BANDS, wanted),
        ]
    )
    rows = strips(index, west_field, east_field, wide, field.reshape(FIELD_ROWS, 128))
    south_rows = along(rows[1], "lat", 1, False)
    north_rows = along(rows[2], "lat", -1, False)
    live = jnp.arange(SLOTS, dtype=jnp.int32) < obs_count[0]
    scale = jnp.where(live, obs_weight, 0.0)
    lanes = (SLOTS // 2, PROBES)
    weight = jnp.concatenate(
        [
            jnp.broadcast_to(scale[: SLOTS // 2, None], lanes),
            jnp.broadcast_to(scale[SLOTS // 2 :, None], lanes),
        ],
        axis=1,
    )
    images, gram = gram_of(rows[0], south_rows, north_rows, weight)
    gram = all_sum(gram)
    total_rows = SLOTS * lax.axis_size("lon") * lax.axis_size("lat")
    basis_t, factor = factor_of(gram, images, float(total_rows) ** 0.5)
    return basis_t.T, factor


def solution(mesh):
    in_specs = (
        P("lat", "lon", None),
        P("lat", "lon", None, None),
        P("lat", "lon", None),
        P("lat", "lon", None),
        P("lat", "lon", None),
        P(("lon", "lat")),
        P(("lon", "lat")),
        P(("lon", "lat")),
    )
    out_specs = (P(("lon", "lat"), None), P())
    return jax.shard_map(
        on_device, mesh=mesh, in_specs=in_specs, out_specs=out_specs, check_vma=False
    )
```

time: 816 us -> 188 us (0.23); the launches traced: 803 us -> 187 us
  other arithmetic: 305 us -> 7.69 us
  matrix products: 153 us -> 0 us
  local copies, waits for them, and re-layouts: 100 us -> 12.8 us
  blocking collectives: 84.3 us -> 0 us
  Pallas kernels: 0 us -> 78.9 us
  between operations: 48.7 us -> 1.53 us
  starting transfers between devices: 63.2 us -> 46.2 us
    sub x83 -> x0, other arithmetic: 272 us -> none  [the longest x4 126 us: advance(): advected + jnp.concatenate([mixed, zero_lev], axis=2)]
    dot_general x78 -> x0, matrix products: 153 us -> none  [highest_dot(): jnp.dot(left, right, precision=lax.Precision.HIGHEST, preferred_element_t...]
    psum x1 -> x0, blocking collectives: 84.3 us -> none  [on_device(): gram = lax.psum(partial_gram, ('lon', 'lat'))]
    pallas_call x0 -> x5, Pallas kernels: none -> 78.9 us  [the longest x1 43.5 us: transport(): pl.pallas_call(transport_kernel, in_specs=[whole(pl.ANY), whole(), whole(...]
    slice x83 -> x6, local copies, waits for them, and re-layouts: 54.7 us -> 2.97 us  [the longest x2 1.68 us: on_device(): from_west = along(tall[:, :, -HALO:], 'lon', 1, True)]
    mul x68 -> x0, other arithmetic: 28.6 us -> none  [the longest x4 27.5 us: advance(): mixed = mixing[:, :, :-1] * (advected[:, :, 1:] - advected[:, :, :-1])]
    ppermute x18 -> x19, starting transfers between devices: 63.2 us -> 46.2 us  [the longest x9 24.2 us: all_sum(): lax.ppermute(x, axis, [(i, i ^ mask) for i in range(size)])]
    sub x1 -> x0, local copies, waits for them, and re-layouts: 9.98 us -> none  [advance(): advected + jnp.concatenate([mixed, zero_lev], axis=2)]
  transfers between devices with their start and end apart: 18 -> 19, of which waited for: 10 -> 10; matrix products, arithmetic and copies ran while one was open for 2% -> 9% of each run, Pallas kernels for 0% -> 25%
where the time goes in v1:
time: 188 us; the launch traced here: 187 us
  Pallas kernels  78.9 us (42%)
  starting transfers between devices  46.2 us (25%)
  waiting for transfers between devices  39.8 us (21%)
  local copies, waits for them, and re-layouts  12.8 us (7%)
  other arithmetic  7.69 us (4%)
    pallas_call x1, Pallas kernels, transport(): pl.pallas_call(transport_kernel, in_specs=[whole(pl.ANY), whole(), whole(...  43.5 us
    ppermute x9, starting transfers between devices, all_sum(): lax.ppermute(x, axis, [(i, i ^ mask) for i in range(size)])  24.2 us
    ppermute x10, waiting for transfers between devices, along(): return lax.ppermute(x, axis, pairs)  22.2 us
    ppermute x10, starting transfers between devices, along(): return lax.ppermute(x, axis, pairs)  22 us
    pallas_call x1, Pallas kernels, strips(): pl.pallas_call(strips_kernel, in_specs=[whole(pltpu.SMEM), whole(), whole...  21.6 us
    ppermute x9, waiting for transfers between devices, all_sum(): lax.ppermute(x, axis, [(i, i ^ mask) for i in range(size)])  17.6 us
    pallas_call x1, Pallas kernels, factor_of(): pl.pallas_call(lambda *refs: factor_kernel(root, *refs), in_specs=[whole(...  8.37 us
    unnamed x15, local copies, waits for them, and re-layouts  4.17 us
  transfers between devices with their start and end apart: 19, of which 10 were waited for; matrix products, arithmetic and copies ran while one was open for 9% of the time, Pallas kernels for 25%

profile of v1, /device:TPU:0, one launch (start us, length us, event | category | flops | bytes accessed | tf_op | source)
XLA Modules:
  0.0 186.9 jit_solution(9711058450196984672)
XLA Ops:
  0.6 1.4 collective-permute-start
  2.1 3.0 %collective-permute-start.1 = (s32[1024]{0:T(1024)}, s32[1024]{0:T(1024)S(1)}, u32[]{:S(2)}, u32[]{:S(2)}) collective-permute-start(s32[1024]{0:T(1024)} %param.15), channel_id=1, source_target_pairs={{0,1},{1,2},{2,3},{3,4},{4,5},{5,6},{6,7},{7,8},{8,9},{9,10},{10,1... | collective-permute-start | bytes 12296 | tf_op jit(solution)/shard_map/ppermute | solution.py:35
  5.1 1.1 copy.15
  6.3 1.1 copy.13
  7.4 1.1 copy.14
  8.6 0.8 pad_maximum_fusion.3
  9.4 3.9 %collective-permute-start.4 = (f32[3,4,36,47]{2,3,1,0:T(8,128)}, f32[3,4,36,47]{2,3,1,0:T(8,128)}, u32[]{:S(2)}, u32[]{:S(2)}) collective-permute-start(f32[3,4,36,47]{2,3,1,0:T(8,128)} %get-tuple-element.28), channel_id=1, source_target_pairs={{0,1},{1,2},{2,3},{3,4},{4,5},{5,6},{6,7},{7,8},{8,9},{9,10},{10,1... | collective-permute-start | bytes 243656 | tf_op jit(solution)/shard_map/ppermute | solution.py:35
  13.3 1.3 collective-permute-start.5
  14.6 0.6 fusion.23
  15.2 3.1 %pack_edges.1 = (f32[6,4,48,128]{3,2,1,0:T(8,128)}, f32[6,4,48,128]{3,2,1,0:T(8,128)}) custom-call(f32[12,36,47,64]{3,2,1,0:T(8,128)} %conc.1, f32[12,36,47,64]{3,2,1,0:T(8,128)} %conc.1, f32[12,4,64]{2,1,0:T(4,128)} %get-tuple-element.36.flux_west, f32[12,4,64]{2,1,0:T(4,128)} %get-tuple-element.35.flux_east), custom_call_target="tpu_custom_call" | custom-call | tf_op jit(solution)/shard_map/pack_edges/pallas_call | solution.py:64
  18.3 1.5 collective-permute-start.2
  20.6 0.8 pad_maximum_fusion.5.flux
  21.4 3.5 %collective-permute-start.3 = (f32[6,4,48,128]{3,2,1,0:T(8,128)}, f32[6,4,48,128]{3,2,1,0:T(8,128)}, u32[]{:S(2)}, u32[]{:S(2)}) collective-permute-start(f32[6,4,48,128]{3,2,1,0:T(8,128)} %get-tuple-element.21), channel_id=1, source_target_pairs={{0,112},{16,0},{32,16},{48,32},{64,48},{80,64},{96,80},{112,96},{1... | collective-permute-start | bytes 1769480 | tf_op jit(solution)/shard_map/ppermute | solution.py:35
  25.0 1.2 pad_maximum_fusion
  26.7 1.2 copy.16
  27.9 0.6 copy.17
  28.5 4.2 %collective-permute-start.7 = (f32[3,20,4,47]{3,2,1,0:T(4,128)S(1)}, f32[3,20,4,47]{3,2,1,0:T(4,128)}, u32[]{:S(2)}, u32[]{:S(2)}) collective-permute-start(f32[3,20,4,47]{3,2,1,0:T(4,128)S(1)} %copy.17), channel_id=1, source_target_pairs={{0,112},{16,0},{32,16},{48,32},{64,48},{80,64},{96,80},{112,96},{1... | collective-permute-start | bytes 135368 | tf_op jit(solution)/shard_map/ppermute | solution.py:35
  32.7 0.6 pad_add_fusion.index
  33.3 19.3 %collective-permute-done.6 = f32[3,20,4,47]{3,2,1,0:T(4,128)S(1)} collective-permute-done((f32[3,20,4,47]{3,2,1,0:T(4,128)}, f32[3,20,4,47]{3,2,1,0:T(4,128)S(1)}, u32[]{:S(2)}, u32[]{:S(2)}) %collective-permute-start.6) | collective-permute-done | bytes 45152 | tf_op jit(solution)/shard_map/ppermute | solution.py:35
  52.6 0.6 copy.18
  53.3 0.7 collective-permute-done.7
  54.0 1.5 copy.19
  55.5 2.0 %maximum_bitcast_fusion = f32[3,20,47,44]{3,2,1,0:T(8,128)S(1)} fusion(f32[3,20,4,47]{2,3,1,0:T(8,128)S(1)} %copy.19, f32[3,4,36,47]{2,3,1,0:T(8,128)} %collective-permute-done.5, f32[1,12,36,47]{2,3,1,0:T(8,128)} %copy-done, f32[1,12,36,47]{2,3,1,0:T(8,128)S(1)} %bitcast.24, f32[1,12,36,47]{2,3,1,0:T(8,128)S(1)} %bitcast.21, ...), kind=kLoop, calls=%fused_computation.1 | loop fusion | flops 744480 | bytes 992640 | tf_op jit(solution)/shard_map/transpose | solution.py:447
  57.5 1.3 pad.10.coef
  58.8 43.5 %transport.1 = f32[20,18,48,128]{3,2,1,0:T(8,128)} custom-call(f32[12,36,47,64]{3,2,1,0:T(8,128)} %conc.1, f32[12,26,128]{2,1,0:T(8,128)} %pad_maximum_fusion.5.flux, f32[3,20,48,128]{3,2,1,0:T(8,128)} %pad.10.coef), custom_call_target="tpu_custom_call" | custom-call | tf_op jit(solution)/shard_map/transport/pallas_call | solution.py:195
  102.3 21.6 %strips.1 = f32[3,512,128]{2,1,0:T(8,128)} custom-call(s32[3,1024]{1,0:T(4,128)} %pad_add_fusion.index, f32[6,4,48,128]{3,2,1,0:T(8,128)} %collective-permute-done.2.west, f32[6,4,48,128]{3,2,1,0:T(8,128)} %collective-permute-done.3.east, f32[3,20,48,128]{3,2,1,0:T(8,128)} %pad.10.coef, f32[17280,128]{1,0:T(8,128)} %bitcast.18), custom_call_target="tpu_custom_call" | custom-call | tf_op jit(solution)/shard_map/strips/pallas_call | solution.py:322
  123.9 1.9 slice_bitcast_fusion
  125.8 2.0 %collective-permute-start.8 = (f32[512,128]{1,0:T(8,128)S(1)}, f32[512,128]{1,0:T(8,128)S(1)}, u32[]{:S(2)}, u32[]{:S(2)}) collective-permute-start(f32[512,128]{1,0:T(8,128)S(1)} %get-tuple-element.31), channel_id=1, source_target_pairs={{0,1},{1,2},{2,3},{3,4},{4,5},{5,6},{6,7},{7,8},{8,9},{9,10},{10,1... | collective-permute-start | bytes 786440 | tf_op jit(solution)/shard_map/ppermute | solution.py:35
  127.8 1.3 collective-permute-start.9
  129.3 0.9 pad_maximum_fusion.4.weight
  130.2 2.2 %collective-permute-done.9.from_north = f32[512,128]{1,0:T(8,128)S(1)} collective-permute-done((f32[512,128]{1,0:T(8,128)S(1)}, f32[512,128]{1,0:T(8,128)S(1)}, u32[]{:S(2)}, u32[]{:S(2)}) %collective-permute-start.9) | collective-permute-done | bytes 262176 | tf_op jit(solution)/shard_map/ppermute | solution.py:35
  132.4 0.7 copy-done.3
  133.1 2.4 %gram.1 = (f32[512,128]{1,0:T(8,128)}, f32[32,128]{1,0:T(8,128)}) custom-call(f32[512,128]{1,0:T(8,128)} %get-tuple-element.32.own, f32[512,128]{1,0:T(8,128)} %copy-done.2, f32[512,128]{1,0:T(8,128)} %copy-done.3, f32[512,128]{1,0:T(8,128)} %pad_maximum_fusion.4.weight), custom_call_target="tpu_custom_call" | custom-call | tf_op jit(solution)/shard_map/gram/pallas_call | solution.py:366
  135.5 4.8 %collective-permute-start.10 = (f32[32,128]{1,0:T(8,128)}, f32[32,128]{1,0:T(8,128)S(1)}, u32[]{:S(2)}, u32[]{:S(2)}) collective-permute-start(f32[32,128]{1,0:T(8,128)} %get-tuple-element.22), channel_id=1, source_target_pairs={{0,1},{1,0},{2,3},{3,2},{4,5},{5,4},{6,7},{7,6},{8,9},{9,8},{10,11... | collective-permute-start | bytes 49160 | tf_op jit(solution)/shard_map/ppermute | solution.py:42
  140.2 1.0 collective-permute-done.10
  141.3 0.7 add.133
  142.0 1.6 collective-permute-start.11
  143.6 12.7 %collective-permute-start.12 = (f32[32,128]{1,0:T(8,128)S(1)}, f32[32,128]{1,0:T(8,128)S(1)}, u32[]{:S(2)}, u32[]{:S(2)}) collective-permute-start(f32[32,128]{1,0:T(8,128)S(1)} %add.133), channel_id=1, source_target_pairs={{0,4},{1,5},{2,6},{3,7},{4,0},{5,1},{6,2},{7,3},{8,12},{9,13},{10,... | collective-permute-start | bytes 49160 | tf_op jit(solution)/shard_map/ppermute | solution.py:42
  156.3 1.9 %collective-permute-done.12 = f32[32,128]{1,0:T(8,128)S(1)} collective-permute-done((f32[32,128]{1,0:T(8,128)S(1)}, f32[32,128]{1,0:T(8,128)S(1)}, u32[]{:S(2)}, u32[]{:S(2)}) %collective-permute-start.12) | collective-permute-done | bytes 16416 | tf_op jit(solution)/shard_map/ppermute | solution.py:42
  158.2 3.1 %collective-permute-done.13 = f32[32,128]{1,0:T(8,128)S(1)} collective-permute-done((f32[32,128]{1,0:T(8,128)S(1)}, f32[32,128]{1,0:T(8,128)S(1)}, u32[]{:S(2)}, u32[]{:S(2)}) %collective-permute-start.13) | collective-permute-done | bytes 16416 | tf_op jit(solution)/shard_map/ppermute | solution.py:42
  161.4 2.6 %collective-permute-start.15 = (f32[32,128]{1,0:T(8,128)S(1)}, f32[32,128]{1,0:T(8,128)S(1)}, u32[]{:S(2)}, u32[]{:S(2)}) collective-permute-start(f32[32,128]{1,0:T(8,128)S(1)} %add_add_fusion.1), channel_id=1, source_target_pairs={{0,64},{16,80},{32,96},{48,112},{64,0},{80,16},{96,32},{112,48},{1... | collective-permute-start | bytes 49160 | tf_op jit(solution)/shard_map/ppermute | solution.py:42
  164.0 1.9 %collective-permute-start.16 = (f32[32,128]{1,0:T(8,128)S(1)}, f32[32,128]{1,0:T(8,128)S(1)}, u32[]{:S(2)}, u32[]{:S(2)}) collective-permute-start(f32[32,128]{1,0:T(8,128)S(1)} %add_add_fusion.1), channel_id=1, source_target_pairs={{0,96},{16,112},{32,64},{48,80},{64,32},{80,48},{96,0},{112,16},{1... | collective-permute-start | bytes 49160 | tf_op jit(solution)/shard_map/ppermute | solution.py:42
  166.0 0.7 collective-permute-done.15
  166.7 2.3 %collective-permute-done.16 = f32[32,128]{1,0:T(8,128)S(1)} collective-permute-done((f32[32,128]{1,0:T(8,128)S(1)}, f32[32,128]{1,0:T(8,128)S(1)}, u32[]{:S(2)}, u32[]{:S(2)}) %collective-permute-start.16) | collective-permute-done | bytes 16416 | tf_op jit(solution)/shard_map/ppermute | solution.py:42
  169.4 3.3 %collective-permute-done.17 = f32[32,128]{1,0:T(8,128)S(1)} collective-permute-done((f32[32,128]{1,0:T(8,128)S(1)}, f32[32,128]{1,0:T(8,128)S(1)}, u32[]{:S(2)}, u32[]{:S(2)}) %collective-permute-start.17) | collective-permute-done | bytes 16416 | tf_op jit(solution)/shard_map/ppermute | solution.py:42
  172.7 5.2 %collective-permute-done.18 = f32[32,128]{1,0:T(8,128)S(1)} collective-permute-done((f32[32,128]{1,0:T(8,128)S(1)}, f32[32,128]{1,0:T(8,128)S(1)}, u32[]{:S(2)}, u32[]{:S(2)}) %collective-permute-start.18) | collective-permute-done | bytes 16416 | tf_op jit(solution)/shard_map/ppermute | solution.py:42
  178.0 0.6 add.141.refs_0_
  178.6 8.4 %factor.1 = (f32[64,1024]{1,0:T(8,128)}, f32[64,64]{1,0:T(8,128)}) custom-call(f32[32,128]{1,0:T(8,128)} %add.141.refs_0_, f32[512,128]{1,0:T(8,128)} %get-tuple-element.23.refs_1_), custom_call_target="tpu_custom_call" | custom-call | tf_op jit(solution)/shard_map/factor/pallas_call | solution.py:418
  (39 shorter events, 1.6 us)
Async XLA Ops:
  0.6 14.0 %copy-start.1 = (f32[12,36,64]{2,1,0:T(8,128)S(1)}, f32[12,36,64]{2,1,0:T(8,128)}, u32[]{:S(2)}) copy-start(f32[12,36,64]{2,1,0:T(8,128)} %param.10) | copy-start | bytes 331780
  0.6 20.8 %collective-permute-start = (s32[1024]{0:T(1024)}, s32[1024]{0:T(1024)S(1)}, u32[]{:S(2)}, u32[]{:S(2)}) collective-permute-start(s32[1024]{0:T(1024)} %param.15), channel_id=1, source_target_pairs={{1,0},{2,1},{3,2},{4,3},{5,4},{6,5},{7,6},{8,7},{9,8},{10,9},{11,1... | collective-permute-start | bytes 12296 | tf_op jit(solution)/shard_map/ppermute | solution.py:35
  2.1 22.8 %collective-permute-start.1 = (s32[1024]{0:T(1024)}, s32[1024]{0:T(1024)S(1)}, u32[]{:S(2)}, u32[]{:S(2)}) collective-permute-start(s32[1024]{0:T(1024)} %param.15), channel_id=1, source_target_pairs={{0,1},{1,2},{2,3},{3,4},{4,5},{5,6},{6,7},{7,8},{8,9},{9,10},{10,1... | collective-permute-start | bytes 12296 | tf_op jit(solution)/shard_map/ppermute | solution.py:35
  8.6 16.4 %copy-start = (f32[1,12,36,47]{2,3,1,0:T(8,128)}, f32[1,12,36,47]{2,3,1,0:T(8,128)S(1)}, u32[]{:S(2)}) copy-start(f32[1,12,36,47]{2,3,1,0:T(8,128)S(1)} %scatter.4) | copy-start | bytes 243652
  9.4 15.5 %collective-permute-start.4 = (f32[3,4,36,47]{2,3,1,0:T(8,128)}, f32[3,4,36,47]{2,3,1,0:T(8,128)}, u32[]{:S(2)}, u32[]{:S(2)}) collective-permute-start(f32[3,4,36,47]{2,3,1,0:T(8,128)} %get-tuple-element.28), channel_id=1, source_target_pairs={{0,1},{1,2},{2,3},{3,4},{4,5},{5,6},{6,7},{7,8},{8,9},{9,10},{10,1... | collective-permute-start | bytes 243656 | tf_op jit(solution)/shard_map/ppermute | solution.py:35
  13.3 11.7 %collective-permute-start.5 = (f32[3,4,36,47]{2,3,1,0:T(8,128)S(1)}, f32[3,4,36,47]{2,3,1,0:T(8,128)}, u32[]{:S(2)}, u32[]{:S(2)}) collective-permute-start(f32[3,4,36,47]{2,3,1,0:T(8,128)S(1)} %get-tuple-element.29), channel_id=1, source_target_pairs={{1,0},{2,1},{3,2},{4,3},{5,4},{6,5},{7,6},{8,7},{9,8},{10,9},{11,1... | collective-permute-start | bytes 243656 | tf_op jit(solution)/shard_map/ppermute | solution.py:35
  15.2 4.7 %copy-start.5 = (s32[1024]{0:T(1024)S(1)}, s32[1024]{0:T(1024)}, u32[]{:S(2)}) copy-start(s32[1024]{0:T(1024)} %param.15) | copy-start | bytes 12292
  15.2 5.4 %copy-start.4 = (f32[1024]{0:T(1024)S(1)}, f32[1024]{0:T(1024)}, u32[]{:S(2)}) copy-start(f32[1024]{0:T(1024)} %param.16) | copy-start | bytes 12292
  18.3 83.9 %collective-permute-start.2 = (f32[6,4,48,128]{3,2,1,0:T(8,128)}, f32[6,4,48,128]{3,2,1,0:T(8,128)}, u32[]{:S(2)}, u32[]{:S(2)}) collective-permute-start(f32[6,4,48,128]{3,2,1,0:T(8,128)} %get-tuple-element.20), channel_id=1, source_target_pairs={{0,16},{16,32},{32,48},{48,64},{64,80},{80,96},{96,112},{112,0},{1... | collective-permute-start | bytes 1769480 | tf_op jit(solution)/shard_map/ppermute | solution.py:35
  21.4 80.9 %collective-permute-start.3 = (f32[6,4,48,128]{3,2,1,0:T(8,128)}, f32[6,4,48,128]{3,2,1,0:T(8,128)}, u32[]{:S(2)}, u32[]{:S(2)}) collective-permute-start(f32[6,4,48,128]{3,2,1,0:T(8,128)} %get-tuple-element.21), channel_id=1, source_target_pairs={{0,112},{16,0},{32,16},{48,32},{64,48},{80,64},{96,80},{112,96},{1... | collective-permute-start | bytes 1769480 | tf_op jit(solution)/shard_map/ppermute | solution.py:35
  27.9 24.7 %collective-permute-start.6 = (f32[3,20,4,47]{3,2,1,0:T(4,128)}, f32[3,20,4,47]{3,2,1,0:T(4,128)S(1)}, u32[]{:S(2)}, u32[]{:S(2)}) collective-permute-start(f32[3,20,4,47]{3,2,1,0:T(4,128)} %copy.16), channel_id=1, source_target_pairs={{0,16},{16,32},{32,48},{48,64},{64,80},{80,96},{96,112},{112,0},{1... | collective-permute-start | bytes 135368 | tf_op jit(solution)/shard_map/ppermute | solution.py:35
  28.5 25.5 %collective-permute-start.7 = (f32[3,20,4,47]{3,2,1,0:T(4,128)S(1)}, f32[3,20,4,47]{3,2,1,0:T(4,128)}, u32[]{:S(2)}, u32[]{:S(2)}) collective-permute-start(f32[3,20,4,47]{3,2,1,0:T(4,128)S(1)} %copy.17), channel_id=1, source_target_pairs={{0,112},{16,0},{32,16},{48,32},{64,48},{80,64},{96,80},{112,96},{1... | collective-permute-start | bytes 135368 | tf_op jit(solution)/shard_map/ppermute | solution.py:35
  125.8 4.4 %collective-permute-start.8 = (f32[512,128]{1,0:T(8,128)S(1)}, f32[512,128]{1,0:T(8,128)S(1)}, u32[]{:S(2)}, u32[]{:S(2)}) collective-permute-start(f32[512,128]{1,0:T(8,128)S(1)} %get-tuple-element.31), channel_id=1, source_target_pairs={{0,1},{1,2},{2,3},{3,4},{4,5},{5,6},{6,7},{7,8},{8,9},{9,10},{10,1... | collective-permute-start | bytes 786440 | tf_op jit(solution)/shard_map/ppermute | solution.py:35
  127.8 4.6 %collective-permute-start.9 = (f32[512,128]{1,0:T(8,128)S(1)}, f32[512,128]{1,0:T(8,128)S(1)}, u32[]{:S(2)}, u32[]{:S(2)}) collective-permute-start(f32[512,128]{1,0:T(8,128)S(1)} %get-tuple-element.30), channel_id=1, source_target_pairs={{1,0},{2,1},{3,2},{4,3},{5,4},{6,5},{7,6},{8,7},{9,8},{10,9},{11,1... | collective-permute-start | bytes 786440 | tf_op jit(solution)/shard_map/ppermute | solution.py:35
  130.2 2.2 %copy-start.2 = (f32[512,128]{1,0:T(8,128)}, f32[512,128]{1,0:T(8,128)S(1)}, u32[]{:S(2)}) copy-start(f32[512,128]{1,0:T(8,128)S(1)} %collective-permute-done.8.from_south) | copy-start | bytes 786436
  132.4 0.7 copy-start.3
  135.5 5.8 %collective-permute-start.10 = (f32[32,128]{1,0:T(8,128)}, f32[32,128]{1,0:T(8,128)S(1)}, u32[]{:S(2)}, u32[]{:S(2)}) collective-permute-start(f32[32,128]{1,0:T(8,128)} %get-tuple-element.22), channel_id=1, source_target_pairs={{0,1},{1,0},{2,3},{3,2},{4,5},{5,4},{6,7},{7,6},{8,9},{9,8},{10,11... | collective-permute-start | bytes 49160 | tf_op jit(solution)/shard_map/ppermute | solution.py:42
  142.0 14.3 %collective-permute-start.11 = (f32[32,128]{1,0:T(8,128)S(1)}, f32[32,128]{1,0:T(8,128)S(1)}, u32[]{:S(2)}, u32[]{:S(2)}) collective-permute-start(f32[32,128]{1,0:T(8,128)S(1)} %add.133), channel_id=1, source_target_pairs={{0,2},{1,3},{2,0},{3,1},{4,6},{5,7},{6,4},{7,5},{8,10},{9,11},{10,... | collective-permute-start | bytes 49160 | tf_op jit(solution)/shard_map/ppermute | solution.py:42
  143.6 14.6 %collective-permute-start.12 = (f32[32,128]{1,0:T(8,128)S(1)}, f32[32,128]{1,0:T(8,128)S(1)}, u32[]{:S(2)}, u32[]{:S(2)}) collective-permute-start(f32[32,128]{1,0:T(8,128)S(1)} %add.133), channel_id=1, source_target_pairs={{0,4},{1,5},{2,6},{3,7},{4,0},{5,1},{6,2},{7,3},{8,12},{9,13},{10,... | collective-permute-start | bytes 49160 | tf_op jit(solution)/shard_map/ppermute | solution.py:42
  156.3 4.9 %collective-permute-start.13 = (f32[32,128]{1,0:T(8,128)S(1)}, f32[32,128]{1,0:T(8,128)S(1)}, u32[]{:S(2)}, u32[]{:S(2)}) collective-permute-start(f32[32,128]{1,0:T(8,128)S(1)} %add.133), channel_id=1, source_target_pairs={{0,6},{1,7},{2,4},{3,5},{4,2},{5,3},{6,0},{7,1},{8,14},{9,15},{10,... | collective-permute-start | bytes 49160 | tf_op jit(solution)/shard_map/ppermute | solution.py:42
  161.3 4.7 %collective-permute-start.14 = (f32[32,128]{1,0:T(8,128)S(1)}, f32[32,128]{1,0:T(8,128)S(1)}, u32[]{:S(2)}, u32[]{:S(2)}) collective-permute-start(f32[32,128]{1,0:T(8,128)S(1)} %add_add_fusion.1), channel_id=1, source_target_pairs={{0,32},{16,48},{32,0},{48,16},{64,96},{80,112},{96,64},{112,80},{1... | collective-permute-start | bytes 49160 | tf_op jit(solution)/shard_map/ppermute | solution.py:42
  161.4 5.2 %collective-permute-start.15 = (f32[32,128]{1,0:T(8,128)S(1)}, f32[32,128]{1,0:T(8,128)S(1)}, u32[]{:S(2)}, u32[]{:S(2)}) collective-permute-start(f32[32,128]{1,0:T(8,128)S(1)} %add_add_fusion.1), channel_id=1, source_target_pairs={{0,64},{16,80},{32,96},{48,112},{64,0},{80,16},{96,32},{112,48},{1... | collective-permute-start | bytes 49160 | tf_op jit(solution)/shard_map/ppermute | solution.py:42
  164.0 4.9 %collective-permute-start.16 = (f32[32,128]{1,0:T(8,128)S(1)}, f32[32,128]{1,0:T(8,128)S(1)}, u32[]{:S(2)}, u32[]{:S(2)}) collective-permute-start(f32[32,128]{1,0:T(8,128)S(1)} %add_add_fusion.1), channel_id=1, source_target_pairs={{0,96},{16,112},{32,64},{48,80},{64,32},{80,48},{96,0},{112,16},{1... | collective-permute-start | bytes 49160 | tf_op jit(solution)/shard_map/ppermute | solution.py:42
  169.0 3.7 %collective-permute-start.17 = (f32[32,128]{1,0:T(8,128)S(1)}, f32[32,128]{1,0:T(8,128)S(1)}, u32[]{:S(2)}, u32[]{:S(2)}) collective-permute-start(f32[32,128]{1,0:T(8,128)S(1)} %add_add_fusion), channel_id=1, source_target_pairs={{0,16},{16,0},{32,48},{48,32},{64,80},{80,64},{96,112},{112,96},{1... | collective-permute-start | bytes 49160 | tf_op jit(solution)/shard_map/ppermute | solution.py:42
  172.7 5.2 %collective-permute-start.18 = (f32[32,128]{1,0:T(8,128)S(1)}, f32[32,128]{1,0:T(8,128)S(1)}, u32[]{:S(2)}, u32[]{:S(2)}) collective-permute-start(f32[32,128]{1,0:T(8,128)S(1)} %add.140), channel_id=1, source_target_pairs={{0,8},{1,9},{2,10},{3,11},{4,12},{5,13},{6,14},{7,15},{8,0},{9,1},... | collective-permute-start | bytes 49160 | tf_op jit(solution)/shard_map/ppermute | solution.py:42

commit v2 on v1

v2 whole, which is shorter than its diff:
```python
import jax
import jax.numpy as jnp
from jax import lax
from jax.experimental import pallas as pl
from jax.experimental.pallas import tpu as pltpu
from jax.sharding import PartitionSpec as P

STEPS = 4
BANDS, COLS, LEVS, PROBES = 12, 36, 47, 64
HALO = STEPS
TALL = BANDS + 2 * HALO
WIDE = COLS + 2 * HALO
LEVP = 48
TILES = LEVP // 8
COLP = 40
RING = 4
BLOCK = 4
LAT_ROWS = 3 * HALO * COLP
HALF = COLS // 2
PAIRS = HALF + 2 * HALO
SLOTS = 1024
FIELD_ROWS = TALL * HALF * LEVP
ZERO_ROW = FIELD_ROWS
F32 = jnp.float32
HIGHEST = lax.Precision.HIGHEST
MIB = 1024 * 1024


def params(mib=12):
    return pltpu.CompilerParams(vmem_limit_bytes=mib * MIB)


def whole(space=pltpu.VMEM):
    return pl.BlockSpec(memory_space=space)


def along(x, axis, step, wrap):
    size = lax.axis_size(axis)
    pairs = [(i, (i + step) % size) for i in range(size) if wrap or 0 <= i + step < size]
    return lax.ppermute(x, axis, pairs)


def all_sum(x):
    lats = lax.axis_size("lat")
    size = lats * lax.axis_size("lon")
    for bits in ((1,), (2, 4), (2 * lats, 4 * lats), (lats, 8)):
        masks = [bits[0]] if len(bits) == 1 else [bits[0], bits[1], bits[0] | bits[1]]
        terms = [lax.ppermute(x, ("lon", "lat"), [(i, i ^ m) for i in range(size)]) for m in masks]
        for term in terms:
            x = x + term
    return x


def pack_lat_kernel(u, v, mix, cells, to_south, to_north):
    for which, ref in enumerate((u, v, mix)):
        for band in range(HALO):
            at = (which * HALO + band) * COLP
            to_south[at : at + COLS, 0:LEVS] = ref[band]
            to_north[at : at + COLS, 0:LEVS] = ref[BANDS - HALO + band]
    for dst in (to_south, to_north):
        dst[LAT_ROWS:] = cells[...].astype(F32)


def pack_lat(u, v, mix, cells):
    out = jax.ShapeDtypeStruct((LAT_ROWS + 8, 128), F32)
    return pl.pallas_call(
        pack_lat_kernel,
        in_specs=[whole()] * 4,
        out_specs=[whole()] * 2,
        out_shape=[out, out],
        compiler_params=params(62),
        name="pack_lat",
    )(u, v, mix, cells.reshape(8, 128))


def pack_lon_kernel(west, east, south, north, to_west, to_east):
    for src, dst, col in ((west, to_west, 0), (east, to_east, COLS - HALO)):
        dst[:, HALO // 2 : (HALO + BANDS) // 2] = src[...]
        for which in range(3):
            for edge in range(HALO):
                row = (which * HALO + edge) * COLP + col
                at = HALO * (edge % 2)
                dst[which, edge // 2, at : at + HALO] = south[row : row + HALO]
                dst[which, (HALO + BANDS + edge) // 2, at : at + HALO] = north[row : row + HALO]


def pack_lon(west, east, south, north):
    out = jax.ShapeDtypeStruct((3, TALL // 2, 8, 128), F32)
    return pl.pallas_call(
        pack_lon_kernel,
        in_specs=[whole()] * 4,
        out_specs=[whole()] * 2,
        out_shape=[out, out],
        compiler_params=params(),
        name="pack_lon",
    )(west, east, south, north)


def order_levels(dst, at, src):
    for tile in range(TILES):
        dst[at + (slice(8 * tile, 8 * tile + 8),)] = src[pl.ds(tile, 8, stride=TILES)]


def flip(dst, at, rows, flat, first, last_level):
    flat[0:LEVS, first : first + rows.shape[0]] = rows.T
    if last_level:
        flat[LEVS - 1 : LEVS] = jnp.zeros((1, 128), F32)
    order_levels(dst, at, flat)


def level_tile(ref, at, tile):
    if tile < TILES - 1:
        return ref[at + (pl.ds(tile, 8, stride=TILES),)]
    part = ref[at + (pl.ds(tile, 7, stride=TILES),)]
    return jnp.concatenate([part, jnp.zeros((1, PROBES), F32)], axis=0)


def prepare_kernel(
    west, east, flux, u, v, mix, gains, coef, to_west, to_east, coef_west, coef_east, flat
):
    high = HALF - HALO
    none = jnp.zeros((BANDS, HALO, PROBES), F32)
    gains[:, 0:HALO, 0:PROBES] = none
    gains[:, HALO:, 0:PROBES] = flux[:, 0 : HALF + HALO]
    gains[:, 0 : HALF + HALO, PROBES:] = flux[:, high:]
    gains[:, HALF + HALO :, PROBES:] = none
    for dst, src, first in ((to_west, west, 0), (to_east, east, COLS - HALO)):

        def pack(band, carry):
            for k in range(2):
                for tile in range(TILES):
                    low, up = level_tile(src, (band, k), tile), level_tile(src, (band, k + 2), tile)
                    dst[band, k, 8 * tile : 8 * tile + 8] = jnp.concatenate([low, up], axis=1)
                at = first + k
                pair = jnp.concatenate([flux[band, at : at + 1], flux[band, at + 2 : at + 3]], axis=1)
                dst[band, k, LEVS:LEVP] = pair
            return carry

        lax.fori_loop(0, BANDS, pack, 0)
    flat[...] = jnp.zeros((LEVP, 128), F32)
    for which, ref in enumerate((u, v, mix)):
        for band in range(BANDS):
            flip(coef, (which, band), ref[band], flat, HALO, which == 2)
            at = HALO * (band % 2)
            coef_west[which, band // 2, at : at + HALO, 0:LEVS] = ref[band, 0:HALO]
            coef_east[which, band // 2, at : at + HALO, 0:LEVS] = ref[band, COLS - HALO :]


def prepare(conc, flux, u, v, mix):
    sds = lambda *shape: jax.ShapeDtypeStruct(shape, F32)
    edge = lambda at: pl.BlockSpec((BANDS, HALO, LEVS, PROBES), lambda i: (0, at, 0, 0))
    return pl.pallas_call(
        prepare_kernel,
        grid=(1,),
        in_specs=[edge(0), edge(COLS // HALO - 1)] + [whole()] * 4,
        out_specs=[whole()] * 6,
        out_shape=[
            sds(BANDS, PAIRS, 128),
            sds(3, BANDS, LEVP, 128),
            sds(BANDS, 2, LEVP, 128),
            sds(BANDS, 2, LEVP, 128),
            sds(3, BANDS // 2, 8, 128),
            sds(3, BANDS // 2, 8, 128),
        ],
        scratch_shapes=[pltpu.VMEM((LEVP, 128), F32)],
        compiler_params=params(62),
        name="prepare",
    )(conc, conc, flux, u, v, mix)


def row_code(cells, shift):
    rest = ((cells.astype(F32) + 0.5) * (1.0 / LEVS)).astype(jnp.int32)
    level = cells - rest * LEVS
    line = ((rest.astype(F32) + 0.5) * (1.0 / COLS)).astype(jnp.int32)
    col = rest - line * COLS
    group = ((level.astype(F32) + 0.5) * (1.0 / TILES)).astype(jnp.int32)
    band = line + HALO + shift
    held = (band >= 0) & (band < TALL)
    upper = (col >= HALF).astype(jnp.int32)
    row = (band * HALF + col - HALF * upper) * LEVP + (level - group * TILES) * 8 + group
    later = lax.broadcasted_iota(jnp.int32, cells.shape, 0) * 128 >= SLOTS // 2
    cross = (upper == 1) != later
    return jnp.where(held, row, ZERO_ROW), cross.astype(F32)


def margins_kernel(south, north, cells, coef, codes, turned, flat):
    places = (
        (cells[...], 0),
        (north[LAT_ROWS:].astype(jnp.int32), BANDS),
        (south[LAT_ROWS:].astype(jnp.int32), -BANDS),
    )
    lower = lax.broadcasted_iota(jnp.int32, (128, 128), 1) < PROBES
    for group, (at, shift) in enumerate(places):
        row, cross = row_code(at, shift)
        codes[8 * group : 8 * group + 8] = row
        column = jnp.concatenate([cross, jnp.zeros((120, 128), F32)], axis=0).T
        for k in range(4):
            low = jnp.broadcast_to(column[:, k : k + 1], (128, 128))
            high = jnp.broadcast_to(column[:, k + 4 : k + 5], (128, 128))
            turned[group, 128 * k : 128 * k + 128] = jnp.where(lower, low, high)
    flat[...] = jnp.zeros((LEVP, 128), F32)
    for which in range(3):
        for side, src in enumerate((south, north)):
            for band in range(HALO):
                at = (which * HALO + band) * COLP
                rows = src[at : at + COLS, 0:LEVS]
                flip(coef, (which, side * HALO + band), rows, flat, HALO, which == 2)


def margins(south, north, cells):
    return pl.pallas_call(
        margins_kernel,
        in_specs=[whole()] * 3,
        out_specs=[whole()] * 3,
        out_shape=[
            jax.ShapeDtypeStruct((3, 2 * HALO, LEVP, 128), F32),
            jax.ShapeDtypeStruct((24, 128), jnp.int32),
            jax.ShapeDtypeStruct((3, SLOTS // 2, 128), F32),
        ],
        scratch_shapes=[pltpu.VMEM((LEVP, 128), F32)],
        compiler_params=params(),
        name="margins",
    )(south, north, cells.reshape(8, 128))


def split_terms(x):
    doubled = x + pltpu.roll(x, 64, 1)
    high = doubled.astype(jnp.bfloat16).astype(F32)
    lane = lax.broadcasted_iota(jnp.int32, x.shape, 1)
    return jnp.where(lane < 64, high, doubled - high).astype(jnp.bfloat16)


def selector(tile, low, high, high_sign=1.0):
    shape = (128, 256)
    row = lax.broadcasted_iota(jnp.int32, shape, 0) & 63
    col = lax.broadcasted_iota(jnp.int32, shape, 1)
    pair = 2 * tile + (col >> 7)
    upper = ((col >> 6) & 1) == 1
    weight = jnp.where(upper, high_sign, 1.0)
    return jnp.where(row == jnp.where(upper, high(pair), low(pair)), weight, 0.0).astype(jnp.bfloat16)


def spread(ref, split, chosen, tile, first=0, count=TALL):
    out = jnp.dot(
        split[first * LEVP : (first + count) * LEVP], chosen, preferred_element_type=F32
    )
    out = out.reshape(count, 1, LEVP, 256)
    ref[first : first + count, pl.ds(2 * tile, 1)] = out[..., :128]
    ref[first : first + count, pl.ds(2 * tile + 1, 1)] = out[..., 128:]


def face_flux(speed, behind, ahead):
    return speed * jnp.where(speed > 0.0, behind, ahead)


def mix_levels(dst, line, mixing, at, pair):
    here = [line[pair, 8 * t : 8 * t + 8] for t in range(TILES)]
    above = here[1:] + [pltpu.roll(here[0], 7, 0)]
    moved = [
        mixing[at, pair, 8 * t : 8 * t + 8] * (above[t] - here[t]) for t in range(TILES)
    ]
    below = [pltpu.roll(moved[-1], 1, 0)] + moved[:-1]
    for t in range(TILES):
        dst[at, pair, 8 * t : 8 * t + 8] = here[t] + (moved[t] - below[t])


def join_coef(split, own, margin, west, east, sides, flat):
    for which in range(3):
        for side, src in enumerate((west, east)):
            flat[...] = jnp.zeros((LEVP, 128), F32)
            rows = src[which].reshape(TALL * HALO, 128)
            flat[0:LEVS, 0 : TALL * HALO] = rows.T[0:LEVS]
            if which == 2:
                flat[LEVS - 1 : LEVS] = jnp.zeros((1, 128), F32)
            order_levels(sides, (which, side), flat)
    lane = lax.broadcasted_iota(jnp.int32, (LEVP, 128), 1)

    def join(band, ref, at):
        for which in range(3):
            left = pltpu.roll(sides[which, 0], lax.rem(128 - HALO * band, 128), 1)
            right = pltpu.roll(sides[which, 1], lax.rem(128 + HALO + COLS - HALO * band, 128), 1)
            x = jnp.where(lane < HALO, left, ref[which, at])
            x = jnp.where(lane >= HALO + COLS, right, x)
            x = jnp.where(lane < WIDE, x, 0.0)
            split[which, pl.ds(pl.multiple_of(band * LEVP, LEVP), LEVP)] = split_terms(x)

    def inner(at, carry):
        join(at + HALO, own, at)
        return carry

    lax.fori_loop(0, BANDS, inner, 0)

    def outer(at, carry):
        join(at, margin, at)
        join(at + HALO + BANDS, margin, at + HALO)
        return carry

    lax.fori_loop(0, HALO, outer, 0)


def transport_kernel(
    conc, flux, own, margin, from_west, from_east, out, split,
    c, u, v, m, fs0, fs1, line, sides, flat, stage, in_sem, out_sem,
):
    def fetch(band):
        slot = lax.rem(band, RING)
        return pltpu.make_async_copy(conc.at[band], stage.at[slot], in_sem.at[slot])

    for band in range(RING):
        fetch(band).start()
    join_coef(split, own, margin, from_west, from_east, sides, flat)

    def expand(tile):
        chosen = selector(tile, lambda pair: pair, lambda pair: pair + HALF)
        half = TALL // 2
        for which, ref in enumerate((u, v, m)):
            for first in (0, half):
                yield lambda: spread(ref, split.at[which], chosen, tile, first, half)

    zero = jnp.zeros((8, PROBES), F32)

    def load(band, carry):
        slot = lax.rem(band, RING)
        fetch(band).wait()
        pieces = expand(band)
        for pair in range(PAIRS):
            low, high = pair - HALO, pair - HALO + HALF
            for t in range(TILES):
                left = level_tile(stage, (slot, low), t) if low >= 0 else zero
                right = level_tile(stage, (slot, high), t) if high < COLS else zero
                both = jnp.concatenate([left, right], axis=1)
                c[band + HALO, pair, 8 * t : 8 * t + 8] = both
            if pair % 4 == 3:
                next(pieces)()

        @pl.when(band + RING < BANDS)
        def _():
            fetch(band + RING).start()

        return carry

    lax.fori_loop(0, BANDS, load, 0)
    for piece in expand(BANDS):
        piece()

    def clear(band, carry):
        c[band] = jnp.zeros((PAIRS, LEVP, 128), F32)
        c[band + HALO + BANDS] = jnp.zeros((PAIRS, LEVP, 128), F32)
        return carry

    lax.fori_loop(0, HALO, clear, 0)

    def save(band):
        return pltpu.make_async_copy(c.at[band, pl.ds(HALO, HALF)], out.at[band], out_sem.at[band])

    for step in range(1, STEPS + 1):
        first, last = step, PAIRS - step
        count = last - first
        chunk = count

        def gain(band, carry):
            for pair in range(PAIRS):
                c[band + HALO, pair, 0:1] = c[band + HALO, pair, 0:1] + flux[band, pair : pair + 1]
            return carry

        lax.fori_loop(0, BANDS, gain, 0)
        fs0[first:last] = jnp.zeros((count, LEVP, 128), F32)

        def row(band, below, above):
            north = jnp.minimum(band + 1, TALL - 1)
            here = c[band, first]
            west = face_flux(u[band, first], c[band, first - 1], here)

            def some(at, state):
                here, west = state
                for k in range(chunk):
                    pair = first + at * chunk + k
                    ahead = c[band, pair + 1]
                    east = face_flux(u[band, pair + 1], here, ahead)
                    top = face_flux(v[north, pair], here, c[north, pair])
                    line[pair] = here + (west - east) + (below[pair] - top)
                    above[pair] = top
                    here, west = ahead, east
                return here, west

            lax.fori_loop(0, count // chunk, some, (here, west))

            def level(at, carry):
                for k in range(chunk):
                    pair = first + at * chunk + k
                    mix_levels(c, line, m, band, pair)
                return carry

            lax.fori_loop(0, count // chunk, level, 0)
            if step == STEPS:
                save(band).start()

        def rows(at, carry):
            band = HALO - step + 2 * at
            row(band, fs0, fs1)
            row(band + 1, fs1, fs0)
            return carry

        lax.fori_loop(0, (BANDS + 2 * step) // 2, rows, 0)

    def drain(band, carry):
        save(band).wait()
        return carry

    lax.fori_loop(0, TALL, drain, 0)


def transport(conc, flux, own, margin, from_west, from_east):
    field = pltpu.VMEM((TALL, PAIRS, LEVP, 128), F32)
    line = pltpu.VMEM((PAIRS, LEVP, 128), F32)
    return pl.pallas_call(
        transport_kernel,
        in_specs=[whole(pl.ANY)] + [whole()] * 5,
        out_specs=[whole(pl.ANY), whole()],
        out_shape=[
            jax.ShapeDtypeStruct((TALL, HALF, LEVP, 128), F32),
            jax.ShapeDtypeStruct((3, TALL * LEVP, 128), jnp.bfloat16),
        ],
        scratch_shapes=[
            field,
            field,
            field,
            field,
            line,
            line,
            line,
            pltpu.VMEM((3, 2, LEVP, 128), F32),
            pltpu.VMEM((LEVP, 128), F32),
            pltpu.VMEM((RING, COLS, LEVS, PROBES), F32),
            pltpu.SemaphoreType.DMA((RING,)),
            pltpu.SemaphoreType.DMA((TALL,)),
        ],
        compiler_params=params(62),
        name="transport",
    )(conc, flux, own, margin, from_west, from_east)


def strips_kernel(
    codes, turned, west, east, split, field, own, north, south,
    c, u, v, m, fs0, fs1, line, gain, full, got0, got1, got2, sem,
):
    fetch = pltpu.make_async_copy(field, full.at[pl.ds(0, FIELD_ROWS)], sem)
    fetch.start()

    def expand(tile, carry):
        faces = selector(tile, lambda k: k, lambda k: WIDE - k, -1.0)
        cells = selector(tile, lambda k: k, lambda k: WIDE - 1 - k)
        for which, ref in enumerate((u, v, m)):
            spread(ref, split.at[which], cells if which else faces, tile)
        return carry

    lax.fori_loop(0, HALO, expand, 0)

    def clear(band, carry):
        c[band] = jnp.zeros((2 * HALO, LEVP, 128), F32)
        return carry

    lax.fori_loop(0, TALL, clear, 0)
    lower = lax.broadcasted_iota(jnp.int32, (LEVP, 128), 1) < PROBES
    inside = lax.broadcasted_iota(jnp.int32, (LEVP, 128), 0) < LEVS

    def place(band, carry):
        for k in range(2):
            left, right = west[band, k], east[band, 1 - k]
            outer = jnp.where(lower, left, right)
            inner = pltpu.roll(jnp.where(lower, right, left), PROBES, 1)
            for at, value in ((k, outer), (k + 2, inner)):
                c[band + HALO, at] = jnp.where(inside, value, 0.0)
                gain[band, at, 0:1] = value[LEVS:LEVP]
        return carry

    lax.fori_loop(0, BANDS, place, 0)

    full[ZERO_ROW : ZERO_ROW + 8] = jnp.zeros((8, 128), F32)

    for step in range(1, STEPS + 1):
        region = range(step, step + HALO)

        def add(band, carry):
            for k in range(step - 1, HALO):
                c[band + HALO, k, 0:1] = c[band + HALO, k, 0:1] + gain[band, k, 0:1]
            return carry

        lax.fori_loop(0, BANDS, add, 0)
        for k in region:
            fs0[k] = jnp.zeros((LEVP, 128), F32)

        def row(band, below, above):
            north = jnp.minimum(band + 1, TALL - 1)
            here = c[band, step]
            behind = face_flux(u[band, step], c[band, step - 1], here)
            for k in region:
                if k < step + HALO - 1:
                    ahead = c[band, k + 1]
                    front = face_flux(u[band, k + 1], here, ahead)
                    net = behind - front
                else:
                    net = behind
                top = face_flux(v[north, k], here, c[north, k])
                line[k] = here + net + (below[k] - top)
                above[k] = top
                here, behind = ahead, front
            for k in region:
                mix_levels(c, line, m, band, k)

        def rows(at, carry):
            band = HALO - step + 2 * at
            row(band, fs0, fs1)
            row(band + 1, fs1, fs0)
            return carry

        lax.fori_loop(0, (BANDS + 2 * step) // 2, rows, 0)

    fetch.wait()

    def merge(band, carry):
        base = band * (HALF * LEVP)
        spots, sums = [], []
        for k in range(HALO):
            share = c[band, HALO + k]
            for pair, keep in ((k, lower), (HALF - 1 - k, ~lower)):
                rows = pl.ds(pl.multiple_of(base + pair * LEVP, LEVP), LEVP)
                spots.append(rows)
                sums.append(full[rows] + jnp.where(keep, share, 0.0))
        for rows, value in zip(spots, sums):
            full[rows] = value
        return carry

    lax.fori_loop(0, TALL, merge, 0)

    left_lanes = lax.broadcasted_iota(jnp.int32, (8, 128), 1) < PROBES
    for group, (out, buffer) in enumerate(((own, got0), (north, got1), (south, got2))):

        def pick(at, carry):
            rows = buffer.at[pl.ds(pl.multiple_of(at * 128, 128), 128)]
            for k in range(128):
                rows[k : k + 1] = full[pl.ds(codes[group * 8 + at, k], 1)]
            return carry

        lax.fori_loop(0, SLOTS // 128, pick, 0)

        def join(at, carry):
            for k in range(16):
                at8 = pl.multiple_of(at * 128 + k * 8, 8)
                one, two = buffer[pl.ds(at8, 8)], buffer[pl.ds(at8 + SLOTS // 2, 8)]
                straight = jnp.where(left_lanes, one, two)
                crossed = pltpu.roll(jnp.where(left_lanes, two, one), PROBES, 1)
                out[pl.ds(at8, 8)] = jnp.where(turned[group, pl.ds(at8, 8)] > 0.5, crossed, straight)
            return carry

        lax.fori_loop(0, SLOTS // 256, join, 0)


def strips(codes, turned, west, east, split, field):
    strip = pltpu.VMEM((TALL, 2 * HALO, LEVP, 128), F32)
    line = pltpu.VMEM((2 * HALO, LEVP, 128), F32)
    buffer = pltpu.VMEM((SLOTS, 128), F32)
    return pl.pallas_call(
        strips_kernel,
        in_specs=[whole(pltpu.SMEM), whole(), whole(), whole(), whole(), whole(pl.ANY)],
        out_specs=[whole()] * 3,
        out_shape=[jax.ShapeDtypeStruct((SLOTS // 2, 128), F32)] * 3,
        scratch_shapes=[
            strip,
            strip,
            strip,
            strip,
            line,
            line,
            line,
            pltpu.VMEM((BANDS, HALO, 8, 128), F32),
            pltpu.VMEM((FIELD_ROWS + 8, 128), F32),
            buffer,
            buffer,
            buffer,
            pltpu.SemaphoreType.DMA,
        ],
        compiler_params=params(62),
        name="strips",
    )(codes, turned, west, east, split, field)


def gram_kernel(own, from_south, from_north, weight, images, gram):
    rows = (own[...] + from_south[...] + from_north[...]) * weight[...]
    images[...] = rows
    both = lax.dot_general(
        rows, rows, (((0,), (0,)), ((), ())), precision=HIGHEST, preferred_element_type=F32
    )
    total = both[:PROBES, :PROBES] + both[PROBES:, PROBES:]
    gram[:, 0:PROBES] = total[: PROBES // 2]
    gram[:, PROBES:] = total[PROBES // 2 :]


def gram_of(own, from_south, from_north, weight):
    return pl.pallas_call(
        gram_kernel,
        in_specs=[whole()] * 4,
        out_specs=[whole()] * 2,
        out_shape=[
            jax.ShapeDtypeStruct((SLOTS // 2, 128), F32),
            jax.ShapeDtypeStruct((PROBES // 2, 128), F32),
        ],
        compiler_params=params(),
        name="gram",
    )(own, from_south, from_north, weight)


def factor_kernel(root, gram, images, basis_t, factor, work, pivots):
    sublane = lax.broadcasted_iota(jnp.int32, (8, 128), 0)
    half = PROBES // 2
    work[0:half, 0:PROBES] = gram[:, 0:PROBES]
    work[half:, 0:PROBES] = gram[:, PROBES:]
    diagonal = (
        lax.broadcasted_iota(jnp.int32, (PROBES, PROBES), 0)
        == lax.broadcasted_iota(jnp.int32, (PROBES, PROBES), 1)
    )
    work[:, PROBES:] = diagonal.astype(F32)
    tiles = [work[8 * t : 8 * t + 8] for t in range(PROBES // 8)]
    for first in range(0, PROBES, BLOCK):
        top = first // 8
        live = range(top, PROBES // 8)
        column = {
            (j, t): jnp.broadcast_to(tiles[t][:, first + j : first + j + 1], (8, 128))
            for j in range(BLOCK)
            for t in live
        }
        for j in range(BLOCK):
            at = first + j
            pick = lambda tile, n: jnp.broadcast_to(tile[n % 8 : n % 8 + 1], (8, 128))
            inverse = 1.0 / pick(column[j, top], at)
            pivots[at : at + 1] = column[j, top][at % 8 : at % 8 + 1]
            pivot = pick(tiles[top], at) * inverse
            later = [pick(column[j, top], first + i) * inverse for i in range(j + 1, BLOCK)]
            for t in live:
                share = column[j, t]
                if t == top:
                    share = jnp.where(sublane > at % 8, share, 0.0)
                tiles[t] = tiles[t] - share * pivot
                for i in range(j + 1, BLOCK):
                    column[i, t] = column[i, t] - share * later[i - j - 1]
    for t in range(PROBES // 8):
        rows = slice(8 * t, 8 * t + 8)
        work[rows] = tiles[t] * (1.0 / jnp.sqrt(pivots[rows]))
    both = work[...]
    row = lax.broadcasted_iota(jnp.int32, (PROBES, PROBES), 0)
    col = lax.broadcasted_iota(jnp.int32, (PROBES, PROBES), 1)
    factor[...] = jnp.where(col >= row, both[:, :PROBES], 0.0) * (1.0 / root)
    inverse_t = jnp.where(col <= row, both[:, PROBES:], 0.0) * root
    zero = jnp.zeros((PROBES, PROBES), F32)
    twice = jnp.concatenate(
        [
            jnp.concatenate([inverse_t, zero], axis=1),
            jnp.concatenate([zero, inverse_t], axis=1),
        ],
        axis=0,
    )
    basis = lax.dot_general(
        twice, images[...], (((1,), (1,)), ((), ())), precision=HIGHEST, preferred_element_type=F32
    )
    basis_t[:, 0 : SLOTS // 2] = basis[:PROBES]
    basis_t[:, SLOTS // 2 :] = basis[PROBES:]


def factor_of(gram, images, root):
    return pl.pallas_call(
        lambda *refs: factor_kernel(root, *refs),
        in_specs=[whole()] * 2,
        out_specs=[whole()] * 2,
        out_shape=[
            jax.ShapeDtypeStruct((PROBES, SLOTS), F32),
            jax.ShapeDtypeStruct((PROBES, PROBES), F32),
        ],
        scratch_shapes=[pltpu.VMEM((PROBES, 128), F32)] * 2,
        compiler_params=params(),
        name="factor",
    )(gram, images)


def on_device(
    flux_probes, conc_start, u_courant, v_courant, vert_mix, obs_cell, obs_weight, obs_count
):
    to_south, to_north = pack_lat(u_courant, v_courant, vert_mix, obs_cell)
    from_south = along(to_north, "lat", 1, False)
    from_north = along(to_south, "lat", -1, False)
    flux, own, edge_west, edge_east, coef_west, coef_east = prepare(
        conc_start, flux_probes, u_courant, v_courant, vert_mix
    )
    to_west, to_east = pack_lon(coef_west, coef_east, from_south, from_north)
    from_west = along(to_east, "lon", 1, True)
    from_east = along(to_west, "lon", -1, True)
    margin, codes, turned = margins(from_south, from_north, obs_cell)
    edge_west, edge_east, from_west, from_east = lax.optimization_barrier(
        (edge_west, edge_east, from_west, from_east)
    )
    west_field = along(edge_east, "lon", 1, True)
    east_field = along(edge_west, "lon", -1, True)
    field, split = transport(conc_start, flux, own, margin, from_west, from_east)
    rows, for_north, for_south = strips(
        codes, turned, west_field, east_field, split, field.reshape(FIELD_ROWS, 128)
    )
    south_rows = along(for_north, "lat", 1, False)
    north_rows = along(for_south, "lat", -1, False)
    live = jnp.arange(SLOTS, dtype=jnp.int32) < obs_count[0]
    scale = jnp.where(live, obs_weight, 0.0)
    lanes = (SLOTS // 2, PROBES)
    weight = jnp.concatenate(
        [
            jnp.broadcast_to(scale[: SLOTS // 2, None], lanes),
            jnp.broadcast_to(scale[SLOTS // 2 :, None], lanes),
        ],
        axis=1,
    )
    images, gram = gram_of(rows, south_rows, north_rows, weight)
    gram = all_sum(gram)
    total_rows = SLOTS * lax.axis_size("lon") * lax.axis_size("lat")
    basis_t, factor = factor_of(gram, images, float(total_rows) ** 0.5)
    return basis_t.T, factor


def solution(mesh):
    in_specs = (
        P("lat", "lon", None),
        P("lat", "lon", None, None),
        P("lat", "lon", None),
        P("lat", "lon", None),
        P("lat", "lon", None),
        P(("lon", "lat")),
        P(("lon", "lat")),
        P(("lon", "lat")),
    )
    out_specs = (P(("lon", "lat"), None), P())
    return jax.shard_map(
        on_device, mesh=mesh, in_specs=in_specs, out_specs=out_specs, check_vma=False
    )
```

time: 188 us -> 127 us (0.68)
  waiting for transfers between devices: 39.8 us -> 18.3 us
  Pallas kernels: 78.9 us -> 58 us
  other arithmetic: 7.69 us -> 0.17 us
  local copies, waits for them, and re-layouts: 12.8 us -> 6.34 us
  starting transfers between devices: 46.2 us -> 42.2 us
    ppermute x10 -> x8, waiting for transfers between devices: 22.2 us -> 8.2 us  [along(): return lax.ppermute(x, axis, pairs)]
    pallas_call x1, Pallas kernels: 21.6 us -> 13.5 us  [strips(): pl.pallas_call(strips_kernel, in_specs=[whole(pltpu.SMEM), whole(), whole...]
    ppermute x9 -> x10, waiting for transfers between devices: 17.6 us -> 10.1 us  [all_sum(): lax.ppermute(x, ('lon', 'lat'), [(i, i ^ m) for i in range(size)])]
    pallas_call x2 -> x5, Pallas kernels: 46.6 us -> 40 us  [the longest x1 31.4 us: transport(): pl.pallas_call(transport_kernel, in_specs=[whole(pl.ANY)] + [whole()] * 5...]
    ppermute x10 -> x8, starting transfers between devices: 22 us -> 17.2 us  [along(): return lax.ppermute(x, axis, pairs)]
    pallas_call x1, Pallas kernels: 8.37 us -> 3.97 us  [factor_of(): pl.pallas_call(lambda *refs: factor_kernel(root, *refs), in_specs=[whole(...]
    slice x5 -> x0, local copies, waits for them, and re-layouts: 2.96 us -> none  [the longest x2 1.68 us: on_device(): from_west = along(tall[:, :, -HALO:], 'lon', 1, True)]
    ppermute x2 -> x0, local copies, waits for them, and re-layouts: 2.19 us -> none  [along(): return lax.ppermute(x, axis, pairs)]
  transfers between devices with their start and end apart: 19 -> 18, of which waited for: 10 -> 12; matrix products, arithmetic and copies ran while one was open for 9% -> 0% of each run, Pallas kernels for 25% -> 30%
where the time goes in v2:
time: 127 us
  Pallas kernels  58 us (46%)
  starting transfers between devices  42.2 us (33%)
  waiting for transfers between devices  18.3 us (14%)
  local copies, waits for them, and re-layouts  6.34 us (5%)
  between operations  1.5 us (1%)
    pallas_call x1, Pallas kernels, transport(): pl.pallas_call(transport_kernel, in_specs=[whole(pl.ANY)] + [whole()] * 5...  31.4 us
    ppermute x10, starting transfers between devices, all_sum(): lax.ppermute(x, ('lon', 'lat'), [(i, i ^ m) for i in range(size)])  25 us
    ppermute x8, starting transfers between devices, along(): return lax.ppermute(x, axis, pairs)  17.2 us
    pallas_call x1, Pallas kernels, strips(): pl.pallas_call(strips_kernel, in_specs=[whole(pltpu.SMEM), whole(), whole...  13.5 us
    ppermute x10, waiting for transfers between devices, all_sum(): lax.ppermute(x, ('lon', 'lat'), [(i, i ^ m) for i in range(size)])  10.1 us
    ppermute x8, waiting for transfers between devices, along(): return lax.ppermute(x, axis, pairs)  8.2 us
    unnamed x24, local copies, waits for them, and re-layouts  6.09 us
    pallas_call x1, Pallas kernels, prepare(): pl.pallas_call(prepare_kernel, grid=(1,), in_specs=[edge(0), edge(COLS //...  5.75 us
  transfers between devices with their start and end apart: 18, of which 12 were waited for; matrix products, arithmetic and copies ran while one was open for 0% of the time, Pallas kernels for 30%

profile of v2, /device:TPU:0, one launch (start us, length us, event | category | flops | bytes accessed | tf_op | source)
XLA Modules:
  0.0 126.5 jit_solution(18383799206517314377)
XLA Ops:
  0.6 2.0 %pack_lat.1 = (f32[488,128]{1,0:T(8,128)}, f32[488,128]{1,0:T(8,128)}) custom-call(f32[12,36,47]{2,1,0:T(8,128)} %u.3, f32[12,36,47]{2,1,0:T(8,128)} %v.3, f32[12,36,47]{2,1,0:T(8,128)} %mix.3, s32[8,128]{1,0:T(8,128)} %bitcast.5), custom_call_target="tpu_custom_call" | custom-call | tf_op jit(solution)/shard_map/pack_lat/pallas_call | solution.py:66
  2.6 1.3 %collective-permute-start = (f32[488,128]{1,0:T(8,128)}, f32[488,128]{1,0:T(8,128)S(1)}, u32[]{:S(2)}, u32[]{:S(2)}) collective-permute-start(f32[488,128]{1,0:T(8,128)} %get-tuple-element.28), channel_id=1, source_target_pairs={{0,1},{1,2},{2,3},{3,4},{4,5},{5,6},{6,7},{7,8},{8,9},{9,10},{10,1... | collective-permute-start | bytes 749576 | tf_op jit(solution)/shard_map/ppermute | solution.py:40
  3.9 0.0 copy-start.11
  3.9 0.0 copy-start.5
  3.9 1.3 %collective-permute-start.1 = (f32[488,128]{1,0:T(8,128)}, f32[488,128]{1,0:T(8,128)S(1)}, u32[]{:S(2)}, u32[]{:S(2)}) collective-permute-start(f32[488,128]{1,0:T(8,128)} %get-tuple-element.29), channel_id=1, source_target_pairs={{1,0},{2,1},{3,2},{4,3},{5,4},{6,5},{7,6},{8,7},{9,8},{10,9},{11,1... | collective-permute-start | bytes 749576 | tf_op jit(solution)/shard_map/ppermute | solution.py:40
  5.2 5.8 %prepare.1 = (f32[12,26,128]{2,1,0:T(8,128)}, f32[3,12,48,128]{3,2,1,0:T(8,128)}, f32[12,2,48,128]{3,2,1,0:T(8,128)}, f32[12,2,48,128]{3,2,1,0:T(8,128)}, f32[3,...) custom-call(f32[12,36,47,64]{3,2,1,0:T(8,128)} %conc.1, f32[12,36,47,64]{3,2,1,0:T(8,128)} %conc.1, f32[12,36,64]{2,1,0:T(8,128)} %flux.1, ...), custom_call_target="tpu_custom_call" | custom-call | tf_op jit(solution)/shard_map/prepare/pallas_call | solution.py:152
  11.0 0.9 copy-done.3
  11.9 0.9 copy-done.4
  12.8 2.1 %collective-permute-start.2 = (f32[3,10,8,128]{3,2,1,0:T(8,128)S(1)}, f32[3,10,8,128]{3,2,1,0:T(8,128)S(1)}, u32[]{:S(2)}, u32[]{:S(2)}) collective-permute-start(f32[3,10,8,128]{3,2,1,0:T(8,128)S(1)} %get-tuple-element.36), channel_id=1, source_target_pairs={{0,16},{16,32},{32,48},{48,64},{64,80},{80,96},{96,112},{112,0},{1... | collective-permute-start | bytes 368648 | tf_op jit(solution)/shard_map/ppermute | solution.py:40
  14.9 3.6 %collective-permute-start.3 = (f32[3,10,8,128]{3,2,1,0:T(8,128)S(1)}, f32[3,10,8,128]{3,2,1,0:T(8,128)S(1)}, u32[]{:S(2)}, u32[]{:S(2)}) collective-permute-start(f32[3,10,8,128]{3,2,1,0:T(8,128)S(1)} %get-tuple-element.37), channel_id=1, source_target_pairs={{0,112},{16,0},{32,16},{48,32},{64,48},{80,64},{96,80},{112,96},{1... | collective-permute-start | bytes 368648 | tf_op jit(solution)/shard_map/ppermute | solution.py:40
  18.5 2.8 %collective-permute-done.2.from_west = f32[3,10,8,128]{3,2,1,0:T(8,128)S(1)} collective-permute-done((f32[3,10,8,128]{3,2,1,0:T(8,128)S(1)}, f32[3,10,8,128]{3,2,1,0:T(8,128)S(1)}, u32[]{:S(2)}, u32[]{:S(2)}) %collective-permute-start.2) | collective-permute-done | bytes 122912 | tf_op jit(solution)/shard_map/ppermute | solution.py:40
  21.3 0.7 collective-permute-done.3.from_east
  22.0 1.8 %collective-permute-start.4 = (f32[12,2,48,128]{3,2,1,0:T(8,128)}, f32[12,2,48,128]{3,2,1,0:T(8,128)S(1)}, u32[]{:S(2)}, u32[]{:S(2)}) collective-permute-start(f32[12,2,48,128]{3,2,1,0:T(8,128)} %get-tuple-element.38), channel_id=1, source_target_pairs={{0,16},{16,32},{32,48},{48,64},{64,80},{80,96},{96,112},{112,0},{1... | collective-permute-start | bytes 1769480 | tf_op jit(solution)/shard_map/ppermute | solution.py:40
  23.8 2.3 %collective-permute-start.5 = (f32[12,2,48,128]{3,2,1,0:T(8,128)}, f32[12,2,48,128]{3,2,1,0:T(8,128)S(1)}, u32[]{:S(2)}, u32[]{:S(2)}) collective-permute-start(f32[12,2,48,128]{3,2,1,0:T(8,128)} %get-tuple-element.39), channel_id=1, source_target_pairs={{0,112},{16,0},{32,16},{48,32},{64,48},{80,64},{96,80},{112,96},{1... | collective-permute-start | bytes 1769480 | tf_op jit(solution)/shard_map/ppermute | solution.py:40
  26.8 0.8 margins.1
  27.6 0.9 copy-done
  28.5 0.9 copy-done.1
  29.4 0.6 copy-done.6
  30.0 31.4 %transport.1 = (f32[20,18,48,128]{3,2,1,0:T(8,128)}, bf16[3,960,128]{2,1,0:T(8,128)(2,1)}) custom-call(f32[12,36,47,64]{3,2,1,0:T(8,128)} %conc.1, f32[12,26,128]{2,1,0:T(8,128)} %get-tuple-element.40.flux, f32[3,12,48,128]{3,2,1,0:T(8,128)} %get-tuple-element.41.own, f32[3,8,48,128]{3,2,1,0:T(8,128)} %copy-done.1, f32[3,10,8,128]{3,2,1,0:T(8,128)} %copy-done.9, ...), custom_call_target="tpu_custom_call" | custom-call | tf_op jit(solution)/shard_map/transport/pallas_call | solution.py:416
  61.4 0.8 copy-done.7
  62.2 0.2 copy-done.8
  62.4 13.5 %strips.1 = (f32[512,128]{1,0:T(8,128)}, f32[512,128]{1,0:T(8,128)}, f32[512,128]{1,0:T(8,128)}) custom-call(s32[24,128]{1,0:T(8,128)} %copy-done.6, f32[3,512,128]{2,1,0:T(8,128)} %copy-done, f32[12,2,48,128]{3,2,1,0:T(8,128)} %copy-done.7, f32[12,2,48,128]{3,2,1,0:T(8,128)} %copy-done.8, bf16[3,960,128]{2,1,0:T(8,128)(2,1)} %get-tuple-element.45.split, ...), custom_call_target="tpu_custom_call" | custom-call | tf_op jit(solution)/shard_map/strips/pallas_call | solution.py:563
  75.9 3.5 %collective-permute-start.6 = (f32[512,128]{1,0:T(8,128)}, f32[512,128]{1,0:T(8,128)S(1)}, u32[]{:S(2)}, u32[]{:S(2)}) collective-permute-start(f32[512,128]{1,0:T(8,128)} %get-tuple-element.48), channel_id=1, source_target_pairs={{0,1},{1,2},{2,3},{3,4},{4,5},{5,6},{6,7},{7,8},{8,9},{9,10},{10,1... | collective-permute-start | bytes 786440 | tf_op jit(solution)/shard_map/ppermute | solution.py:40
  79.5 1.3 %collective-permute-start.7 = (f32[512,128]{1,0:T(8,128)}, f32[512,128]{1,0:T(8,128)S(1)}, u32[]{:S(2)}, u32[]{:S(2)}) collective-permute-start(f32[512,128]{1,0:T(8,128)} %get-tuple-element.49), channel_id=1, source_target_pairs={{1,0},{2,1},{3,2},{4,3},{5,4},{6,5},{7,6},{8,7},{9,8},{10,9},{11,1... | collective-permute-start | bytes 786440 | tf_op jit(solution)/shard_map/ppermute | solution.py:40
  80.8 0.1 broadcast_in_dim.18
  80.9 0.1 broadcast_in_dim.9
  81.0 0.1 pad_maximum_fusion.weight
  81.2 4.7 %collective-permute-done.7.from_north = f32[512,128]{1,0:T(8,128)S(1)} collective-permute-done((f32[512,128]{1,0:T(8,128)}, f32[512,128]{1,0:T(8,128)S(1)}, u32[]{:S(2)}, u32[]{:S(2)}) %collective-permute-start.7) | collective-permute-done | bytes 262176 | tf_op jit(solution)/shard_map/ppermute | solution.py:40
  85.9 0.9 copy-done.2
  86.8 0.6 gram.1
  87.4 4.8 %collective-permute-start.8 = (f32[32,128]{1,0:T(8,128)S(1)}, f32[32,128]{1,0:T(8,128)S(1)}, u32[]{:S(2)}, u32[]{:S(2)}) collective-permute-start(f32[32,128]{1,0:T(8,128)S(1)} %get-tuple-element.50), channel_id=1, source_target_pairs={{0,1},{1,0},{2,3},{3,2},{4,5},{5,4},{6,7},{7,6},{8,9},{9,8},{10,11... | collective-permute-start | bytes 49160 | tf_op jit(solution)/shard_map/ppermute | solution.py:48
  92.2 0.8 collective-permute-done.8
  93.0 11.1 %collective-permute-start.11 = (f32[32,128]{1,0:T(8,128)S(1)}, f32[32,128]{1,0:T(8,128)S(1)}, u32[]{:S(2)}, u32[]{:S(2)}) collective-permute-start(f32[32,128]{1,0:T(8,128)S(1)} %add.30), channel_id=1, source_target_pairs={{0,6},{1,7},{2,4},{3,5},{4,2},{5,3},{6,0},{7,1},{8,14},{9,15},{10,... | collective-permute-start | bytes 49160 | tf_op jit(solution)/shard_map/ppermute | solution.py:48
  104.1 0.9 collective-permute-start.9
  105.0 0.8 collective-permute-done.11
  105.8 3.5 %collective-permute-done.10 = f32[32,128]{1,0:T(8,128)S(1)} collective-permute-done((f32[32,128]{1,0:T(8,128)S(1)}, f32[32,128]{1,0:T(8,128)S(1)}, u32[]{:S(2)}, u32[]{:S(2)}) %collective-permute-start.10) | collective-permute-done | bytes 16416 | tf_op jit(solution)/shard_map/ppermute | solution.py:48
  109.3 1.1 collective-permute-start.14
  110.4 2.3 %collective-permute-start.13 = (f32[32,128]{1,0:T(8,128)S(1)}, f32[32,128]{1,0:T(8,128)S(1)}, u32[]{:S(2)}, u32[]{:S(2)}) collective-permute-start(f32[32,128]{1,0:T(8,128)S(1)} %add_add_fusion.2), channel_id=1, source_target_pairs={{0,64},{1,65},{2,66},{3,67},{4,68},{5,69},{6,70},{7,71},{8,72},{9,... | collective-permute-start | bytes 49160 | tf_op jit(solution)/shard_map/ppermute | solution.py:48
  112.7 0.8 collective-permute-start.12
  113.5 0.9 collective-permute-done.14
  114.4 1.3 %collective-permute-done.13 = f32[32,128]{1,0:T(8,128)S(1)} collective-permute-done((f32[32,128]{1,0:T(8,128)S(1)}, f32[32,128]{1,0:T(8,128)S(1)}, u32[]{:S(2)}, u32[]{:S(2)}) %collective-permute-start.13) | collective-permute-done | bytes 16416 | tf_op jit(solution)/shard_map/ppermute | solution.py:48
  115.7 0.8 collective-permute-done.12
  116.5 2.3 %collective-permute-start.16 = (f32[32,128]{1,0:T(8,128)S(1)}, f32[32,128]{1,0:T(8,128)S(1)}, u32[]{:S(2)}, u32[]{:S(2)}) collective-permute-start(f32[32,128]{1,0:T(8,128)S(1)} %add_add_fusion.1), channel_id=1, source_target_pairs={{0,8},{1,9},{2,10},{3,11},{4,12},{5,13},{6,14},{7,15},{8,0},{9,1},... | collective-permute-start | bytes 49160 | tf_op jit(solution)/shard_map/ppermute | solution.py:48
  118.8 1.8 %collective-permute-start.15 = (f32[32,128]{1,0:T(8,128)S(1)}, f32[32,128]{1,0:T(8,128)S(1)}, u32[]{:S(2)}, u32[]{:S(2)}) collective-permute-start(f32[32,128]{1,0:T(8,128)S(1)} %add_add_fusion.1), channel_id=1, source_target_pairs={{0,16},{1,17},{2,18},{3,19},{4,20},{5,21},{6,22},{7,23},{8,24},{9,... | collective-permute-start | bytes 49160 | tf_op jit(solution)/shard_map/ppermute | solution.py:48
  120.6 0.9 collective-permute-done.17
  121.4 0.4 collective-permute-done.16
  121.8 0.7 collective-permute-done.15
  122.5 4.0 %factor.1 = (f32[64,1024]{1,0:T(8,128)}, f32[64,64]{1,0:T(8,128)}) custom-call(f32[32,128]{1,0:T(8,128)S(1)} %add_add_fusion.refs_0_, f32[512,128]{1,0:T(8,128)S(1)} %get-tuple-element.51.refs_1_), custom_call_target="tpu_custom_call" | custom-call | tf_op jit(solution)/shard_map/factor/pallas_call | solution.py:670
  (29 shorter events, 0.1 us)
Async XLA Ops:
  2.6 8.4 %collective-permute-start = (f32[488,128]{1,0:T(8,128)}, f32[488,128]{1,0:T(8,128)S(1)}, u32[]{:S(2)}, u32[]{:S(2)}) collective-permute-start(f32[488,128]{1,0:T(8,128)} %get-tuple-element.28), channel_id=1, source_target_pairs={{0,1},{1,2},{2,3},{3,4},{4,5},{5,6},{6,7},{7,8},{8,9},{9,10},{10,1... | collective-permute-start | bytes 749576 | tf_op jit(solution)/shard_map/ppermute | solution.py:40
  3.9 22.8 %copy-start.11 = (f32[1024]{0:T(1024)S(1)}, f32[1024]{0:T(1024)}, u32[]{:S(2)}) copy-start(f32[1024]{0:T(1024)} %param.14) | copy-start | bytes 12292
  3.9 22.8 %copy-start.5 = (s32[1024]{0:T(1024)S(1)}, s32[1024]{0:T(1024)}, u32[]{:S(2)}) copy-start(s32[1024]{0:T(1024)} %param.13) | copy-start | bytes 12292
  3.9 7.1 %collective-permute-start.1 = (f32[488,128]{1,0:T(8,128)}, f32[488,128]{1,0:T(8,128)S(1)}, u32[]{:S(2)}, u32[]{:S(2)}) collective-permute-start(f32[488,128]{1,0:T(8,128)} %get-tuple-element.29), channel_id=1, source_target_pairs={{1,0},{2,1},{3,2},{4,3},{5,4},{6,5},{7,6},{8,7},{9,8},{10,9},{11,1... | collective-permute-start | bytes 749576 | tf_op jit(solution)/shard_map/ppermute | solution.py:40
  11.0 0.9 copy-start.3
  11.9 0.9 copy-start.4
  12.8 8.4 %collective-permute-start.2 = (f32[3,10,8,128]{3,2,1,0:T(8,128)S(1)}, f32[3,10,8,128]{3,2,1,0:T(8,128)S(1)}, u32[]{:S(2)}, u32[]{:S(2)}) collective-permute-start(f32[3,10,8,128]{3,2,1,0:T(8,128)S(1)} %get-tuple-element.36), channel_id=1, source_target_pairs={{0,16},{16,32},{32,48},{48,64},{64,80},{80,96},{96,112},{112,0},{1... | collective-permute-start | bytes 368648 | tf_op jit(solution)/shard_map/ppermute | solution.py:40
  14.9 7.0 %collective-permute-start.3 = (f32[3,10,8,128]{3,2,1,0:T(8,128)S(1)}, f32[3,10,8,128]{3,2,1,0:T(8,128)S(1)}, u32[]{:S(2)}, u32[]{:S(2)}) collective-permute-start(f32[3,10,8,128]{3,2,1,0:T(8,128)S(1)} %get-tuple-element.37), channel_id=1, source_target_pairs={{0,112},{16,0},{32,16},{48,32},{64,48},{80,64},{96,80},{112,96},{1... | collective-permute-start | bytes 368648 | tf_op jit(solution)/shard_map/ppermute | solution.py:40
  21.2 8.7 %copy-start.9 = (f32[3,10,8,128]{3,2,1,0:T(8,128)}, f32[3,10,8,128]{3,2,1,0:T(8,128)S(1)}, u32[]{:S(2)}) copy-start(f32[3,10,8,128]{3,2,1,0:T(8,128)S(1)} %collective-permute-done.2.from_west) | copy-start | bytes 368644
  22.0 8.0 %copy-start.10 = (f32[3,10,8,128]{3,2,1,0:T(8,128)}, f32[3,10,8,128]{3,2,1,0:T(8,128)S(1)}, u32[]{:S(2)}) copy-start(f32[3,10,8,128]{3,2,1,0:T(8,128)S(1)} %collective-permute-done.3.from_east) | copy-start | bytes 368644
  22.0 39.4 %collective-permute-start.4 = (f32[12,2,48,128]{3,2,1,0:T(8,128)}, f32[12,2,48,128]{3,2,1,0:T(8,128)S(1)}, u32[]{:S(2)}, u32[]{:S(2)}) collective-permute-start(f32[12,2,48,128]{3,2,1,0:T(8,128)} %get-tuple-element.38), channel_id=1, source_target_pairs={{0,16},{16,32},{32,48},{48,64},{64,80},{80,96},{96,112},{112,0},{1... | collective-permute-start | bytes 1769480 | tf_op jit(solution)/shard_map/ppermute | solution.py:40
  23.8 37.6 %collective-permute-start.5 = (f32[12,2,48,128]{3,2,1,0:T(8,128)}, f32[12,2,48,128]{3,2,1,0:T(8,128)S(1)}, u32[]{:S(2)}, u32[]{:S(2)}) collective-permute-start(f32[12,2,48,128]{3,2,1,0:T(8,128)} %get-tuple-element.39), channel_id=1, source_target_pairs={{0,112},{16,0},{32,16},{48,32},{64,48},{80,64},{96,80},{112,96},{1... | collective-permute-start | bytes 1769480 | tf_op jit(solution)/shard_map/ppermute | solution.py:40
  27.6 0.9 copy-start
  28.5 0.9 copy-start.1
  29.4 0.6 copy-start.6
  61.4 0.8 copy-start.7
  61.4 1.0 copy-start.8
  75.9 5.3 %collective-permute-start.6 = (f32[512,128]{1,0:T(8,128)}, f32[512,128]{1,0:T(8,128)S(1)}, u32[]{:S(2)}, u32[]{:S(2)}) collective-permute-start(f32[512,128]{1,0:T(8,128)} %get-tuple-element.48), channel_id=1, source_target_pairs={{0,1},{1,2},{2,3},{3,4},{4,5},{5,6},{6,7},{7,8},{8,9},{9,10},{10,1... | collective-permute-start | bytes 786440 | tf_op jit(solution)/shard_map/ppermute | solution.py:40
  79.5 6.4 %collective-permute-start.7 = (f32[512,128]{1,0:T(8,128)}, f32[512,128]{1,0:T(8,128)S(1)}, u32[]{:S(2)}, u32[]{:S(2)}) collective-permute-start(f32[512,128]{1,0:T(8,128)} %get-tuple-element.49), channel_id=1, source_target_pairs={{1,0},{2,1},{3,2},{4,3},{5,4},{6,5},{7,6},{8,7},{9,8},{10,9},{11,1... | collective-permute-start | bytes 786440 | tf_op jit(solution)/shard_map/ppermute | solution.py:40
  85.9 1.0 copy-start.2
  87.4 5.6 %collective-permute-start.8 = (f32[32,128]{1,0:T(8,128)S(1)}, f32[32,128]{1,0:T(8,128)S(1)}, u32[]{:S(2)}, u32[]{:S(2)}) collective-permute-start(f32[32,128]{1,0:T(8,128)S(1)} %get-tuple-element.50), channel_id=1, source_target_pairs={{0,1},{1,0},{2,3},{3,2},{4,5},{5,4},{6,7},{7,6},{8,9},{9,8},{10,11... | collective-permute-start | bytes 49160 | tf_op jit(solution)/shard_map/ppermute | solution.py:48
  93.0 12.8 %collective-permute-start.11 = (f32[32,128]{1,0:T(8,128)S(1)}, f32[32,128]{1,0:T(8,128)S(1)}, u32[]{:S(2)}, u32[]{:S(2)}) collective-permute-start(f32[32,128]{1,0:T(8,128)S(1)} %add.30), channel_id=1, source_target_pairs={{0,6},{1,7},{2,4},{3,5},{4,2},{5,3},{6,0},{7,1},{8,14},{9,15},{10,... | collective-permute-start | bytes 49160 | tf_op jit(solution)/shard_map/ppermute | solution.py:48
  104.1 5.2 %collective-permute-start.10 = (f32[32,128]{1,0:T(8,128)S(1)}, f32[32,128]{1,0:T(8,128)S(1)}, u32[]{:S(2)}, u32[]{:S(2)}) collective-permute-start(f32[32,128]{1,0:T(8,128)S(1)} %add.30), channel_id=1, source_target_pairs={{0,4},{1,5},{2,6},{3,7},{4,0},{5,1},{6,2},{7,3},{8,12},{9,13},{10,... | collective-permute-start | bytes 49160 | tf_op jit(solution)/shard_map/ppermute | solution.py:48
  104.1 5.2 %collective-permute-start.9 = (f32[32,128]{1,0:T(8,128)S(1)}, f32[32,128]{1,0:T(8,128)S(1)}, u32[]{:S(2)}, u32[]{:S(2)}) collective-permute-start(f32[32,128]{1,0:T(8,128)S(1)} %add.30), channel_id=1, source_target_pairs={{0,2},{1,3},{2,0},{3,1},{4,6},{5,7},{6,4},{7,5},{8,10},{9,11},{10,... | collective-permute-start | bytes 49160 | tf_op jit(solution)/shard_map/ppermute | solution.py:48
  109.3 5.0 %collective-permute-start.14 = (f32[32,128]{1,0:T(8,128)S(1)}, f32[32,128]{1,0:T(8,128)S(1)}, u32[]{:S(2)}, u32[]{:S(2)}) collective-permute-start(f32[32,128]{1,0:T(8,128)S(1)} %add_add_fusion.2), channel_id=1, source_target_pairs={{0,96},{1,97},{2,98},{3,99},{4,100},{5,101},{6,102},{7,103},{8,104... | collective-permute-start | bytes 49160 | tf_op jit(solution)/shard_map/ppermute | solution.py:48
  110.4 5.2 %collective-permute-start.13 = (f32[32,128]{1,0:T(8,128)S(1)}, f32[32,128]{1,0:T(8,128)S(1)}, u32[]{:S(2)}, u32[]{:S(2)}) collective-permute-start(f32[32,128]{1,0:T(8,128)S(1)} %add_add_fusion.2), channel_id=1, source_target_pairs={{0,64},{1,65},{2,66},{3,67},{4,68},{5,69},{6,70},{7,71},{8,72},{9,... | collective-permute-start | bytes 49160 | tf_op jit(solution)/shard_map/ppermute | solution.py:48
  112.7 3.7 %collective-permute-start.12 = (f32[32,128]{1,0:T(8,128)S(1)}, f32[32,128]{1,0:T(8,128)S(1)}, u32[]{:S(2)}, u32[]{:S(2)}) collective-permute-start(f32[32,128]{1,0:T(8,128)S(1)} %add_add_fusion.2), channel_id=1, source_target_pairs={{0,32},{1,33},{2,34},{3,35},{4,36},{5,37},{6,38},{7,39},{8,40},{9,... | collective-permute-start | bytes 49160 | tf_op jit(solution)/shard_map/ppermute | solution.py:48
  116.5 4.9 %collective-permute-start.17 = (f32[32,128]{1,0:T(8,128)S(1)}, f32[32,128]{1,0:T(8,128)S(1)}, u32[]{:S(2)}, u32[]{:S(2)}) collective-permute-start(f32[32,128]{1,0:T(8,128)S(1)} %add_add_fusion.1), channel_id=1, source_target_pairs={{0,24},{1,25},{2,26},{3,27},{4,28},{5,29},{6,30},{7,31},{8,16},{9,... | collective-permute-start | bytes 49160 | tf_op jit(solution)/shard_map/ppermute | solution.py:48
  116.5 5.3 %collective-permute-start.16 = (f32[32,128]{1,0:T(8,128)S(1)}, f32[32,128]{1,0:T(8,128)S(1)}, u32[]{:S(2)}, u32[]{:S(2)}) collective-permute-start(f32[32,128]{1,0:T(8,128)S(1)} %add_add_fusion.1), channel_id=1, source_target_pairs={{0,8},{1,9},{2,10},{3,11},{4,12},{5,13},{6,14},{7,15},{8,0},{9,1},... | collective-permute-start | bytes 49160 | tf_op jit(solution)/shard_map/ppermute | solution.py:48
  118.8 3.7 %collective-permute-start.15 = (f32[32,128]{1,0:T(8,128)S(1)}, f32[32,128]{1,0:T(8,128)S(1)}, u32[]{:S(2)}, u32[]{:S(2)}) collective-permute-start(f32[32,128]{1,0:T(8,128)S(1)} %add_add_fusion.1), channel_id=1, source_target_pairs={{0,16},{1,17},{2,18},{3,19},{4,20},{5,21},{6,22},{7,23},{8,24},{9,... | collective-permute-start | bytes 49160 | tf_op jit(solution)/shard_map/ppermute | solution.py:48

commit v3 on v2

v3 whole, which is shorter than its diff:
```python
import jax
import jax.numpy as jnp
from jax import lax
from jax.experimental import pallas as pl
from jax.experimental.pallas import tpu as pltpu
from jax.sharding import PartitionSpec as P

STEPS = 4
BANDS, COLS, LEVS, PROBES = 12, 36, 47, 64
HALO = STEPS
TALL = BANDS + 2 * HALO
WIDE = COLS + 2 * HALO
LEVP = 48
TILES = LEVP // 8
COLP = 40
RING = 6
BLOCK = 4
LAT_ROWS = 3 * (HALO // 2) * COLP
LON_BANDS = TALL // 2
HALF = COLS // 2
PAIRS = HALF + 2 * HALO
SLOTS = 1024
FIELD_ROWS = TALL * HALF * LEVP
ZERO_ROW = FIELD_ROWS
F32 = jnp.float32
HIGHEST = lax.Precision.HIGHEST
MIB = 1024 * 1024


def params(mib=12):
    return pltpu.CompilerParams(vmem_limit_bytes=mib * MIB)


def whole(space=pltpu.VMEM):
    return pl.BlockSpec(memory_space=space)


def swap(x, axis, apart, wrap=False):
    size = lax.axis_size(axis)
    partner = [((i + 1) ^ 1) - 1 if apart else i ^ 1 for i in range(size)]
    if wrap:
        partner = [j % size for j in partner]
    return lax.ppermute(x, axis, [(i, j) for i, j in enumerate(partner) if 0 <= j < size])


def all_sum(x):
    lats = lax.axis_size("lat")
    size = lats * lax.axis_size("lon")
    for bits in ((1,), (2, 4), (2 * lats, 4 * lats), (lats, 8)):
        masks = [bits[0]] if len(bits) == 1 else [bits[0], bits[1], bits[0] | bits[1]]
        terms = [lax.ppermute(x, ("lon", "lat"), [(i, i ^ m) for i in range(size)]) for m in masks]
        for term in terms:
            x = x + term
    return x


def north_far(odd):
    return odd[0] & 1


def near_west(odd):
    return odd[0] >> 1


def lat_at(which, band):
    return (which * (HALO // 2) + band % (HALO // 2)) * COLP, 64 * (band // (HALO // 2))


def lon_at(band):
    place = band % LON_BANDS
    return place // 2, HALO * (place % 2), 64 * (band // LON_BANDS)


def pack_lat_kernel(odd, u, v, mix, cells, to_far, to_near, to_west, to_east):
    far = north_far(odd) * (BANDS - HALO)
    near = BANDS - HALO - far
    for which, ref in enumerate((u, v, mix)):
        for band in range(HALO):
            row, lane = lat_at(which, band)
            to_far[row : row + COLS, lane : lane + LEVS] = ref[far + band]
            to_near[row : row + COLS, lane : lane + LEVS] = ref[near + band]
        for band in range(BANDS):
            tile, row, lane = lon_at(band + HALO)
            for dst, col in ((to_west, 0), (to_east, COLS - HALO)):
                dst[which, tile, row : row + HALO, lane : lane + LEVS] = ref[band, col : col + HALO]
    for dst in (to_far, to_near):
        dst[LAT_ROWS:] = cells[...].astype(F32)


def pack_lat(odd, u, v, mix, cells):
    lat = jax.ShapeDtypeStruct((LAT_ROWS + 8, 128), F32)
    lon = jax.ShapeDtypeStruct((3, LON_BANDS // 2, 8, 128), F32)
    return pl.pallas_call(
        pack_lat_kernel,
        in_specs=[whole(pltpu.SMEM)] + [whole()] * 4,
        out_specs=[whole()] * 4,
        out_shape=[lat, lat, lon, lon],
        compiler_params=params(62),
        name="pack_lat",
    )(odd, u, v, mix, cells.reshape(8, 128))


def pack_lon_kernel(odd, west, east, far, near, to_far, to_near, edge_west, edge_east):
    far_north, west_near = north_far(odd) == 1, near_west(odd) == 1
    for src, dst, col in ((west, edge_west, 0), (east, edge_east, COLS - HALO)):
        dst[...] = src[...]
        for which in range(3):
            for edge in range(HALO):
                row, lane = lat_at(which, edge)
                ours = (slice(row + col, row + col + HALO), slice(lane, lane + LEVS))
                one, two = far[ours], near[ours]
                for rows, band in (
                    (jnp.where(far_north, two, one), edge),
                    (jnp.where(far_north, one, two), HALO + BANDS + edge),
                ):
                    tile, at, first = lon_at(band)
                    dst[which, tile, at : at + HALO, first : first + LEVS] = rows
    one, two = edge_west[...], edge_east[...]
    to_near[...] = jnp.where(west_near, one, two)
    to_far[...] = jnp.where(west_near, two, one)


def pack_lon(odd, west, east, far, near):
    out = jax.ShapeDtypeStruct(west.shape, F32)
    return pl.pallas_call(
        pack_lon_kernel,
        in_specs=[whole(pltpu.SMEM)] + [whole()] * 4,
        out_specs=[whole()] * 2,
        out_shape=[out, out],
        scratch_shapes=[pltpu.VMEM(west.shape, F32)] * 2,
        compiler_params=params(),
        name="pack_lon",
    )(odd, west, east, far, near)


def turn(dst, at, rows, flat, last_level):
    flat[0:LEVS, HALO : HALO + COLS] = rows.T
    if last_level:
        flat[LEVS - 1 : LEVS] = jnp.zeros((1, 128), F32)
    for tile in range(TILES):
        dst[at + (slice(8 * tile, 8 * tile + 8),)] = flat[pl.ds(tile, 8, stride=TILES)]


def two_terms(x, lane):
    high = x.astype(jnp.bfloat16).astype(F32)
    return jnp.where(lane < 64, high, x - high)


def level_tile(ref, at, tile):
    if tile < TILES - 1:
        return ref[at + (pl.ds(tile, 8, stride=TILES),)]
    part = ref[at + (pl.ds(tile, 7, stride=TILES),)]
    return jnp.concatenate([part, jnp.zeros((1, PROBES), F32)], axis=0)


def edges_kernel(odd, far, near, flux, to_far, to_near):
    for dst, src, west in ((to_far, far, 1 - near_west(odd)), (to_near, near, near_west(odd))):
        first = (1 - west) * (COLS - HALO)

        def pack(band, carry):
            for k in range(2):
                for tile in range(TILES):
                    low, up = level_tile(src, (band, k), tile), level_tile(src, (band, k + 2), tile)
                    dst[band, k, 8 * tile : 8 * tile + 8] = jnp.concatenate([low, up], axis=1)
                at = first + k
                pair = [flux[band, pl.ds(at, 1)], flux[band, pl.ds(at + 2, 1)]]
                dst[band, k, LEVS:LEVP] = jnp.concatenate(pair, axis=1)
            return carry

        lax.fori_loop(0, BANDS, pack, 0)


def pack_edges(odd, conc, flux):
    out = jax.ShapeDtypeStruct((BANDS, 2, LEVP, 128), F32)
    last = COLS // HALO - 1
    shape = (BANDS, HALO, LEVS, PROBES)
    return pl.pallas_call(
        edges_kernel,
        grid_spec=pltpu.PrefetchScalarGridSpec(
            num_scalar_prefetch=1,
            grid=(1,),
            in_specs=[
                pl.BlockSpec(shape, lambda i, odd: (0, last * near_west(odd), 0, 0)),
                pl.BlockSpec(shape, lambda i, odd: (0, last * (1 - near_west(odd)), 0, 0)),
                whole(),
            ],
            out_specs=[whole()] * 2,
        ),
        out_shape=[out, out],
        compiler_params=params(62),
        name="pack_edges",
    )(odd, conc, conc, flux)


def row_code(cells, shift):
    rest = ((cells.astype(F32) + 0.5) * (1.0 / LEVS)).astype(jnp.int32)
    level = cells - rest * LEVS
    line = ((rest.astype(F32) + 0.5) * (1.0 / COLS)).astype(jnp.int32)
    col = rest - line * COLS
    group = ((level.astype(F32) + 0.5) * (1.0 / TILES)).astype(jnp.int32)
    band = line + HALO + shift
    held = (band >= 0) & (band < TALL)
    upper = (col >= HALF).astype(jnp.int32)
    row = (band * HALF + col - HALF * upper) * LEVP + (level - group * TILES) * 8 + group
    later = lax.broadcasted_iota(jnp.int32, cells.shape, 0) * 128 >= SLOTS // 2
    cross = (upper == 1) != later
    return jnp.where(held, row, ZERO_ROW), cross.astype(F32)


def prepare_kernel(odd, flux, u, v, mix, far, near, cells, gains, coef, codes, turned, *flats):
    high = HALF - HALO
    none = jnp.zeros((BANDS, HALO, PROBES), F32)
    gains[:, 0:HALO, 0:PROBES] = none
    gains[:, HALO:, 0:PROBES] = flux[:, 0 : HALF + HALO]
    gains[:, 0 : HALF + HALO, PROBES:] = flux[:, high:]
    gains[:, HALF + HALO :, PROBES:] = none
    north = north_far(odd) * 2 - 1
    places = (
        (cells[...], 0),
        (far[LAT_ROWS:].astype(jnp.int32), BANDS * north),
        (near[LAT_ROWS:].astype(jnp.int32), -BANDS * north),
    )
    lower = lax.broadcasted_iota(jnp.int32, (128, 128), 1) < PROBES
    for group, (at, shift) in enumerate(places):
        row, cross = row_code(at, shift)
        codes[8 * group : 8 * group + 8] = row
        column = jnp.concatenate([cross, jnp.zeros((120, 128), F32)], axis=0).T
        for k in range(4):
            low = jnp.broadcast_to(column[:, k : k + 1], (128, 128))
            up = jnp.broadcast_to(column[:, k + 4 : k + 5], (128, 128))
            turned[group, 128 * k : 128 * k + 128] = jnp.where(lower, low, up)
    for flat in flats:
        flat[...] = jnp.zeros((LEVP, 128), F32)
    far_at = north_far(odd) * (HALO + BANDS)
    near_at = HALO + BANDS - far_at
    for which, ref in enumerate((u, v, mix)):
        for band in range(BANDS):
            turn(coef, (which, band + HALO), ref[band], flats[band % 4], which == 2)
        for band in range(HALO):
            row, lane = lat_at(which, band)
            for k, (first, src) in enumerate(((far_at, far), (near_at, near))):
                rows = src[row : row + COLS, lane : lane + LEVS]
                turn(coef, (which, first + band), rows, flats[band % 2 * 2 + k], which == 2)
    lane = lax.broadcasted_iota(jnp.int32, (LEVP, 128), 1)

    def split(at, carry):
        for which in range(3):
            for k in range(4):
                x = coef[which, at * 4 + k]
                coef[which, at * 4 + k] = two_terms(x + pltpu.roll(x, 64, 1), lane)
        return carry

    lax.fori_loop(0, TALL // 4, split, 0)


def prepare(odd, flux, u, v, mix, far, near, cells):
    return pl.pallas_call(
        prepare_kernel,
        in_specs=[whole(pltpu.SMEM)] + [whole()] * 7,
        out_specs=[whole()] * 4,
        out_shape=[
            jax.ShapeDtypeStruct((BANDS, PAIRS, 128), F32),
            jax.ShapeDtypeStruct((3, TALL, LEVP, 128), F32),
            jax.ShapeDtypeStruct((24, 128), jnp.int32),
            jax.ShapeDtypeStruct((3, SLOTS // 2, 128), F32),
        ],
        scratch_shapes=[pltpu.VMEM((LEVP, 128), F32)] * 4,
        compiler_params=params(62),
        name="prepare",
    )(odd, flux, u, v, mix, far, near, cells.reshape(8, 128))


def join_coef(odd, split, coef, far, near, sides, flat):
    span = 5 * HALO
    lane = lax.broadcasted_iota(jnp.int32, (8, 128), 1)
    west_near = near_west(odd) == 1
    flat[...] = jnp.zeros((LEVP, 128), F32)
    for which in range(3):
        one, two = far[which].reshape(-1, 128), near[which].reshape(-1, 128)
        west = jnp.where(west_near, two, one).T
        east = jnp.where(west_near, one, two).T
        for group in range(4):
            levels = slice(64 * (group // 2), 64 * (group // 2) + LEVS)
            cols = slice(span * (group % 2), span * (group % 2) + span)
            for at, src in ((0, west), (HALO + COLS, east)):
                flat[0:LEVS, at : at + span] = src[levels, cols]
            if which == 2:
                flat[LEVS - 1 : LEVS] = jnp.zeros((1, 128), F32)
            for tile in range(TILES):
                x = flat[pl.ds(tile, 8, stride=TILES)]
                x = x + pltpu.roll(x, 64, 1)
                sides[which, group, 8 * tile : 8 * tile + 8] = two_terms(x, lane)
    column = lax.broadcasted_iota(jnp.int32, (LEVP, 128), 1) & 63
    margin = (column < HALO) | ((column >= HALO + COLS) & (column < WIDE))

    def join(group, carry):
        for k in range(5):
            band = group * 5 + k
            rows = pl.ds(pl.multiple_of(band * LEVP, LEVP), LEVP)
            for which in range(3):
                beside = sides[which, group]
                if k:
                    beside = pltpu.roll(beside, 128 - HALO * k, 1)
                x = jnp.where(margin, beside, coef[which, band])
                split[which, rows] = x.astype(jnp.bfloat16)
        return carry

    lax.fori_loop(0, 4, join, 0)


def selector(tile, low, high, high_sign=1.0):
    shape = (128, 256)
    row = lax.broadcasted_iota(jnp.int32, shape, 0) & 63
    col = lax.broadcasted_iota(jnp.int32, shape, 1)
    pair = 2 * tile + (col >> 7)
    upper = ((col >> 6) & 1) == 1
    weight = jnp.where(upper, high_sign, 1.0)
    return jnp.where(row == jnp.where(upper, high(pair), low(pair)), weight, 0.0).astype(jnp.bfloat16)


def spread(ref, split, chosen, tile, first=0, count=TALL):
    out = jnp.dot(
        split[first * LEVP : (first + count) * LEVP], chosen, preferred_element_type=F32
    )
    out = out.reshape(count, 1, LEVP, 256)
    ref[first : first + count, pl.ds(2 * tile, 1)] = out[..., :128]
    ref[first : first + count, pl.ds(2 * tile + 1, 1)] = out[..., 128:]


def face_flux(speed, behind, ahead):
    return speed * jnp.where(speed > 0.0, behind, ahead)


def mix_levels(dst, line, mixing, at, pair):
    here = [line[pair, 8 * t : 8 * t + 8] for t in range(TILES)]
    above = here[1:] + [pltpu.roll(here[0], 7, 0)]
    moved = [
        mixing[at, pair, 8 * t : 8 * t + 8] * (above[t] - here[t]) for t in range(TILES)
    ]
    below = [pltpu.roll(moved[-1], 1, 0)] + moved[:-1]
    for t in range(TILES):
        dst[at, pair, 8 * t : 8 * t + 8] = here[t] + (moved[t] - below[t])


def two_rows(band, pairs, c, u, v, m, fs, line0, line1, closed=False):
    first, north = pairs[0], jnp.minimum(band + 2, TALL - 1)
    here0, here1 = c[band, first], c[band + 1, first]
    west0 = face_flux(u[band, first], c[band, first - 1], here0)
    west1 = face_flux(u[band + 1, first], c[band + 1, first - 1], here1)
    for pair in pairs:
        middle = face_flux(v[band + 1, pair], here0, here1)
        top = face_flux(v[north, pair], here1, c[north, pair])
        net0, net1 = here0 + west0, here1 + west1
        if not (closed and pair == pairs[-1]):
            ahead0, ahead1 = c[band, pair + 1], c[band + 1, pair + 1]
            west0 = face_flux(u[band, pair + 1], here0, ahead0)
            west1 = face_flux(u[band + 1, pair + 1], here1, ahead1)
            net0, net1 = net0 - west0, net1 - west1
            here0, here1 = ahead0, ahead1
        line0[pair] = net0 + (fs[pair] - middle)
        line1[pair] = net1 + (middle - top)
        fs[pair] = top
    for pair in pairs:
        mix_levels(c, line0, m, band, pair)
        mix_levels(c, line1, m, band + 1, pair)


def transport_kernel(
    odd, conc, flux, coef, far, near, out, split,
    c, u, v, m, fs, line0, line1, sides, flat, stage, in_sem, out_sem,
):
    def fetch(band):
        slot = lax.rem(band, RING)
        return pltpu.make_async_copy(conc.at[band], stage.at[slot], in_sem.at[slot])

    for band in range(RING):
        fetch(band).start()
    join_coef(odd, split, coef, far, near, sides, flat)

    def expand(tile):
        chosen = selector(tile, lambda pair: pair, lambda pair: pair + HALF)
        half = TALL // 2
        for which, ref in enumerate((u, v, m)):
            for first in (0, half):
                yield lambda: spread(ref, split.at[which], chosen, tile, first, half)

    zero = jnp.zeros((8, PROBES), F32)

    def load(band, carry):
        slot = lax.rem(band, RING)
        fetch(band).wait()
        pieces = expand(band)
        for pair in range(PAIRS):
            low, high = pair - HALO, pair - HALO + HALF
            for t in range(TILES):
                left = level_tile(stage, (slot, low), t) if low >= 0 else zero
                right = level_tile(stage, (slot, high), t) if high < COLS else zero
                both = jnp.concatenate([left, right], axis=1)
                c[band + HALO, pair, 8 * t : 8 * t + 8] = both
            if pair % 4 == 3:
                next(pieces)()

        @pl.when(band + RING < BANDS)
        def _():
            fetch(band + RING).start()

        return carry

    lax.fori_loop(0, BANDS, load, 0)
    for piece in expand(BANDS):
        piece()

    def clear(band, carry):
        c[band] = jnp.zeros((PAIRS, LEVP, 128), F32)
        c[band + HALO + BANDS] = jnp.zeros((PAIRS, LEVP, 128), F32)
        return carry

    lax.fori_loop(0, HALO, clear, 0)

    def save(band):
        return pltpu.make_async_copy(c.at[band, pl.ds(HALO, HALF)], out.at[band], out_sem.at[band])

    for step in range(1, STEPS + 1):
        first, last = step, PAIRS - step
        count = last - first

        def gain(band, carry):
            for pair in range(PAIRS):
                c[band + HALO, pair, 0:1] = c[band + HALO, pair, 0:1] + flux[band, pair : pair + 1]
            return carry

        lax.fori_loop(0, BANDS, gain, 0)
        fs[first:last] = jnp.zeros((count, LEVP, 128), F32)

        def rows(at, carry):
            band = HALO - step + 2 * at
            two_rows(band, range(first, last), c, u, v, m, fs, line0, line1)
            if step == STEPS:
                save(band).start()
                save(band + 1).start()
            return carry

        lax.fori_loop(0, (BANDS + 2 * step) // 2, rows, 0)

    def drain(band, carry):
        save(band).wait()
        return carry

    lax.fori_loop(0, TALL, drain, 0)


def transport(odd, conc, flux, coef, far, near):
    field = pltpu.VMEM((TALL, PAIRS, LEVP, 128), F32)
    line = pltpu.VMEM((PAIRS, LEVP, 128), F32)
    return pl.pallas_call(
        transport_kernel,
        in_specs=[whole(pltpu.SMEM), whole(pl.ANY)] + [whole()] * 4,
        out_specs=[whole(pl.ANY), whole()],
        out_shape=[
            jax.ShapeDtypeStruct((TALL, HALF, LEVP, 128), F32),
            jax.ShapeDtypeStruct((3, TALL * LEVP, 128), jnp.bfloat16),
        ],
        scratch_shapes=[
            field,
            field,
            field,
            field,
            line,
            line,
            line,
            pltpu.VMEM((3, 4, LEVP, 128), F32),
            pltpu.VMEM((LEVP, 128), F32),
            pltpu.VMEM((RING, COLS, LEVS, PROBES), F32),
            pltpu.SemaphoreType.DMA((RING,)),
            pltpu.SemaphoreType.DMA((TALL,)),
        ],
        compiler_params=params(62),
        name="transport",
    )(odd, conc, flux, coef, far, near)


def strips_kernel(
    odd, codes, turned, edge_far, edge_near, split, field, own, far, near,
    c, u, v, m, fs, line0, line1, gain, full, got0, got1, got2, sem,
):
    fetch = pltpu.make_async_copy(field, full.at[pl.ds(0, FIELD_ROWS)], sem)
    fetch.start()

    def expand(tile, carry):
        faces = selector(tile, lambda k: k, lambda k: WIDE - k, -1.0)
        cells = selector(tile, lambda k: k, lambda k: WIDE - 1 - k)
        for which, ref in enumerate((u, v, m)):
            spread(ref, split.at[which], cells if which else faces, tile)
        return carry

    lax.fori_loop(0, HALO, expand, 0)

    def clear(band, carry):
        c[band] = jnp.zeros((2 * HALO, LEVP, 128), F32)
        return carry

    lax.fori_loop(0, TALL, clear, 0)
    lower = lax.broadcasted_iota(jnp.int32, (LEVP, 128), 1) < PROBES
    inside = lax.broadcasted_iota(jnp.int32, (LEVP, 128), 0) < LEVS

    west_near = near_west(odd) == 1

    def place(band, carry):
        for k in range(2):
            left = jnp.where(west_near, edge_near[band, k], edge_far[band, k])
            right = jnp.where(west_near, edge_far[band, 1 - k], edge_near[band, 1 - k])
            outer = jnp.where(lower, left, right)
            inner = pltpu.roll(jnp.where(lower, right, left), PROBES, 1)
            for at, value in ((k, outer), (k + 2, inner)):
                c[band + HALO, at] = jnp.where(inside, value, 0.0)
                gain[band, at, 0:1] = value[LEVS:LEVP]
        return carry

    lax.fori_loop(0, BANDS, place, 0)

    full[ZERO_ROW : ZERO_ROW + 8] = jnp.zeros((8, 128), F32)

    for step in range(1, STEPS + 1):
        region = range(step, step + HALO)

        def add(band, carry):
            for k in range(step - 1, HALO):
                c[band + HALO, k, 0:1] = c[band + HALO, k, 0:1] + gain[band, k, 0:1]
            return carry

        lax.fori_loop(0, BANDS, add, 0)
        for k in region:
            fs[k] = jnp.zeros((LEVP, 128), F32)

        def rows(at, carry):
            two_rows(HALO - step + 2 * at, region, c, u, v, m, fs, line0, line1, closed=True)
            return carry

        lax.fori_loop(0, (BANDS + 2 * step) // 2, rows, 0)

    fetch.wait()

    def merge(band, carry):
        base = band * (HALF * LEVP)
        spots, sums = [], []
        for k in range(HALO):
            share = c[band, HALO + k]
            for pair, keep in ((k, lower), (HALF - 1 - k, ~lower)):
                rows = pl.ds(pl.multiple_of(base + pair * LEVP, LEVP), LEVP)
                spots.append(rows)
                sums.append(full[rows] + jnp.where(keep, share, 0.0))
        for rows, value in zip(spots, sums):
            full[rows] = value
        return carry

    lax.fori_loop(0, TALL, merge, 0)

    left_lanes = lax.broadcasted_iota(jnp.int32, (8, 128), 1) < PROBES
    for group, (out, buffer) in enumerate(((own, got0), (far, got1), (near, got2))):

        def pick(at, carry):
            rows = buffer.at[pl.ds(pl.multiple_of(at * 128, 128), 128)]
            for k in range(128):
                rows[k : k + 1] = full[pl.ds(codes[group * 8 + at, k], 1)]
            return carry

        lax.fori_loop(0, SLOTS // 128, pick, 0)

        def join(at, carry):
            for k in range(16):
                at8 = pl.multiple_of(at * 128 + k * 8, 8)
                one, two = buffer[pl.ds(at8, 8)], buffer[pl.ds(at8 + SLOTS // 2, 8)]
                straight = jnp.where(left_lanes, one, two)
                crossed = pltpu.roll(jnp.where(left_lanes, two, one), PROBES, 1)
                out[pl.ds(at8, 8)] = jnp.where(turned[group, pl.ds(at8, 8)] > 0.5, crossed, straight)
            return carry

        lax.fori_loop(0, SLOTS // 256, join, 0)


def strips(odd, codes, turned, far, near, split, field):
    strip = pltpu.VMEM((TALL, 2 * HALO, LEVP, 128), F32)
    line = pltpu.VMEM((2 * HALO, LEVP, 128), F32)
    buffer = pltpu.VMEM((SLOTS, 128), F32)
    return pl.pallas_call(
        strips_kernel,
        in_specs=[whole(pltpu.SMEM), whole(pltpu.SMEM), whole(), whole(), whole(), whole(), whole(pl.ANY)],
        out_specs=[whole()] * 3,
        out_shape=[jax.ShapeDtypeStruct((SLOTS // 2, 128), F32)] * 3,
        scratch_shapes=[
            strip,
            strip,
            strip,
            strip,
            line,
            line,
            line,
            pltpu.VMEM((BANDS, HALO, 8, 128), F32),
            pltpu.VMEM((FIELD_ROWS + 8, 128), F32),
            buffer,
            buffer,
            buffer,
            pltpu.SemaphoreType.DMA,
        ],
        compiler_params=params(56),
        name="strips",
    )(odd, codes, turned, far, near, split, field)


def gram_kernel(own, far, near, weight, images, gram):
    rows = (own[...] + far[...] + near[...]) * weight[...]
    images[...] = rows
    both = lax.dot_general(
        rows, rows, (((0,), (0,)), ((), ())), precision=HIGHEST, preferred_element_type=F32
    )
    total = both[:PROBES, :PROBES] + both[PROBES:, PROBES:]
    gram[:, 0:PROBES] = total[: PROBES // 2]
    gram[:, PROBES:] = total[PROBES // 2 :]


def gram_of(own, far, near, weight):
    return pl.pallas_call(
        gram_kernel,
        in_specs=[whole()] * 4,
        out_specs=[whole()] * 2,
        out_shape=[
            jax.ShapeDtypeStruct((SLOTS // 2, 128), F32),
            jax.ShapeDtypeStruct((PROBES // 2, 128), F32),
        ],
        compiler_params=params(),
        name="gram",
    )(own, far, near, weight)


def factor_kernel(root, gram, images, basis_t, factor, work, pivots):
    sublane = lax.broadcasted_iota(jnp.int32, (8, 128), 0)
    half = PROBES // 2
    work[0:half, 0:PROBES] = gram[:, 0:PROBES]
    work[half:, 0:PROBES] = gram[:, PROBES:]
    diagonal = (
        lax.broadcasted_iota(jnp.int32, (PROBES, PROBES), 0)
        == lax.broadcasted_iota(jnp.int32, (PROBES, PROBES), 1)
    )
    work[:, PROBES:] = diagonal.astype(F32)
    tiles = [work[8 * t : 8 * t + 8] for t in range(PROBES // 8)]
    for first in range(0, PROBES, BLOCK):
        top = first // 8
        live = range(top, PROBES // 8)
        column = {
            (j, t): jnp.broadcast_to(tiles[t][:, first + j : first + j + 1], (8, 128))
            for j in range(BLOCK)
            for t in live
        }
        for j in range(BLOCK):
            at = first + j
            pick = lambda tile, n: jnp.broadcast_to(tile[n % 8 : n % 8 + 1], (8, 128))
            inverse = 1.0 / pick(column[j, top], at)
            pivots[at : at + 1] = column[j, top][at % 8 : at % 8 + 1]
            pivot = pick(tiles[top], at) * inverse
            later = [pick(column[j, top], first + i) * inverse for i in range(j + 1, BLOCK)]
            for t in live:
                share = column[j, t]
                if t == top:
                    share = jnp.where(sublane > at % 8, share, 0.0)
                tiles[t] = tiles[t] - share * pivot
                for i in range(j + 1, BLOCK):
                    column[i, t] = column[i, t] - share * later[i - j - 1]
    for t in range(PROBES // 8):
        rows = slice(8 * t, 8 * t + 8)
        work[rows] = tiles[t] * (1.0 / jnp.sqrt(pivots[rows]))
    both = work[...]
    row = lax.broadcasted_iota(jnp.int32, (PROBES, PROBES), 0)
    col = lax.broadcasted_iota(jnp.int32, (PROBES, PROBES), 1)
    factor[...] = jnp.where(col >= row, both[:, :PROBES], 0.0) * (1.0 / root)
    inverse_t = jnp.where(col <= row, both[:, PROBES:], 0.0) * root
    zero = jnp.zeros((PROBES, PROBES), F32)
    twice = jnp.concatenate(
        [
            jnp.concatenate([inverse_t, zero], axis=1),
            jnp.concatenate([zero, inverse_t], axis=1),
        ],
        axis=0,
    )
    basis = lax.dot_general(
        twice, images[...], (((1,), (1,)), ((), ())), precision=HIGHEST, preferred_element_type=F32
    )
    basis_t[:, 0 : SLOTS // 2] = basis[:PROBES]
    basis_t[:, SLOTS // 2 :] = basis[PROBES:]


def factor_of(gram, images, root):
    return pl.pallas_call(
        lambda *refs: factor_kernel(root, *refs),
        in_specs=[whole()] * 2,
        out_specs=[whole()] * 2,
        out_shape=[
            jax.ShapeDtypeStruct((PROBES, SLOTS), F32),
            jax.ShapeDtypeStruct((PROBES, PROBES), F32),
        ],
        scratch_shapes=[pltpu.VMEM((PROBES, 128), F32)] * 2,
        compiler_params=params(),
        name="factor",
    )(gram, images)


def on_device(
    flux_probes, conc_start, u_courant, v_courant, vert_mix, obs_cell, obs_weight, obs_count
):
    odd = (lax.axis_index("lat") % 2 + 2 * (lax.axis_index("lon") % 2)).astype(jnp.int32).reshape(1)
    to_far, to_near, own_west, own_east = pack_lat(odd, u_courant, v_courant, vert_mix, obs_cell)
    from_far = swap(to_far, "lat", True)
    from_near = swap(to_near, "lat", False)
    edges = pack_edges(odd, conc_start, flux_probes)
    own_west, own_east, *edges = lax.optimization_barrier((own_west, own_east, *edges))
    lon_far, lon_near = pack_lon(odd, own_west, own_east, from_far, from_near)
    lon_far = swap(lon_far, "lon", True, wrap=True)
    lon_near = swap(lon_near, "lon", False)
    gains, coef, codes, turned = prepare(
        odd, flux_probes, u_courant, v_courant, vert_mix, from_far, from_near, obs_cell
    )
    edge_far, edge_near, coef, lon_far, lon_near = lax.optimization_barrier(
        (*edges, coef, lon_far, lon_near)
    )
    edge_far = swap(edge_far, "lon", True, wrap=True)
    edge_near = swap(edge_near, "lon", False)
    field, split = transport(odd, conc_start, gains, coef, lon_far, lon_near)
    rows, for_far, for_near = strips(
        odd, codes, turned, edge_far, edge_near, split, field.reshape(FIELD_ROWS, 128)
    )
    far_rows = swap(for_far, "lat", True)
    near_rows = swap(for_near, "lat", False)
    live = jnp.arange(SLOTS, dtype=jnp.int32) < obs_count[0]
    scale = jnp.where(live, obs_weight, 0.0)
    lanes = (SLOTS // 2, PROBES)
    weight = jnp.concatenate(
        [
            jnp.broadcast_to(scale[: SLOTS // 2, None], lanes),
            jnp.broadcast_to(scale[SLOTS // 2 :, None], lanes),
        ],
        axis=1,
    )
    images, gram = gram_of(rows, far_rows, near_rows, weight)
    gram = all_sum(gram)
    total_rows = SLOTS * lax.axis_size("lon") * lax.axis_size("lat")
    basis_t, factor = factor_of(gram, images, float(total_rows) ** 0.5)
    return basis_t.T, factor


def solution(mesh):
    in_specs = (
        P("lat", "lon", None),
        P("lat", "lon", None, None),
        P("lat", "lon", None),
        P("lat", "lon", None),
        P("lat", "lon", None),
        P(("lon", "lat")),
        P(("lon", "lat")),
        P(("lon", "lat")),
    )
    out_specs = (P(("lon", "lat"), None), P())
    return jax.shard_map(
        on_device, mesh=mesh, in_specs=in_specs, out_specs=out_specs, check_vma=False
    )
```

time: 127 us -> 111 us (0.87)
  starting transfers between devices: 42.2 us -> 34.1 us
  waiting for transfers between devices: 18.3 us -> 12.6 us
  local copies, waits for them, and re-layouts: 6.34 us -> 2.2 us
  Pallas kernels: 58 us -> 60.3 us
    ppermute x8, waiting for transfers between devices: 8.2 us -> 0.96 us  [swap(): lax.ppermute(x, axis, [(i, j) for i, j in enumerate(partner) if 0 <= j <...]
    ppermute x10, starting transfers between devices: 25 us -> 19.5 us  [all_sum(): lax.ppermute(x, ('lon', 'lat'), [(i, i ^ m) for i in range(size)])]
    unnamed x24 -> x20, local copies, waits for them, and re-layouts: 6.09 us -> 1.95 us
    ppermute x8, starting transfers between devices: 17.2 us -> 14.7 us  [swap(): lax.ppermute(x, axis, [(i, j) for i, j in enumerate(partner) if 0 <= j <...]
    pallas_call x6, Pallas kernels: 53.5 us -> 55.8 us  [the longest x1 29.7 us: transport(): pl.pallas_call(transport_kernel, in_specs=[whole(pltpu.SMEM), whole(pl.AN...]
    ppermute x10, waiting for transfers between devices: 10.1 us -> 11.6 us  [all_sum(): lax.ppermute(x, ('lon', 'lat'), [(i, i ^ m) for i in range(size)])]
  transfers between devices with their start and end apart: 18 -> 18, of which waited for: 12 -> 8; matrix products, arithmetic and copies ran while one was open for 0% -> 0% of each run, Pallas kernels for 30% -> 36%
where the time goes in v3:
time: 111 us
  Pallas kernels  60.3 us (54%)
  starting transfers between devices  34.1 us (31%)
  waiting for transfers between devices  12.6 us (11%)
  local copies, waits for them, and re-layouts  2.2 us (2%)
  between operations  1.53 us (1%)
    pallas_call x1, Pallas kernels, transport(): pl.pallas_call(transport_kernel, in_specs=[whole(pltpu.SMEM), whole(pl.AN...  29.7 us
    ppermute x10, starting transfers between devices, all_sum(): lax.ppermute(x, ('lon', 'lat'), [(i, i ^ m) for i in range(size)])  19.5 us
    ppermute x8, starting transfers between devices, swap(): lax.ppermute(x, axis, [(i, j) for i, j in enumerate(partner) if 0 <= j <...  14.7 us
    pallas_call x1, Pallas kernels, strips(): pl.pallas_call(strips_kernel, in_specs=[whole(pltpu.SMEM), whole(pltpu.SM...  13.5 us
    ppermute x10, waiting for transfers between devices, all_sum(): lax.ppermute(x, ('lon', 'lat'), [(i, i ^ m) for i in range(size)])  11.6 us
    pallas_call x1, Pallas kernels, prepare(): pl.pallas_call(prepare_kernel, in_specs=[whole(pltpu.SMEM)] + [whole()] *...  5.78 us
    pallas_call x1, Pallas kernels, pack_edges(): pl.pallas_call(edges_kernel, grid_spec=pltpu.PrefetchScalarGridSpec(num_s...  4.65 us
    pallas_call x1, Pallas kernels, factor_of(): pl.pallas_call(lambda *refs: factor_kernel(root, *refs), in_specs=[whole(...  3.96 us
  transfers between devices with their start and end apart: 18, of which 8 were waited for; matrix products, arithmetic and copies ran while one was open for 0% of the time, Pallas kernels for 36%

profile of v3, /device:TPU:0, one launch (start us, length us, event | category | flops | bytes accessed | tf_op | source)
XLA Modules:
  0.0 110.9 jit_solution(7971193205011843863)
XLA Ops:
  0.6 2.1 %pack_lat.1 = (f32[248,128]{1,0:T(8,128)}, f32[248,128]{1,0:T(8,128)}, f32[3,5,8,128]{3,2,1,0:T(8,128)}, f32[3,5,8,128]{3,2,1,0:T(8,128)}) custom-call(s32[1]{0:T(128)} %bitcast.odd, f32[12,36,47]{2,1,0:T(8,128)} %u.3, f32[12,36,47]{2,1,0:T(8,128)} %v.3, f32[12,36,47]{2,1,0:T(8,128)} %mix.3, s32[8,128]{1,0:T(8,128)} %bitcast.7), custom_call_target="tpu_custom_call" | custom-call | tf_op jit(solution)/shard_map/pack_lat/pallas_call | solution.py:93
  2.7 0.7 collective-permute-start
  3.4 0.0 copy-start.9
  3.4 3.1 %collective-permute-start.1 = (f32[248,128]{1,0:T(8,128)}, f32[248,128]{1,0:T(8,128)S(1)}, u32[]{:S(2)}, u32[]{:S(2)}) collective-permute-start(f32[248,128]{1,0:T(8,128)} %get-tuple-element.33), channel_id=1, source_target_pairs={{0,1},{1,0},{2,3},{3,2},{4,5},{5,4},{6,7},{7,6},{8,9},{9,8},{10,11... | collective-permute-start | bytes 380936 | tf_op jit(solution)/shard_map/ppermute | solution.py:43
  6.5 4.6 %pack_edges.1 = (f32[12,2,48,128]{3,2,1,0:T(8,128)}, f32[12,2,48,128]{3,2,1,0:T(8,128)}) custom-call(s32[1]{0:T(128)} %bitcast.odd, f32[12,36,47,64]{3,2,1,0:T(8,128)} %conc.1, f32[12,36,47,64]{3,2,1,0:T(8,128)} %conc.1, f32[12,36,64]{2,1,0:T(8,128)} %flux.3), custom_call_target="tpu_custom_call" | custom-call | tf_op jit(solution)/shard_map/pack_edges/pallas_call | solution.py:177
  11.2 0.0 collective-permute-done.far
  11.2 0.0 collective-permute-done.1.near
  11.2 0.1 pack_lon.1
  11.3 5.0 %collective-permute-start.2 = (f32[3,5,8,128]{3,2,1,0:T(8,128)S(1)}, f32[3,5,8,128]{3,2,1,0:T(8,128)S(1)}, u32[]{:S(2)}, u32[]{:S(2)}) collective-permute-start(f32[3,5,8,128]{3,2,1,0:T(8,128)S(1)} %get-tuple-element.45), channel_id=1, source_target_pairs={{0,112},{16,32},{32,16},{48,64},{64,48},{80,96},{96,80},{112,0},{1... | collective-permute-start | bytes 184328 | tf_op jit(solution)/shard_map/ppermute | solution.py:43
  16.4 0.0 collective-permute-start.3
  16.4 5.8 %prepare.1 = (f32[12,26,128]{2,1,0:T(8,128)}, f32[3,20,48,128]{3,2,1,0:T(8,128)}, s32[24,128]{1,0:T(8,128)}, f32[3,512,128]{2,1,0:T(8,128)}) custom-call(s32[1]{0:T(128)} %bitcast.odd, f32[12,36,64]{2,1,0:T(8,128)} %flux.3, f32[12,36,47]{2,1,0:T(8,128)} %u.3, f32[12,36,47]{2,1,0:T(8,128)} %v.3, f32[12,36,47]{2,1,0:T(8,128)} %mix.3, f32[248,128]{1,0:T(8,128)} %copy-done, ...), custom_call_target="tpu_custom_call" | custom-call | tf_op jit(solution)/shard_map/prepare/pallas_call | solution.py:257
  22.2 0.0 collective-permute-done.2.far
  22.2 0.0 collective-permute-done.3.near
  22.2 1.9 %collective-permute-start.4 = (f32[12,2,48,128]{3,2,1,0:T(8,128)}, f32[12,2,48,128]{3,2,1,0:T(8,128)S(1)}, u32[]{:S(2)}, u32[]{:S(2)}) collective-permute-start(f32[12,2,48,128]{3,2,1,0:T(8,128)} %get-tuple-element.47), channel_id=1, source_target_pairs={{0,112},{16,32},{32,16},{48,64},{64,48},{80,96},{96,80},{112,0},{1... | collective-permute-start | bytes 1769480 | tf_op jit(solution)/shard_map/ppermute | solution.py:43
  24.1 0.3 collective-permute-start.5
  25.1 29.7 %transport.1 = (f32[20,18,48,128]{3,2,1,0:T(8,128)}, bf16[3,960,128]{2,1,0:T(8,128)(2,1)}) custom-call(s32[1]{0:T(128)} %bitcast.odd, f32[12,36,47,64]{3,2,1,0:T(8,128)} %conc.1, f32[12,26,128]{2,1,0:T(8,128)} %get-tuple-element.49.flux, f32[3,20,48,128]{3,2,1,0:T(8,128)} %get-tuple-element.50.coef, f32[3,5,8,128]{3,2,1,0:T(8,128)} %copy-done.7, ...), custom_call_target="tpu_custom_call" | custom-call | tf_op jit(solution)/shard_map/transport/pallas_call | solution.py:455
  54.7 0.0 collective-permute-done.4.edge_far
  54.8 0.8 copy-done.5
  55.6 0.2 copy-done.6
  55.8 13.5 %strips.1 = (f32[512,128]{1,0:T(8,128)}, f32[512,128]{1,0:T(8,128)}, f32[512,128]{1,0:T(8,128)}) custom-call(s32[1]{0:T(128)} %bitcast.odd, s32[24,128]{1,0:T(8,128)} %get-tuple-element.34.codes, f32[3,512,128]{2,1,0:T(8,128)} %get-tuple-element.35.turned, f32[12,2,48,128]{3,2,1,0:T(8,128)} %copy-done.5, f32[12,2,48,128]{3,2,1,0:T(8,128)} %copy-done.6, ...), custom_call_target="tpu_custom_call" | custom-call | tf_op jit(solution)/shard_map/strips/pallas_call | solution.py:585
  69.3 0.7 collective-permute-start.6
  70.0 3.0 %collective-permute-start.7 = (f32[512,128]{1,0:T(8,128)}, f32[512,128]{1,0:T(8,128)S(1)}, u32[]{:S(2)}, u32[]{:S(2)}) collective-permute-start(f32[512,128]{1,0:T(8,128)} %get-tuple-element.57), channel_id=1, source_target_pairs={{0,1},{1,0},{2,3},{3,2},{4,5},{5,4},{6,7},{7,6},{8,9},{9,8},{10,11... | collective-permute-start | bytes 786440 | tf_op jit(solution)/shard_map/ppermute | solution.py:43
  73.0 0.1 broadcast_in_dim.18
  73.1 0.1 broadcast_in_dim.9
  73.2 0.1 pad_maximum_fusion.weight
  73.4 0.9 collective-permute-done.7.near
  74.3 0.9 copy-done.2
  75.3 0.6 gram.1
  75.8 2.8 %collective-permute-start.8 = (f32[32,128]{1,0:T(8,128)S(1)}, f32[32,128]{1,0:T(8,128)S(1)}, u32[]{:S(2)}, u32[]{:S(2)}) collective-permute-start(f32[32,128]{1,0:T(8,128)S(1)} %get-tuple-element.58), channel_id=1, source_target_pairs={{0,1},{1,0},{2,3},{3,2},{4,5},{5,4},{6,7},{7,6},{8,9},{9,8},{10,11... | collective-permute-start | bytes 49160 | tf_op jit(solution)/shard_map/ppermute | solution.py:51
  78.7 0.8 collective-permute-done.8
  79.5 7.3 %collective-permute-start.11 = (f32[32,128]{1,0:T(8,128)S(1)}, f32[32,128]{1,0:T(8,128)S(1)}, u32[]{:S(2)}, u32[]{:S(2)}) collective-permute-start(f32[32,128]{1,0:T(8,128)S(1)} %add.43), channel_id=1, source_target_pairs={{0,6},{1,7},{2,4},{3,5},{4,2},{5,3},{6,0},{7,1},{8,14},{9,15},{10,... | collective-permute-start | bytes 49160 | tf_op jit(solution)/shard_map/ppermute | solution.py:51
  86.9 0.9 collective-permute-start.9
  87.8 0.8 collective-permute-done.11
  88.6 3.5 %collective-permute-done.10 = f32[32,128]{1,0:T(8,128)S(1)} collective-permute-done((f32[32,128]{1,0:T(8,128)S(1)}, f32[32,128]{1,0:T(8,128)S(1)}, u32[]{:S(2)}, u32[]{:S(2)}) %collective-permute-start.10) | collective-permute-done | bytes 16416 | tf_op jit(solution)/shard_map/ppermute | solution.py:51
  92.1 0.0 collective-permute-done.9
  92.1 2.7 %collective-permute-start.14 = (f32[32,128]{1,0:T(8,128)S(1)}, f32[32,128]{1,0:T(8,128)S(1)}, u32[]{:S(2)}, u32[]{:S(2)}) collective-permute-start(f32[32,128]{1,0:T(8,128)S(1)} %add_add_fusion.2), channel_id=1, source_target_pairs={{0,96},{1,97},{2,98},{3,99},{4,100},{5,101},{6,102},{7,103},{8,104... | collective-permute-start | bytes 49160 | tf_op jit(solution)/shard_map/ppermute | solution.py:51
  94.8 0.8 collective-permute-start.13
  95.7 0.7 collective-permute-start.12
  96.3 0.9 collective-permute-done.14
  97.2 2.9 %collective-permute-done.13 = f32[32,128]{1,0:T(8,128)S(1)} collective-permute-done((f32[32,128]{1,0:T(8,128)S(1)}, f32[32,128]{1,0:T(8,128)S(1)}, u32[]{:S(2)}, u32[]{:S(2)}) %collective-permute-start.13) | collective-permute-done | bytes 16416 | tf_op jit(solution)/shard_map/ppermute | solution.py:51
  100.1 0.0 collective-permute-done.12
  100.1 1.6 %collective-permute-start.17 = (f32[32,128]{1,0:T(8,128)S(1)}, f32[32,128]{1,0:T(8,128)S(1)}, u32[]{:S(2)}, u32[]{:S(2)}) collective-permute-start(f32[32,128]{1,0:T(8,128)S(1)} %add_add_fusion.1), channel_id=1, source_target_pairs={{0,24},{1,25},{2,26},{3,27},{4,28},{5,29},{6,30},{7,31},{8,16},{9,... | collective-permute-start | bytes 49160 | tf_op jit(solution)/shard_map/ppermute | solution.py:51
  101.7 1.5 %collective-permute-start.16 = (f32[32,128]{1,0:T(8,128)S(1)}, f32[32,128]{1,0:T(8,128)S(1)}, u32[]{:S(2)}, u32[]{:S(2)}) collective-permute-start(f32[32,128]{1,0:T(8,128)S(1)} %add_add_fusion.1), channel_id=1, source_target_pairs={{0,8},{1,9},{2,10},{3,11},{4,12},{5,13},{6,14},{7,15},{8,0},{9,1},... | collective-permute-start | bytes 49160 | tf_op jit(solution)/shard_map/ppermute | solution.py:51
  103.2 1.0 collective-permute-start.15
  104.2 0.9 collective-permute-done.17
  105.1 1.8 %collective-permute-done.16 = f32[32,128]{1,0:T(8,128)S(1)} collective-permute-done((f32[32,128]{1,0:T(8,128)S(1)}, f32[32,128]{1,0:T(8,128)S(1)}, u32[]{:S(2)}, u32[]{:S(2)}) %collective-permute-start.16) | collective-permute-done | bytes 16416 | tf_op jit(solution)/shard_map/ppermute | solution.py:51
  106.9 0.0 collective-permute-done.15
  107.0 4.0 %factor.1 = (f32[64,1024]{1,0:T(8,128)}, f32[64,64]{1,0:T(8,128)}) custom-call(f32[32,128]{1,0:T(8,128)S(1)} %add_add_fusion.refs_0_, f32[512,128]{1,0:T(8,128)S(1)} %get-tuple-element.59.refs_1_), custom_call_target="tpu_custom_call" | custom-call | tf_op jit(solution)/shard_map/factor/pallas_call | solution.py:692
  (25 shorter events, 0.1 us)
Async XLA Ops:
  2.7 8.4 %collective-permute-start = (f32[248,128]{1,0:T(8,128)}, f32[248,128]{1,0:T(8,128)S(1)}, u32[]{:S(2)}, u32[]{:S(2)}) collective-permute-start(f32[248,128]{1,0:T(8,128)} %get-tuple-element.32), channel_id=1, source_target_pairs={{1,2},{2,1},{3,4},{4,3},{5,6},{6,5},{7,8},{8,7},{9,10},{10,9},{11,... | collective-permute-start | bytes 380936 | tf_op jit(solution)/shard_map/ppermute | solution.py:43
  3.4 7.8 %copy-start.3 = (f32[3,5,8,128]{3,2,1,0:T(8,128)S(1)}, f32[3,5,8,128]{3,2,1,0:T(8,128)}, u32[]{:S(2)}) copy-start(f32[3,5,8,128]{3,2,1,0:T(8,128)} %get-tuple-element.43.west) | copy-start | bytes 184324
  3.4 7.8 %copy-start.4 = (f32[3,5,8,128]{3,2,1,0:T(8,128)S(1)}, f32[3,5,8,128]{3,2,1,0:T(8,128)}, u32[]{:S(2)}) copy-start(f32[3,5,8,128]{3,2,1,0:T(8,128)} %get-tuple-element.44.east) | copy-start | bytes 184324
  3.4 21.6 %copy-start.9 = (f32[1024]{0:T(1024)S(1)}, f32[1024]{0:T(1024)}, u32[]{:S(2)}) copy-start(f32[1024]{0:T(1024)} %param.14) | copy-start | bytes 12292
  3.4 7.7 %collective-permute-start.1 = (f32[248,128]{1,0:T(8,128)}, f32[248,128]{1,0:T(8,128)S(1)}, u32[]{:S(2)}, u32[]{:S(2)}) collective-permute-start(f32[248,128]{1,0:T(8,128)} %get-tuple-element.33), channel_id=1, source_target_pairs={{0,1},{1,0},{2,3},{3,2},{4,5},{5,4},{6,7},{7,6},{8,9},{9,8},{10,11... | collective-permute-start | bytes 380936 | tf_op jit(solution)/shard_map/ppermute | solution.py:43
  11.2 5.2 %copy-start = (f32[248,128]{1,0:T(8,128)}, f32[248,128]{1,0:T(8,128)S(1)}, u32[]{:S(2)}) copy-start(f32[248,128]{1,0:T(8,128)S(1)} %collective-permute-done.far) | copy-start | bytes 380932
  11.2 5.2 %copy-start.1 = (f32[248,128]{1,0:T(8,128)}, f32[248,128]{1,0:T(8,128)S(1)}, u32[]{:S(2)}) copy-start(f32[248,128]{1,0:T(8,128)S(1)} %collective-permute-done.1.near) | copy-start | bytes 380932
  11.3 10.8 %collective-permute-start.2 = (f32[3,5,8,128]{3,2,1,0:T(8,128)S(1)}, f32[3,5,8,128]{3,2,1,0:T(8,128)S(1)}, u32[]{:S(2)}, u32[]{:S(2)}) collective-permute-start(f32[3,5,8,128]{3,2,1,0:T(8,128)S(1)} %get-tuple-element.45), channel_id=1, source_target_pairs={{0,112},{16,32},{32,16},{48,64},{64,48},{80,96},{96,80},{112,0},{1... | collective-permute-start | bytes 184328 | tf_op jit(solution)/shard_map/ppermute | solution.py:43
  16.4 5.8 %collective-permute-start.3 = (f32[3,5,8,128]{3,2,1,0:T(8,128)S(1)}, f32[3,5,8,128]{3,2,1,0:T(8,128)S(1)}, u32[]{:S(2)}, u32[]{:S(2)}) collective-permute-start(f32[3,5,8,128]{3,2,1,0:T(8,128)S(1)} %get-tuple-element.46), channel_id=1, source_target_pairs={{0,16},{16,0},{32,48},{48,32},{64,80},{80,64},{96,112},{112,96},{1... | collective-permute-start | bytes 184328 | tf_op jit(solution)/shard_map/ppermute | solution.py:43
  22.2 2.9 %copy-start.7 = (f32[3,5,8,128]{3,2,1,0:T(8,128)}, f32[3,5,8,128]{3,2,1,0:T(8,128)S(1)}, u32[]{:S(2)}) copy-start(f32[3,5,8,128]{3,2,1,0:T(8,128)S(1)} %collective-permute-done.2.far) | copy-start | bytes 184324
  22.2 2.9 %copy-start.8 = (f32[3,5,8,128]{3,2,1,0:T(8,128)}, f32[3,5,8,128]{3,2,1,0:T(8,128)S(1)}, u32[]{:S(2)}) copy-start(f32[3,5,8,128]{3,2,1,0:T(8,128)S(1)} %collective-permute-done.3.near) | copy-start | bytes 184324
  22.2 32.6 %collective-permute-start.4 = (f32[12,2,48,128]{3,2,1,0:T(8,128)}, f32[12,2,48,128]{3,2,1,0:T(8,128)S(1)}, u32[]{:S(2)}, u32[]{:S(2)}) collective-permute-start(f32[12,2,48,128]{3,2,1,0:T(8,128)} %get-tuple-element.47), channel_id=1, source_target_pairs={{0,112},{16,32},{32,16},{48,64},{64,48},{80,96},{96,80},{112,0},{1... | collective-permute-start | bytes 1769480 | tf_op jit(solution)/shard_map/ppermute | solution.py:43
  24.1 30.6 %collective-permute-start.5 = (f32[12,2,48,128]{3,2,1,0:T(8,128)}, f32[12,2,48,128]{3,2,1,0:T(8,128)S(1)}, u32[]{:S(2)}, u32[]{:S(2)}) collective-permute-start(f32[12,2,48,128]{3,2,1,0:T(8,128)} %get-tuple-element.48), channel_id=1, source_target_pairs={{0,16},{16,0},{32,48},{48,32},{64,80},{80,64},{96,112},{112,96},{1... | collective-permute-start | bytes 1769480 | tf_op jit(solution)/shard_map/ppermute | solution.py:43
  54.8 0.8 copy-start.5
  54.8 1.0 copy-start.6
  69.3 4.1 %collective-permute-start.6 = (f32[512,128]{1,0:T(8,128)}, f32[512,128]{1,0:T(8,128)S(1)}, u32[]{:S(2)}, u32[]{:S(2)}) collective-permute-start(f32[512,128]{1,0:T(8,128)} %get-tuple-element.56), channel_id=1, source_target_pairs={{1,2},{2,1},{3,4},{4,3},{5,6},{6,5},{7,8},{8,7},{9,10},{10,9},{11,... | collective-permute-start | bytes 786440 | tf_op jit(solution)/shard_map/ppermute | solution.py:43
  70.0 4.4 %collective-permute-start.7 = (f32[512,128]{1,0:T(8,128)}, f32[512,128]{1,0:T(8,128)S(1)}, u32[]{:S(2)}, u32[]{:S(2)}) collective-permute-start(f32[512,128]{1,0:T(8,128)} %get-tuple-element.57), channel_id=1, source_target_pairs={{0,1},{1,0},{2,3},{3,2},{4,5},{5,4},{6,7},{7,6},{8,9},{9,8},{10,11... | collective-permute-start | bytes 786440 | tf_op jit(solution)/shard_map/ppermute | solution.py:43
  74.3 0.9 copy-start.2
  75.8 3.7 %collective-permute-start.8 = (f32[32,128]{1,0:T(8,128)S(1)}, f32[32,128]{1,0:T(8,128)S(1)}, u32[]{:S(2)}, u32[]{:S(2)}) collective-permute-start(f32[32,128]{1,0:T(8,128)S(1)} %get-tuple-element.58), channel_id=1, source_target_pairs={{0,1},{1,0},{2,3},{3,2},{4,5},{5,4},{6,7},{7,6},{8,9},{9,8},{10,11... | collective-permute-start | bytes 49160 | tf_op jit(solution)/shard_map/ppermute | solution.py:51
  79.5 9.1 %collective-permute-start.11 = (f32[32,128]{1,0:T(8,128)S(1)}, f32[32,128]{1,0:T(8,128)S(1)}, u32[]{:S(2)}, u32[]{:S(2)}) collective-permute-start(f32[32,128]{1,0:T(8,128)S(1)} %add.43), channel_id=1, source_target_pairs={{0,6},{1,7},{2,4},{3,5},{4,2},{5,3},{6,0},{7,1},{8,14},{9,15},{10,... | collective-permute-start | bytes 49160 | tf_op jit(solution)/shard_map/ppermute | solution.py:51
  86.9 5.2 %collective-permute-start.10 = (f32[32,128]{1,0:T(8,128)S(1)}, f32[32,128]{1,0:T(8,128)S(1)}, u32[]{:S(2)}, u32[]{:S(2)}) collective-permute-start(f32[32,128]{1,0:T(8,128)S(1)} %add.43), channel_id=1, source_target_pairs={{0,4},{1,5},{2,6},{3,7},{4,0},{5,1},{6,2},{7,3},{8,12},{9,13},{10,... | collective-permute-start | bytes 49160 | tf_op jit(solution)/shard_map/ppermute | solution.py:51
  86.9 5.2 %collective-permute-start.9 = (f32[32,128]{1,0:T(8,128)S(1)}, f32[32,128]{1,0:T(8,128)S(1)}, u32[]{:S(2)}, u32[]{:S(2)}) collective-permute-start(f32[32,128]{1,0:T(8,128)S(1)} %add.43), channel_id=1, source_target_pairs={{0,2},{1,3},{2,0},{3,1},{4,6},{5,7},{6,4},{7,5},{8,10},{9,11},{10,... | collective-permute-start | bytes 49160 | tf_op jit(solution)/shard_map/ppermute | solution.py:51
  92.1 5.0 %collective-permute-start.14 = (f32[32,128]{1,0:T(8,128)S(1)}, f32[32,128]{1,0:T(8,128)S(1)}, u32[]{:S(2)}, u32[]{:S(2)}) collective-permute-start(f32[32,128]{1,0:T(8,128)S(1)} %add_add_fusion.2), channel_id=1, source_target_pairs={{0,96},{1,97},{2,98},{3,99},{4,100},{5,101},{6,102},{7,103},{8,104... | collective-permute-start | bytes 49160 | tf_op jit(solution)/shard_map/ppermute | solution.py:51
  94.8 5.2 %collective-permute-start.13 = (f32[32,128]{1,0:T(8,128)S(1)}, f32[32,128]{1,0:T(8,128)S(1)}, u32[]{:S(2)}, u32[]{:S(2)}) collective-permute-start(f32[32,128]{1,0:T(8,128)S(1)} %add_add_fusion.2), channel_id=1, source_target_pairs={{0,64},{1,65},{2,66},{3,67},{4,68},{5,69},{6,70},{7,71},{8,72},{9,... | collective-permute-start | bytes 49160 | tf_op jit(solution)/shard_map/ppermute | solution.py:51
  95.7 4.4 %collective-permute-start.12 = (f32[32,128]{1,0:T(8,128)S(1)}, f32[32,128]{1,0:T(8,128)S(1)}, u32[]{:S(2)}, u32[]{:S(2)}) collective-permute-start(f32[32,128]{1,0:T(8,128)S(1)} %add_add_fusion.2), channel_id=1, source_target_pairs={{0,32},{1,33},{2,34},{3,35},{4,36},{5,37},{6,38},{7,39},{8,40},{9,... | collective-permute-start | bytes 49160 | tf_op jit(solution)/shard_map/ppermute | solution.py:51
  100.1 5.0 %collective-permute-start.17 = (f32[32,128]{1,0:T(8,128)S(1)}, f32[32,128]{1,0:T(8,128)S(1)}, u32[]{:S(2)}, u32[]{:S(2)}) collective-permute-start(f32[32,128]{1,0:T(8,128)S(1)} %add_add_fusion.1), channel_id=1, source_target_pairs={{0,24},{1,25},{2,26},{3,27},{4,28},{5,29},{6,30},{7,31},{8,16},{9,... | collective-permute-start | bytes 49160 | tf_op jit(solution)/shard_map/ppermute | solution.py:51
  101.7 5.2 %collective-permute-start.16 = (f32[32,128]{1,0:T(8,128)S(1)}, f32[32,128]{1,0:T(8,128)S(1)}, u32[]{:S(2)}, u32[]{:S(2)}) collective-permute-start(f32[32,128]{1,0:T(8,128)S(1)} %add_add_fusion.1), channel_id=1, source_target_pairs={{0,8},{1,9},{2,10},{3,11},{4,12},{5,13},{6,14},{7,15},{8,0},{9,1},... | collective-permute-start | bytes 49160 | tf_op jit(solution)/shard_map/ppermute | solution.py:51
  103.2 3.7 %collective-permute-start.15 = (f32[32,128]{1,0:T(8,128)S(1)}, f32[32,128]{1,0:T(8,128)S(1)}, u32[]{:S(2)}, u32[]{:S(2)}) collective-permute-start(f32[32,128]{1,0:T(8,128)S(1)} %add_add_fusion.1), channel_id=1, source_target_pairs={{0,16},{1,17},{2,18},{3,19},{4,20},{5,21},{6,22},{7,23},{8,24},{9,... | collective-permute-start | bytes 49160 | tf_op jit(solution)/shard_map/ppermute | solution.py:51

commit v4 on v3

--- a/solution.py
+++ b/solution.py
@@ -14,7 +14,7 @@
 TILES = LEVP // 8
 COLP = 40
 RING = 6
-BLOCK = 4
+BLOCK = 8
 LAT_ROWS = 3 * (HALO // 2) * COLP
 LON_BANDS = TALL // 2
 HALF = COLS // 2
@@ -153,24 +153,49 @@
     return jnp.concatenate([part, jnp.zeros((1, PROBES), F32)], axis=0)
 
 
-def edges_kernel(odd, far, near, flux, to_far, to_near):
+def edges_kernel(odd, far, near, flux, u, v, mix, to_far, to_near, gains, coef, *flats):
     for dst, src, west in ((to_far, far, 1 - near_west(odd)), (to_near, near, near_west(odd))):
         first = (1 - west) * (COLS - HALO)
 
-        def pack(band, carry):
-            for k in range(2):
-                for tile in range(TILES):
-                    low, up = level_tile(src, (band, k), tile), level_tile(src, (band, k + 2), tile)
-                    dst[band, k, 8 * tile : 8 * tile + 8] = jnp.concatenate([low, up], axis=1)
-                at = first + k
-                pair = [flux[band, pl.ds(at, 1)], flux[band, pl.ds(at + 2, 1)]]
-                dst[band, k, LEVS:LEVP] = jnp.concatenate(pair, axis=1)
+        def pack(at, carry):
+            for band in (2 * at, 2 * at + 1):
+                for k in range(2):
+                    pair = jnp.concatenate([src[band, k], src[band, k + 2]], axis=1)
+                    dst[band, k, 0:LEVS] = pair
+                    col = first + k
+                    gain = [flux[band, pl.ds(col, 1)], flux[band, pl.ds(col + 2, 1)]]
+                    dst[band, k, LEVS:LEVP] = jnp.concatenate(gain, axis=1)
             return carry
 
-        lax.fori_loop(0, BANDS, pack, 0)
-
-
-def pack_edges(odd, conc, flux):
+        lax.fori_loop(0, BANDS // 2, pack, 0)
+    high = HALF - HALO
+    none = jnp.zeros((BANDS, HALO, PROBES), F32)
+    gains[:, 0:HALO, 0:PROBES] = none
+    gains[:, HALO:, 0:PROBES] = flux[:, 0 : HALF + HALO]
+    gains[:, 0 : HALF + HALO, PROBES:] = flux[:, high:]
+    gains[:, HALF + HALO :, PROBES:] = none
+    for flat in flats:
+        flat[...] = jnp.zeros((LEVP, 128), F32)
+    for which, ref in enumerate((u, v, mix)):
+        for band in range(BANDS):
+            turn(coef, (which, band), ref[band], flats[band % 4], which == 2)
+    split_all(coef, BANDS)
+
+
+def split_all(coef, bands):
+    lane = lax.broadcasted_iota(jnp.int32, (LEVP, 128), 1)
+
+    def split(at, carry):
+        for which in range(3):
+            for k in range(4):
+                x = coef[which, at * 4 + k]
+                coef[which, at * 4 + k] = two_terms(x + pltpu.roll(x, 64, 1), lane)
+        return carry
+
+    lax.fori_loop(0, bands // 4, split, 0)
+
+
+def pack_edges(odd, conc, flux, u, v, mix):
     out = jax.ShapeDtypeStruct((BANDS, 2, LEVP, 128), F32)
     last = COLS // HALO - 1
     shape = (BANDS, HALO, LEVS, PROBES)
@@ -182,14 +207,20 @@
             in_specs=[
                 pl.BlockSpec(shape, lambda i, odd: (0, last * near_west(odd), 0, 0)),
                 pl.BlockSpec(shape, lambda i, odd: (0, last * (1 - near_west(odd)), 0, 0)),
-                whole(),
-            ],
-            out_specs=[whole()] * 2,
+            ]
+            + [whole()] * 4,
+            out_specs=[whole()] * 4,
+            scratch_shapes=[pltpu.VMEM((LEVP, 128), F32)] * 4,
         ),
-        out_shape=[out, out],
+        out_shape=[
+            out,
+            out,
+            jax.ShapeDtypeStruct((BANDS, PAIRS, 128), F32),
+            jax.ShapeDtypeStruct((3, BANDS, LEVP, 128), F32),
+        ],
         compiler_params=params(62),
         name="pack_edges",
-    )(odd, conc, conc, flux)
+    )(odd, conc, conc, flux, u, v, mix)
 
 
 def row_code(cells, shift):
@@ -207,13 +238,7 @@
     return jnp.where(held, row, ZERO_ROW), cross.astype(F32)
 
 
-def prepare_kernel(odd, flux, u, v, mix, far, near, cells, gains, coef, codes, turned, *flats):
-    high = HALF - HALO
-    none = jnp.zeros((BANDS, HALO, PROBES), F32)
-    gains[:, 0:HALO, 0:PROBES] = none
-    gains[:, HALO:, 0:PROBES] = flux[:, 0 : HALF + HALO]
-    gains[:, 0 : HALF + HALO, PROBES:] = flux[:, high:]
-    gains[:, HALF + HALO :, PROBES:] = none
+def margins_kernel(odd, far, near, cells, coef, codes, turned, *flats):
     north = north_far(odd) * 2 - 1
     places = (
         (cells[...], 0),
@@ -231,46 +256,34 @@
             turned[group, 128 * k : 128 * k + 128] = jnp.where(lower, low, up)
     for flat in flats:
         flat[...] = jnp.zeros((LEVP, 128), F32)
-    far_at = north_far(odd) * (HALO + BANDS)
-    near_at = HALO + BANDS - far_at
-    for which, ref in enumerate((u, v, mix)):
-        for band in range(BANDS):
-            turn(coef, (which, band + HALO), ref[band], flats[band % 4], which == 2)
+    far_at = north_far(odd) * HALO
+    near_at = HALO - far_at
+    for which in range(3):
         for band in range(HALO):
             row, lane = lat_at(which, band)
             for k, (first, src) in enumerate(((far_at, far), (near_at, near))):
                 rows = src[row : row + COLS, lane : lane + LEVS]
                 turn(coef, (which, first + band), rows, flats[band % 2 * 2 + k], which == 2)
-    lane = lax.broadcasted_iota(jnp.int32, (LEVP, 128), 1)
-
-    def split(at, carry):
-        for which in range(3):
-            for k in range(4):
-                x = coef[which, at * 4 + k]
-                coef[which, at * 4 + k] = two_terms(x + pltpu.roll(x, 64, 1), lane)
-        return carry
-
-    lax.fori_loop(0, TALL // 4, split, 0)
-
-
-def prepare(odd, flux, u, v, mix, far, near, cells):
+    split_all(coef, 2 * HALO)
+
+
+def margins(odd, far, near, cells):
     return pl.pallas_call(
-        prepare_kernel,
-        in_specs=[whole(pltpu.SMEM)] + [whole()] * 7,
-        out_specs=[whole()] * 4,
+        margins_kernel,
+        in_specs=[whole(pltpu.SMEM)] + [whole()] * 3,
+        out_specs=[whole()] * 3,
         out_shape=[
-            jax.ShapeDtypeStruct((BANDS, PAIRS, 128), F32),
-            jax.ShapeDtypeStruct((3, TALL, LEVP, 128), F32),
+            jax.ShapeDtypeStruct((3, 2 * HALO, LEVP, 128), F32),
             jax.ShapeDtypeStruct((24, 128), jnp.int32),
             jax.ShapeDtypeStruct((3, SLOTS // 2, 128), F32),
         ],
         scratch_shapes=[pltpu.VMEM((LEVP, 128), F32)] * 4,
         compiler_params=params(62),
-        name="prepare",
-    )(odd, flux, u, v, mix, far, near, cells.reshape(8, 128))
-
-
-def join_coef(odd, split, coef, far, near, sides, flat):
+        name="margins",
+    )(odd, far, near, cells.reshape(8, 128))
+
+
+def join_coef(odd, split, own, beyond, far, near, sides, flat):
     span = 5 * HALO
     lane = lax.broadcasted_iota(jnp.int32, (8, 128), 1)
     west_near = near_west(odd) == 1
@@ -293,19 +306,27 @@
     column = lax.broadcasted_iota(jnp.int32, (LEVP, 128), 1) & 63
     margin = (column < HALO) | ((column >= HALO + COLS) & (column < WIDE))
 
-    def join(group, carry):
-        for k in range(5):
-            band = group * 5 + k
-            rows = pl.ds(pl.multiple_of(band * LEVP, LEVP), LEVP)
-            for which in range(3):
-                beside = sides[which, group]
-                if k:
-                    beside = pltpu.roll(beside, 128 - HALO * k, 1)
-                x = jnp.where(margin, beside, coef[which, band])
-                split[which, rows] = x.astype(jnp.bfloat16)
-        return carry
-
-    lax.fori_loop(0, 4, join, 0)
+    def join(band, ref, at):
+        group = lax.div(band, 5)
+        rows = pl.ds(pl.multiple_of(band * LEVP, LEVP), LEVP)
+        for which in range(3):
+            shift = lax.rem(128 - HALO * lax.rem(band, 5), 128)
+            beside = pltpu.roll(sides[which, group], shift, 1)
+            x = jnp.where(margin, beside, ref[which, at])
+            split[which, rows] = x.astype(jnp.bfloat16)
+
+    def inner(at, carry):
+        for k in range(4):
+            join(HALO + 4 * at + k, own, 4 * at + k)
+        return carry
+
+    def outer(at, carry):
+        for k in range(HALO):
+            join(at * (HALO + BANDS) + k, beyond, at * HALO + k)
+        return carry
+
+    lax.fori_loop(0, BANDS // 4, inner, 0)
+    lax.fori_loop(0, 2, outer, 0)
 
 
 def selector(tile, low, high, high_sign=1.0):
@@ -366,7 +387,7 @@
 
 
 def transport_kernel(
-    odd, conc, flux, coef, far, near, out, split,
+    odd, conc, flux, own, beyond, far, near, out, split,
     c, u, v, m, fs, line0, line1, sides, flat, stage, in_sem, out_sem,
 ):
     def fetch(band):
@@ -375,7 +396,7 @@
 
     for band in range(RING):
         fetch(band).start()
-    join_coef(odd, split, coef, far, near, sides, flat)
+    join_coef(odd, split, own, beyond, far, near, sides, flat)
 
     def expand(tile):
         chosen = selector(tile, lambda pair: pair, lambda pair: pair + HALF)
@@ -449,12 +470,12 @@
     lax.fori_loop(0, TALL, drain, 0)
 
 
-def transport(odd, conc, flux, coef, far, near):
+def transport(odd, conc, flux, own, beyond, far, near):
     field = pltpu.VMEM((TALL, PAIRS, LEVP, 128), F32)
     line = pltpu.VMEM((PAIRS, LEVP, 128), F32)
     return pl.pallas_call(
         transport_kernel,
-        in_specs=[whole(pltpu.SMEM), whole(pl.ANY)] + [whole()] * 4,
+        in_specs=[whole(pltpu.SMEM), whole(pl.ANY)] + [whole()] * 5,
         out_specs=[whole(pl.ANY), whole()],
         out_shape=[
             jax.ShapeDtypeStruct((TALL, HALF, LEVP, 128), F32),
@@ -476,7 +497,7 @@
         ],
         compiler_params=params(62),
         name="transport",
-    )(odd, conc, flux, coef, far, near)
+    )(odd, conc, flux, own, beyond, far, near)
 
 
 def strips_kernel(
@@ -501,19 +522,24 @@
 
     lax.fori_loop(0, TALL, clear, 0)
     lower = lax.broadcasted_iota(jnp.int32, (LEVP, 128), 1) < PROBES
-    inside = lax.broadcasted_iota(jnp.int32, (LEVP, 128), 0) < LEVS
-
+    inside = lax.broadcasted_iota(jnp.int32, (8, 128), 0) < 7
+    low_lanes = lax.broadcasted_iota(jnp.int32, (8, 128), 1) < PROBES
     west_near = near_west(odd) == 1
 
     def place(band, carry):
         for k in range(2):
-            left = jnp.where(west_near, edge_near[band, k], edge_far[band, k])
-            right = jnp.where(west_near, edge_far[band, 1 - k], edge_near[band, 1 - k])
-            outer = jnp.where(lower, left, right)
-            inner = pltpu.roll(jnp.where(lower, right, left), PROBES, 1)
-            for at, value in ((k, outer), (k + 2, inner)):
-                c[band + HALO, at] = jnp.where(inside, value, 0.0)
-                gain[band, at, 0:1] = value[LEVS:LEVP]
+            for tile in range(TILES):
+                rows = pl.ds(tile, 8, stride=TILES)
+                one, two = edge_far[band, k, rows], edge_near[band, k, rows]
+                three, four = edge_far[band, 1 - k, rows], edge_near[band, 1 - k, rows]
+                left, right = jnp.where(west_near, two, one), jnp.where(west_near, three, four)
+                outer = jnp.where(low_lanes, left, right)
+                inner = pltpu.roll(jnp.where(low_lanes, right, left), PROBES, 1)
+                for at, value in ((k, outer), (k + 2, inner)):
+                    if tile == TILES - 1:
+                        gain[band, at, 0:1] = value[7:8]
+                        value = jnp.where(inside, value, 0.0)
+                    c[band + HALO, at, 8 * tile : 8 * tile + 8] = value
         return carry
 
     lax.fori_loop(0, BANDS, place, 0)
@@ -555,27 +581,28 @@
 
     lax.fori_loop(0, TALL, merge, 0)
 
+    half = SLOTS // 2
     left_lanes = lax.broadcasted_iota(jnp.int32, (8, 128), 1) < PROBES
     for group, (out, buffer) in enumerate(((own, got0), (far, got1), (near, got2))):
 
         def pick(at, carry):
-            rows = buffer.at[pl.ds(pl.multiple_of(at * 128, 128), 128)]
-            for k in range(128):
-                rows[k : k + 1] = full[pl.ds(codes[group * 8 + at, k], 1)]
-            return carry
-
-        lax.fori_loop(0, SLOTS // 128, pick, 0)
-
-        def join(at, carry):
-            for k in range(16):
-                at8 = pl.multiple_of(at * 128 + k * 8, 8)
-                one, two = buffer[pl.ds(at8, 8)], buffer[pl.ds(at8 + SLOTS // 2, 8)]
+            first = pl.multiple_of(at * 128, 128)
+            rows = buffer.at[pl.ds(first, 128)], buffer.at[pl.ds(first + half, 128)]
+            done = out.at[pl.ds(first, 128)]
+            cross = turned.at[group, pl.ds(first, 128)]
+            for tile in range(16):
+                tiles = slice(8 * tile, 8 * tile + 8)
+                for part in range(2):
+                    for k in range(8 * tile, 8 * tile + 8):
+                        place = codes[group * 8 + at + 4 * part, k]
+                        rows[part][k : k + 1] = full[pl.ds(place, 1)]
+                one, two = rows[0][tiles], rows[1][tiles]
                 straight = jnp.where(left_lanes, one, two)
                 crossed = pltpu.roll(jnp.where(left_lanes, two, one), PROBES, 1)
-                out[pl.ds(at8, 8)] = jnp.where(turned[group, pl.ds(at8, 8)] > 0.5, crossed, straight)
+                done[tiles] = jnp.where(cross[tiles] > 0.5, crossed, straight)
             return carry
 
-        lax.fori_loop(0, SLOTS // 256, join, 0)
+        lax.fori_loop(0, half // 128, pick, 0)
 
 
 def strips(odd, codes, turned, far, near, split, field):
@@ -608,7 +635,7 @@
 
 
 def gram_kernel(own, far, near, weight, images, gram):
-    rows = (own[...] + far[...] + near[...]) * weight[...]
+    rows = own[...] + (far[...] + near[...]) * weight[...]
     images[...] = rows
     both = lax.dot_general(
         rows, rows, (((0,), (0,)), ((), ())), precision=HIGHEST, preferred_element_type=F32
@@ -710,20 +737,20 @@
     to_far, to_near, own_west, own_east = pack_lat(odd, u_courant, v_courant, vert_mix, obs_cell)
     from_far = swap(to_far, "lat", True)
     from_near = swap(to_near, "lat", False)
-    edges = pack_edges(odd, conc_start, flux_probes)
+    *edges, gains, own = pack_edges(
+        odd, conc_start, flux_probes, u_courant, v_courant, vert_mix
+    )
     own_west, own_east, *edges = lax.optimization_barrier((own_west, own_east, *edges))
     lon_far, lon_near = pack_lon(odd, own_west, own_east, from_far, from_near)
     lon_far = swap(lon_far, "lon", True, wrap=True)
     lon_near = swap(lon_near, "lon", False)
-    gains, coef, codes, turned = prepare(
-        odd, flux_probes, u_courant, v_courant, vert_mix, from_far, from_near, obs_cell
-    )
-    edge_far, edge_near, coef, lon_far, lon_near = lax.optimization_barrier(
-        (*edges, coef, lon_far, lon_near)
+    beyond, codes, turned = margins(odd, from_far, from_near, obs_cell)
+    edge_far, edge_near, beyond, lon_far, lon_near = lax.optimization_barrier(
+        (*edges, beyond, lon_far, lon_near)
     )
     edge_far = swap(edge_far, "lon", True, wrap=True)
     edge_near = swap(edge_near, "lon", False)
-    field, split = transport(odd, conc_start, gains, coef, lon_far, lon_near)
+    field, split = transport(odd, conc_start, gains, own, beyond, lon_far, lon_near)
     rows, for_far, for_near = strips(
         odd, codes, turned, edge_far, edge_near, split, field.reshape(FIELD_ROWS, 128)
     )
@@ -739,7 +766,7 @@
         ],
         axis=1,
     )
-    images, gram = gram_of(rows, far_rows, near_rows, weight)
+    images, gram = gram_of(rows * weight, far_rows, near_rows, weight)
     gram = all_sum(gram)
     total_rows = SLOTS * lax.axis_size("lon") * lax.axis_size("lat")
     basis_t, factor = factor_of(gram, images, float(total_rows) ** 0.5)

time: 111 us -> 110 us (level)
    pallas_call x1, Pallas kernels: 5.78 us -> 4.49 us  [margins(): pl.pallas_call(margins_kernel, in_specs=[whole(pltpu.SMEM)] + [whole()] *...]
  transfers between devices with their start and end apart: 18 -> 18, of which waited for: 8 -> 7; matrix products, arithmetic and copies ran while one was open for 0% -> 1% of each run, Pallas kernels for 36% -> 36%
where the time goes in v4:
time: 110 us; the launch traced here: 109 us
  Pallas kernels  59.2 us (54%)
  starting transfers between devices  34.4 us (31%)
  waiting for transfers between devices  11.7 us (11%)
  between operations  1.53 us (1%)
  local copies, waits for them, and re-layouts  1.29 us (1%)
  other arithmetic  1.12 us (1%)
    pallas_call x1, Pallas kernels, transport(): pl.pallas_call(transport_kernel, in_specs=[whole(pltpu.SMEM), whole(pl.AN...  29.8 us
    ppermute x10, starting transfers between devices, all_sum(): lax.ppermute(x, ('lon', 'lat'), [(i, i ^ m) for i in range(size)])  19.7 us
    ppermute x8, starting transfers between devices, swap(): lax.ppermute(x, axis, [(i, j) for i, j in enumerate(partner) if 0 <= j <...  14.7 us
    pallas_call x1, Pallas kernels, strips(): pl.pallas_call(strips_kernel, in_specs=[whole(pltpu.SMEM), whole(pltpu.SM...  13.9 us
    ppermute x10, waiting for transfers between devices, all_sum(): lax.ppermute(x, ('lon', 'lat'), [(i, i ^ m) for i in range(size)])  11.7 us
    pallas_call x1, Pallas kernels, pack_edges(): pl.pallas_call(edges_kernel, grid_spec=pltpu.PrefetchScalarGridSpec(num_s...  5.32 us
    pallas_call x1, Pallas kernels, margins(): pl.pallas_call(margins_kernel, in_specs=[whole(pltpu.SMEM)] + [whole()] *...  4.49 us
    pallas_call x1, Pallas kernels, factor_of(): pl.pallas_call(lambda *refs: factor_kernel(root, *refs), in_specs=[whole(...  3 us
  transfers between devices with their start and end apart: 18, of which 7 were waited for; matrix products, arithmetic and copies ran while one was open for 1% of the time, Pallas kernels for 36%

profile of v4, /device:TPU:0, one launch (start us, length us, event | category | flops | bytes accessed | tf_op | source)
XLA Modules:
  0.0 109.3 jit_solution(8967011168246288293)
XLA Ops:
  0.6 2.1 %pack_lat.1 = (f32[248,128]{1,0:T(8,128)}, f32[248,128]{1,0:T(8,128)}, f32[3,5,8,128]{3,2,1,0:T(8,128)}, f32[3,5,8,128]{3,2,1,0:T(8,128)}) custom-call(s32[1]{0:T(128)} %bitcast.odd, f32[12,36,47]{2,1,0:T(8,128)} %u.3, f32[12,36,47]{2,1,0:T(8,128)} %v.3, f32[12,36,47]{2,1,0:T(8,128)} %mix.3, s32[8,128]{1,0:T(8,128)} %bitcast.7), custom_call_target="tpu_custom_call" | custom-call | tf_op jit(solution)/shard_map/pack_lat/pallas_call | solution.py:93
  2.7 0.7 collective-permute-start
  3.4 0.0 copy-start.8
  3.4 3.1 %collective-permute-start.1 = (f32[248,128]{1,0:T(8,128)}, f32[248,128]{1,0:T(8,128)S(1)}, u32[]{:S(2)}, u32[]{:S(2)}) collective-permute-start(f32[248,128]{1,0:T(8,128)} %get-tuple-element.34), channel_id=1, source_target_pairs={{0,1},{1,0},{2,3},{3,2},{4,5},{5,4},{6,7},{7,6},{8,9},{9,8},{10,11... | collective-permute-start | bytes 380936 | tf_op jit(solution)/shard_map/ppermute | solution.py:43
  6.5 5.3 %pack_edges.1 = (f32[12,2,48,128]{3,2,1,0:T(8,128)}, f32[12,2,48,128]{3,2,1,0:T(8,128)}, f32[12,26,128]{2,1,0:T(8,128)}, f32[3,12,48,128]{3,2,1,0:T(8,128)}) custom-call(s32[1]{0:T(128)} %bitcast.odd, f32[12,36,47,64]{3,2,1,0:T(8,128)} %conc.1, f32[12,36,47,64]{3,2,1,0:T(8,128)} %conc.1, f32[12,36,64]{2,1,0:T(8,128)} %flux.1, f32[12,36,47]{2,1,0:T(8,128)} %u.3, ...), custom_call_target="tpu_custom_call" | custom-call | tf_op jit(solution)/shard_map/pack_edges/pallas_call | solution.py:202
  11.8 0.0 collective-permute-done.far
  11.8 0.0 collective-permute-done.1.near
  11.9 0.1 pack_lon.1
  12.0 5.0 %collective-permute-start.2 = (f32[3,5,8,128]{3,2,1,0:T(8,128)S(1)}, f32[3,5,8,128]{3,2,1,0:T(8,128)S(1)}, u32[]{:S(2)}, u32[]{:S(2)}) collective-permute-start(f32[3,5,8,128]{3,2,1,0:T(8,128)S(1)} %get-tuple-element.46), channel_id=1, source_target_pairs={{0,112},{16,32},{32,16},{48,64},{64,48},{80,96},{96,80},{112,0},{1... | collective-permute-start | bytes 184328 | tf_op jit(solution)/shard_map/ppermute | solution.py:43
  17.0 0.0 collective-permute-start.3
  17.1 4.5 %margins.1 = (f32[3,8,48,128]{3,2,1,0:T(8,128)}, s32[24,128]{1,0:T(8,128)}, f32[3,512,128]{2,1,0:T(8,128)}) custom-call(s32[1]{0:T(128)} %bitcast.odd, f32[248,128]{1,0:T(8,128)} %copy-done, f32[248,128]{1,0:T(8,128)} %copy-done.1, s32[8,128]{1,0:T(8,128)} %bitcast.8), custom_call_target="tpu_custom_call" | custom-call | tf_op jit(solution)/shard_map/margins/pallas_call | solution.py:271
  21.6 0.0 collective-permute-done.2.far
  21.6 0.0 collective-permute-done.3.near
  21.6 2.3 %collective-permute-start.4 = (f32[12,2,48,128]{3,2,1,0:T(8,128)}, f32[12,2,48,128]{3,2,1,0:T(8,128)S(1)}, u32[]{:S(2)}, u32[]{:S(2)}) collective-permute-start(f32[12,2,48,128]{3,2,1,0:T(8,128)} %get-tuple-element.48), channel_id=1, source_target_pairs={{0,112},{16,32},{32,16},{48,64},{64,48},{80,96},{96,80},{112,0},{1... | collective-permute-start | bytes 1769480 | tf_op jit(solution)/shard_map/ppermute | solution.py:43
  23.8 0.0 collective-permute-start.5
  24.5 29.8 %transport.1 = (f32[20,18,48,128]{3,2,1,0:T(8,128)}, bf16[3,960,128]{2,1,0:T(8,128)(2,1)}) custom-call(s32[1]{0:T(128)} %bitcast.odd, f32[12,36,47,64]{3,2,1,0:T(8,128)} %conc.1, f32[12,26,128]{2,1,0:T(8,128)} %get-tuple-element.50.flux, f32[3,12,48,128]{3,2,1,0:T(8,128)} %get-tuple-element.51.own, f32[3,8,48,128]{3,2,1,0:T(8,128)} %get-tuple-element.52.beyond, ...), custom_call_target="tpu_custom_call" | custom-call | tf_op jit(solution)/shard_map/transport/pallas_call | solution.py:476
  54.3 0.0 collective-permute-done.4.edge_far
  54.3 0.0 collective-permute-done.5.edge_near
  54.4 0.8 copy-done.4
  55.1 0.2 copy-done.5
  55.4 13.9 %strips.1 = (f32[512,128]{1,0:T(8,128)}, f32[512,128]{1,0:T(8,128)}, f32[512,128]{1,0:T(8,128)}) custom-call(s32[1]{0:T(128)} %bitcast.odd, s32[24,128]{1,0:T(8,128)} %get-tuple-element.35.codes, f32[3,512,128]{2,1,0:T(8,128)} %get-tuple-element.36.turned, f32[12,2,48,128]{3,2,1,0:T(8,128)} %copy-done.4, f32[12,2,48,128]{3,2,1,0:T(8,128)} %copy-done.5, ...), custom_call_target="tpu_custom_call" | custom-call | tf_op jit(solution)/shard_map/strips/pallas_call | solution.py:612
  69.2 0.7 collective-permute-start.6
  69.9 3.0 %collective-permute-start.7 = (f32[512,128]{1,0:T(8,128)}, f32[512,128]{1,0:T(8,128)S(1)}, u32[]{:S(2)}, u32[]{:S(2)}) collective-permute-start(f32[512,128]{1,0:T(8,128)} %get-tuple-element.59), channel_id=1, source_target_pairs={{0,1},{1,0},{2,3},{3,2},{4,5},{5,4},{6,7},{7,6},{8,9},{9,8},{10,11... | collective-permute-start | bytes 786440 | tf_op jit(solution)/shard_map/ppermute | solution.py:43
  72.9 0.1 broadcast_in_dim.18
  73.1 0.1 broadcast_in_dim.9
  73.2 1.1 pad_maximum_fusion
  74.3 0.0 collective-permute-done.6.far
  74.3 0.0 collective-permute-done.7.near
  74.3 0.6 gram.1
  74.9 2.8 %collective-permute-start.8 = (f32[32,128]{1,0:T(8,128)S(1)}, f32[32,128]{1,0:T(8,128)S(1)}, u32[]{:S(2)}, u32[]{:S(2)}) collective-permute-start(f32[32,128]{1,0:T(8,128)S(1)} %get-tuple-element.60), channel_id=1, source_target_pairs={{0,1},{1,0},{2,3},{3,2},{4,5},{5,4},{6,7},{7,6},{8,9},{9,8},{10,11... | collective-permute-start | bytes 49160 | tf_op jit(solution)/shard_map/ppermute | solution.py:51
  77.7 0.8 collective-permute-done.8
  78.5 3.6 %collective-permute-start.10 = (f32[32,128]{1,0:T(8,128)S(1)}, f32[32,128]{1,0:T(8,128)S(1)}, u32[]{:S(2)}, u32[]{:S(2)}) collective-permute-start(f32[32,128]{1,0:T(8,128)S(1)} %add.43), channel_id=1, source_target_pairs={{0,4},{1,5},{2,6},{3,7},{4,0},{5,1},{6,2},{7,3},{8,12},{9,13},{10,... | collective-permute-start | bytes 49160 | tf_op jit(solution)/shard_map/ppermute | solution.py:51
  82.1 3.1 %collective-permute-start.11 = (f32[32,128]{1,0:T(8,128)S(1)}, f32[32,128]{1,0:T(8,128)S(1)}, u32[]{:S(2)}, u32[]{:S(2)}) collective-permute-start(f32[32,128]{1,0:T(8,128)S(1)} %add.43), channel_id=1, source_target_pairs={{0,6},{1,7},{2,4},{3,5},{4,2},{5,3},{6,0},{7,1},{8,14},{9,15},{10,... | collective-permute-start | bytes 49160 | tf_op jit(solution)/shard_map/ppermute | solution.py:51
  85.2 0.8 collective-permute-start.9
  86.0 0.0 collective-permute-done.10
  86.0 1.1 %collective-permute-done.11 = f32[32,128]{1,0:T(8,128)S(1)} collective-permute-done((f32[32,128]{1,0:T(8,128)S(1)}, f32[32,128]{1,0:T(8,128)S(1)}, u32[]{:S(2)}, u32[]{:S(2)}) %collective-permute-start.11) | collective-permute-done | bytes 16416 | tf_op jit(solution)/shard_map/ppermute | solution.py:51
  87.1 1.8 %collective-permute-done.9 = f32[32,128]{1,0:T(8,128)S(1)} collective-permute-done((f32[32,128]{1,0:T(8,128)S(1)}, f32[32,128]{1,0:T(8,128)S(1)}, u32[]{:S(2)}, u32[]{:S(2)}) %collective-permute-start.9) | collective-permute-done | bytes 16416 | tf_op jit(solution)/shard_map/ppermute | solution.py:51
  88.9 1.4 %collective-permute-start.12 = (f32[32,128]{1,0:T(8,128)S(1)}, f32[32,128]{1,0:T(8,128)S(1)}, u32[]{:S(2)}, u32[]{:S(2)}) collective-permute-start(f32[32,128]{1,0:T(8,128)S(1)} %add_add_fusion.2), channel_id=1, source_target_pairs={{0,32},{1,33},{2,34},{3,35},{4,36},{5,37},{6,38},{7,39},{8,40},{9,... | collective-permute-start | bytes 49160 | tf_op jit(solution)/shard_map/ppermute | solution.py:51
  90.3 2.7 %collective-permute-start.13 = (f32[32,128]{1,0:T(8,128)S(1)}, f32[32,128]{1,0:T(8,128)S(1)}, u32[]{:S(2)}, u32[]{:S(2)}) collective-permute-start(f32[32,128]{1,0:T(8,128)S(1)} %add_add_fusion.2), channel_id=1, source_target_pairs={{0,64},{1,65},{2,66},{3,67},{4,68},{5,69},{6,70},{7,71},{8,72},{9,... | collective-permute-start | bytes 49160 | tf_op jit(solution)/shard_map/ppermute | solution.py:51
  93.0 0.6 collective-permute-start.14
  93.6 1.9 %collective-permute-done.13 = f32[32,128]{1,0:T(8,128)S(1)} collective-permute-done((f32[32,128]{1,0:T(8,128)S(1)}, f32[32,128]{1,0:T(8,128)S(1)}, u32[]{:S(2)}, u32[]{:S(2)}) %collective-permute-start.13) | collective-permute-done | bytes 16416 | tf_op jit(solution)/shard_map/ppermute | solution.py:51
  95.6 2.4 %collective-permute-done.14 = f32[32,128]{1,0:T(8,128)S(1)} collective-permute-done((f32[32,128]{1,0:T(8,128)S(1)}, f32[32,128]{1,0:T(8,128)S(1)}, u32[]{:S(2)}, u32[]{:S(2)}) %collective-permute-start.14) | collective-permute-done | bytes 16416 | tf_op jit(solution)/shard_map/ppermute | solution.py:51
  97.9 0.3 collective-permute-start.15
  98.2 3.1 %collective-permute-start.16 = (f32[32,128]{1,0:T(8,128)S(1)}, f32[32,128]{1,0:T(8,128)S(1)}, u32[]{:S(2)}, u32[]{:S(2)}) collective-permute-start(f32[32,128]{1,0:T(8,128)S(1)} %add_add_fusion.1), channel_id=1, source_target_pairs={{0,8},{1,9},{2,10},{3,11},{4,12},{5,13},{6,14},{7,15},{8,0},{9,1},... | collective-permute-start | bytes 49160 | tf_op jit(solution)/shard_map/ppermute | solution.py:51
  101.3 1.4 %collective-permute-start.17 = (f32[32,128]{1,0:T(8,128)S(1)}, f32[32,128]{1,0:T(8,128)S(1)}, u32[]{:S(2)}, u32[]{:S(2)}) collective-permute-start(f32[32,128]{1,0:T(8,128)S(1)} %add_add_fusion.1), channel_id=1, source_target_pairs={{0,24},{1,25},{2,26},{3,27},{4,28},{5,29},{6,30},{7,31},{8,16},{9,... | collective-permute-start | bytes 49160 | tf_op jit(solution)/shard_map/ppermute | solution.py:51
  102.7 0.8 collective-permute-done.16
  103.5 2.8 %collective-permute-done.17 = f32[32,128]{1,0:T(8,128)S(1)} collective-permute-done((f32[32,128]{1,0:T(8,128)S(1)}, f32[32,128]{1,0:T(8,128)S(1)}, u32[]{:S(2)}, u32[]{:S(2)}) %collective-permute-start.17) | collective-permute-done | bytes 16416 | tf_op jit(solution)/shard_map/ppermute | solution.py:51
  106.3 3.0 %factor.1 = (f32[64,1024]{1,0:T(8,128)}, f32[64,64]{1,0:T(8,128)}) custom-call(f32[32,128]{1,0:T(8,128)S(1)} %add_add_fusion.refs_0_, f32[512,128]{1,0:T(8,128)S(1)} %get-tuple-element.61.refs_1_), custom_call_target="tpu_custom_call" | custom-call | tf_op jit(solution)/shard_map/factor/pallas_call | solution.py:719
  (23 shorter events, 0.1 us)
Async XLA Ops:
  2.7 9.1 %collective-permute-start = (f32[248,128]{1,0:T(8,128)}, f32[248,128]{1,0:T(8,128)S(1)}, u32[]{:S(2)}, u32[]{:S(2)}) collective-permute-start(f32[248,128]{1,0:T(8,128)} %get-tuple-element.33), channel_id=1, source_target_pairs={{1,2},{2,1},{3,4},{4,3},{5,6},{6,5},{7,8},{8,7},{9,10},{10,9},{11,... | collective-permute-start | bytes 380936 | tf_op jit(solution)/shard_map/ppermute | solution.py:43
  3.4 8.5 %copy-start.2 = (f32[3,5,8,128]{3,2,1,0:T(8,128)S(1)}, f32[3,5,8,128]{3,2,1,0:T(8,128)}, u32[]{:S(2)}) copy-start(f32[3,5,8,128]{3,2,1,0:T(8,128)} %get-tuple-element.44.west) | copy-start | bytes 184324
  3.4 8.5 %copy-start.3 = (f32[3,5,8,128]{3,2,1,0:T(8,128)S(1)}, f32[3,5,8,128]{3,2,1,0:T(8,128)}, u32[]{:S(2)}) copy-start(f32[3,5,8,128]{3,2,1,0:T(8,128)} %get-tuple-element.45.east) | copy-start | bytes 184324
  3.4 21.1 %copy-start.8 = (f32[1024]{0:T(1024)S(1)}, f32[1024]{0:T(1024)}, u32[]{:S(2)}) copy-start(f32[1024]{0:T(1024)} %param.14) | copy-start | bytes 12292
  3.4 8.4 %collective-permute-start.1 = (f32[248,128]{1,0:T(8,128)}, f32[248,128]{1,0:T(8,128)S(1)}, u32[]{:S(2)}, u32[]{:S(2)}) collective-permute-start(f32[248,128]{1,0:T(8,128)} %get-tuple-element.34), channel_id=1, source_target_pairs={{0,1},{1,0},{2,3},{3,2},{4,5},{5,4},{6,7},{7,6},{8,9},{9,8},{10,11... | collective-permute-start | bytes 380936 | tf_op jit(solution)/shard_map/ppermute | solution.py:43
  11.8 5.2 %copy-start = (f32[248,128]{1,0:T(8,128)}, f32[248,128]{1,0:T(8,128)S(1)}, u32[]{:S(2)}) copy-start(f32[248,128]{1,0:T(8,128)S(1)} %collective-permute-done.far) | copy-start | bytes 380932
  11.9 5.2 %copy-start.1 = (f32[248,128]{1,0:T(8,128)}, f32[248,128]{1,0:T(8,128)S(1)}, u32[]{:S(2)}) copy-start(f32[248,128]{1,0:T(8,128)S(1)} %collective-permute-done.1.near) | copy-start | bytes 380932
  12.0 9.6 %collective-permute-start.2 = (f32[3,5,8,128]{3,2,1,0:T(8,128)S(1)}, f32[3,5,8,128]{3,2,1,0:T(8,128)S(1)}, u32[]{:S(2)}, u32[]{:S(2)}) collective-permute-start(f32[3,5,8,128]{3,2,1,0:T(8,128)S(1)} %get-tuple-element.46), channel_id=1, source_target_pairs={{0,112},{16,32},{32,16},{48,64},{64,48},{80,96},{96,80},{112,0},{1... | collective-permute-start | bytes 184328 | tf_op jit(solution)/shard_map/ppermute | solution.py:43
  17.0 4.5 %collective-permute-start.3 = (f32[3,5,8,128]{3,2,1,0:T(8,128)S(1)}, f32[3,5,8,128]{3,2,1,0:T(8,128)S(1)}, u32[]{:S(2)}, u32[]{:S(2)}) collective-permute-start(f32[3,5,8,128]{3,2,1,0:T(8,128)S(1)} %get-tuple-element.47), channel_id=1, source_target_pairs={{0,16},{16,0},{32,48},{48,32},{64,80},{80,64},{96,112},{112,96},{1... | collective-permute-start | bytes 184328 | tf_op jit(solution)/shard_map/ppermute | solution.py:43
  21.6 3.0 %copy-start.6 = (f32[3,5,8,128]{3,2,1,0:T(8,128)}, f32[3,5,8,128]{3,2,1,0:T(8,128)S(1)}, u32[]{:S(2)}) copy-start(f32[3,5,8,128]{3,2,1,0:T(8,128)S(1)} %collective-permute-done.2.far) | copy-start | bytes 184324
  21.6 3.0 %copy-start.7 = (f32[3,5,8,128]{3,2,1,0:T(8,128)}, f32[3,5,8,128]{3,2,1,0:T(8,128)S(1)}, u32[]{:S(2)}) copy-start(f32[3,5,8,128]{3,2,1,0:T(8,128)S(1)} %collective-permute-done.3.near) | copy-start | bytes 184324
  21.6 32.7 %collective-permute-start.4 = (f32[12,2,48,128]{3,2,1,0:T(8,128)}, f32[12,2,48,128]{3,2,1,0:T(8,128)S(1)}, u32[]{:S(2)}, u32[]{:S(2)}) collective-permute-start(f32[12,2,48,128]{3,2,1,0:T(8,128)} %get-tuple-element.48), channel_id=1, source_target_pairs={{0,112},{16,32},{32,16},{48,64},{64,48},{80,96},{96,80},{112,0},{1... | collective-permute-start | bytes 1769480 | tf_op jit(solution)/shard_map/ppermute | solution.py:43
  23.8 30.5 %collective-permute-start.5 = (f32[12,2,48,128]{3,2,1,0:T(8,128)}, f32[12,2,48,128]{3,2,1,0:T(8,128)S(1)}, u32[]{:S(2)}, u32[]{:S(2)}) collective-permute-start(f32[12,2,48,128]{3,2,1,0:T(8,128)} %get-tuple-element.49), channel_id=1, source_target_pairs={{0,16},{16,0},{32,48},{48,32},{64,80},{80,64},{96,112},{112,96},{1... | collective-permute-start | bytes 1769480 | tf_op jit(solution)/shard_map/ppermute | solution.py:43
  54.3 0.8 copy-start.4
  54.4 1.0 copy-start.5
  69.2 5.1 %collective-permute-start.6 = (f32[512,128]{1,0:T(8,128)}, f32[512,128]{1,0:T(8,128)S(1)}, u32[]{:S(2)}, u32[]{:S(2)}) collective-permute-start(f32[512,128]{1,0:T(8,128)} %get-tuple-element.58), channel_id=1, source_target_pairs={{1,2},{2,1},{3,4},{4,3},{5,6},{6,5},{7,8},{8,7},{9,10},{10,9},{11,... | collective-permute-start | bytes 786440 | tf_op jit(solution)/shard_map/ppermute | solution.py:43
  69.9 4.4 %collective-permute-start.7 = (f32[512,128]{1,0:T(8,128)}, f32[512,128]{1,0:T(8,128)S(1)}, u32[]{:S(2)}, u32[]{:S(2)}) collective-permute-start(f32[512,128]{1,0:T(8,128)} %get-tuple-element.59), channel_id=1, source_target_pairs={{0,1},{1,0},{2,3},{3,2},{4,5},{5,4},{6,7},{7,6},{8,9},{9,8},{10,11... | collective-permute-start | bytes 786440 | tf_op jit(solution)/shard_map/ppermute | solution.py:43
  74.9 3.7 %collective-permute-start.8 = (f32[32,128]{1,0:T(8,128)S(1)}, f32[32,128]{1,0:T(8,128)S(1)}, u32[]{:S(2)}, u32[]{:S(2)}) collective-permute-start(f32[32,128]{1,0:T(8,128)S(1)} %get-tuple-element.60), channel_id=1, source_target_pairs={{0,1},{1,0},{2,3},{3,2},{4,5},{5,4},{6,7},{7,6},{8,9},{9,8},{10,11... | collective-permute-start | bytes 49160 | tf_op jit(solution)/shard_map/ppermute | solution.py:51
  78.5 7.5 %collective-permute-start.10 = (f32[32,128]{1,0:T(8,128)S(1)}, f32[32,128]{1,0:T(8,128)S(1)}, u32[]{:S(2)}, u32[]{:S(2)}) collective-permute-start(f32[32,128]{1,0:T(8,128)S(1)} %add.43), channel_id=1, source_target_pairs={{0,4},{1,5},{2,6},{3,7},{4,0},{5,1},{6,2},{7,3},{8,12},{9,13},{10,... | collective-permute-start | bytes 49160 | tf_op jit(solution)/shard_map/ppermute | solution.py:51
  82.1 4.9 %collective-permute-start.11 = (f32[32,128]{1,0:T(8,128)S(1)}, f32[32,128]{1,0:T(8,128)S(1)}, u32[]{:S(2)}, u32[]{:S(2)}) collective-permute-start(f32[32,128]{1,0:T(8,128)S(1)} %add.43), channel_id=1, source_target_pairs={{0,6},{1,7},{2,4},{3,5},{4,2},{5,3},{6,0},{7,1},{8,14},{9,15},{10,... | collective-permute-start | bytes 49160 | tf_op jit(solution)/shard_map/ppermute | solution.py:51
  85.2 3.7 %collective-permute-start.9 = (f32[32,128]{1,0:T(8,128)S(1)}, f32[32,128]{1,0:T(8,128)S(1)}, u32[]{:S(2)}, u32[]{:S(2)}) collective-permute-start(f32[32,128]{1,0:T(8,128)S(1)} %add.43), channel_id=1, source_target_pairs={{0,2},{1,3},{2,0},{3,1},{4,6},{5,7},{6,4},{7,5},{8,10},{9,11},{10,... | collective-permute-start | bytes 49160 | tf_op jit(solution)/shard_map/ppermute | solution.py:51
  88.9 4.7 %collective-permute-start.12 = (f32[32,128]{1,0:T(8,128)S(1)}, f32[32,128]{1,0:T(8,128)S(1)}, u32[]{:S(2)}, u32[]{:S(2)}) collective-permute-start(f32[32,128]{1,0:T(8,128)S(1)} %add_add_fusion.2), channel_id=1, source_target_pairs={{0,32},{1,33},{2,34},{3,35},{4,36},{5,37},{6,38},{7,39},{8,40},{9,... | collective-permute-start | bytes 49160 | tf_op jit(solution)/shard_map/ppermute | solution.py:51
  90.3 5.2 %collective-permute-start.13 = (f32[32,128]{1,0:T(8,128)S(1)}, f32[32,128]{1,0:T(8,128)S(1)}, u32[]{:S(2)}, u32[]{:S(2)}) collective-permute-start(f32[32,128]{1,0:T(8,128)S(1)} %add_add_fusion.2), channel_id=1, source_target_pairs={{0,64},{1,65},{2,66},{3,67},{4,68},{5,69},{6,70},{7,71},{8,72},{9,... | collective-permute-start | bytes 49160 | tf_op jit(solution)/shard_map/ppermute | solution.py:51
  93.0 4.9 %collective-permute-start.14 = (f32[32,128]{1,0:T(8,128)S(1)}, f32[32,128]{1,0:T(8,128)S(1)}, u32[]{:S(2)}, u32[]{:S(2)}) collective-permute-start(f32[32,128]{1,0:T(8,128)S(1)} %add_add_fusion.2), channel_id=1, source_target_pairs={{0,96},{1,97},{2,98},{3,99},{4,100},{5,101},{6,102},{7,103},{8,104... | collective-permute-start | bytes 49160 | tf_op jit(solution)/shard_map/ppermute | solution.py:51
  97.9 4.7 %collective-permute-start.15 = (f32[32,128]{1,0:T(8,128)S(1)}, f32[32,128]{1,0:T(8,128)S(1)}, u32[]{:S(2)}, u32[]{:S(2)}) collective-permute-start(f32[32,128]{1,0:T(8,128)S(1)} %add_add_fusion.1), channel_id=1, source_target_pairs={{0,16},{1,17},{2,18},{3,19},{4,20},{5,21},{6,22},{7,23},{8,24},{9,... | collective-permute-start | bytes 49160 | tf_op jit(solution)/shard_map/ppermute | solution.py:51
  98.2 5.2 %collective-permute-start.16 = (f32[32,128]{1,0:T(8,128)S(1)}, f32[32,128]{1,0:T(8,128)S(1)}, u32[]{:S(2)}, u32[]{:S(2)}) collective-permute-start(f32[32,128]{1,0:T(8,128)S(1)} %add_add_fusion.1), channel_id=1, source_target_pairs={{0,8},{1,9},{2,10},{3,11},{4,12},{5,13},{6,14},{7,15},{8,0},{9,1},... | collective-permute-start | bytes 49160 | tf_op jit(solution)/shard_map/ppermute | solution.py:51
  101.3 4.9 %collective-permute-start.17 = (f32[32,128]{1,0:T(8,128)S(1)}, f32[32,128]{1,0:T(8,128)S(1)}, u32[]{:S(2)}, u32[]{:S(2)}) collective-permute-start(f32[32,128]{1,0:T(8,128)S(1)} %add_add_fusion.1), channel_id=1, source_target_pairs={{0,24},{1,25},{2,26},{3,27},{4,28},{5,29},{6,30},{7,31},{8,16},{9,... | collective-permute-start | bytes 49160 | tf_op jit(solution)/shard_map/ppermute | solution.py:51

commit v5 on v4

--- a/solution.py
+++ b/solution.py
@@ -13,12 +13,12 @@
 LEVP = 48
 TILES = LEVP // 8
 COLP = 40
-RING = 6
 BLOCK = 8
 LAT_ROWS = 3 * (HALO // 2) * COLP
 LON_BANDS = TALL // 2
 HALF = COLS // 2
-PAIRS = HALF + 2 * HALO
+SPILL = 2
+PAIRS = SPILL + HALF
 SLOTS = 1024
 FIELD_ROWS = TALL * HALF * LEVP
 ZERO_ROW = FIELD_ROWS
@@ -168,12 +168,8 @@
             return carry
 
         lax.fori_loop(0, BANDS // 2, pack, 0)
-    high = HALF - HALO
-    none = jnp.zeros((BANDS, HALO, PROBES), F32)
-    gains[:, 0:HALO, 0:PROBES] = none
-    gains[:, HALO:, 0:PROBES] = flux[:, 0 : HALF + HALO]
-    gains[:, 0 : HALF + HALO, PROBES:] = flux[:, high:]
-    gains[:, HALF + HALO :, PROBES:] = none
+    gains[:, :, 0:PROBES] = flux[:, :HALF]
+    gains[:, :, PROBES:] = flux[:, HALF:]
     for flat in flats:
         flat[...] = jnp.zeros((LEVP, 128), F32)
     for which, ref in enumerate((u, v, mix)):
@@ -215,7 +211,7 @@
         out_shape=[
             out,
             out,
-            jax.ShapeDtypeStruct((BANDS, PAIRS, 128), F32),
+            jax.ShapeDtypeStruct((BANDS, HALF, 128), F32),
             jax.ShapeDtypeStruct((3, BANDS, LEVP, 128), F32),
         ],
         compiler_params=params(62),
@@ -386,50 +382,105 @@
         mix_levels(c, line1, m, band + 1, pair)
 
 
+def block_rows(step, band, c, u, v, m, fs, line0, line1, last):
+    north = jnp.minimum(band + 2, TALL - 1)
+    lower = lax.broadcasted_iota(jnp.int32, (LEVP, 128), 1) < PROBES
+    begin, end = SPILL, PAIRS - 1
+    fluxes, spills = [], []
+    for k in range(2):
+        at = band + k
+        far, near, head, tail = (c[at, place] for place in (0, 1, begin, end))
+        into = face_flux(u[at, begin], jnp.where(lower, near, pltpu.roll(tail, PROBES, 1)), head)
+        out = face_flux(u[at, 1], tail, jnp.where(lower, pltpu.roll(head, PROBES, 1), near))
+        last[k] = out
+        fluxes.append(into)
+        if step < STEPS:
+            outer = face_flux(
+                u[at, 0], jnp.where(lower, far, near), jnp.where(lower, near, far)
+            )
+            net = {1: jnp.where(lower, outer - into, out - outer)}
+            if step == 2:
+                net[0] = jnp.where(lower, -outer, outer)
+            spills.append(net)
+
+    def advance(place, here0, here1, net0, net1):
+        middle = face_flux(v[band + 1, place], here0, here1)
+        top = face_flux(v[north, place], here1, c[north, place])
+        line0[place] = net0 + (fs[place] - middle)
+        line1[place] = net1 + (middle - top)
+        fs[place] = top
+
+    places = list(range(begin, PAIRS))
+    if step < STEPS:
+        for place in spills[0]:
+            here0, here1 = c[band, place], c[band + 1, place]
+            advance(place, here0, here1, here0 + spills[0][place], here1 + spills[1][place])
+            places.append(place)
+    here0, here1 = c[band, begin], c[band + 1, begin]
+    west0, west1 = fluxes
+    for place in range(begin, PAIRS):
+        net0, net1 = here0 + west0, here1 + west1
+        old0, old1 = here0, here1
+        if place < end:
+            here0, here1 = c[band, place + 1], c[band + 1, place + 1]
+            west0 = face_flux(u[band, place + 1], old0, here0)
+            west1 = face_flux(u[band + 1, place + 1], old1, here1)
+        else:
+            west0, west1 = last[0], last[1]
+        advance(place, old0, old1, net0 - west0, net1 - west1)
+    for place in places:
+        mix_levels(c, line0, m, band, place)
+        mix_levels(c, line1, m, band + 1, place)
+
+
 def transport_kernel(
     odd, conc, flux, own, beyond, far, near, out, split,
-    c, u, v, m, fs, line0, line1, sides, flat, stage, in_sem, out_sem,
+    c, u, v, m, fs, line0, line1, last, sides, flat, stage, in_sem, out_sem,
 ):
     def fetch(band):
-        slot = lax.rem(band, RING)
-        return pltpu.make_async_copy(conc.at[band], stage.at[slot], in_sem.at[slot])
-
-    for band in range(RING):
+        return pltpu.make_async_copy(conc.at[band], stage.at[band], in_sem.at[band])
+
+    for band in range(BANDS):
         fetch(band).start()
     join_coef(odd, split, own, beyond, far, near, sides, flat)
 
     def expand(tile):
-        chosen = selector(tile, lambda pair: pair, lambda pair: pair + HALF)
+        def cells(low, shift):
+            outside = jnp.where(low == 1, HALO - 1 if not shift else HALO + COLS, HALO - 2 if not shift else HALO + COLS + 1)
+            return jnp.where(low >= SPILL, low + HALO - SPILL + shift, outside)
+
+        def faces(low, shift):
+            outside = jnp.where(low == 1, HALO + HALF + shift, HALO - 1 if not shift else HALO + COLS + 1)
+            return jnp.where(low >= SPILL, low + HALO - SPILL + shift, outside)
+
+        at_faces = selector(tile, lambda p: faces(p, 0), lambda p: faces(p, HALF))
+        at_cells = selector(tile, lambda p: cells(p, 0), lambda p: cells(p, HALF))
         half = TALL // 2
-        for which, ref in enumerate((u, v, m)):
+        for which, (ref, chosen) in enumerate(((u, at_faces), (v, at_cells), (m, at_cells))):
             for first in (0, half):
                 yield lambda: spread(ref, split.at[which], chosen, tile, first, half)
 
-    zero = jnp.zeros((8, PROBES), F32)
-
-    def load(band, carry):
-        slot = lax.rem(band, RING)
+    def load(band, pieces):
         fetch(band).wait()
-        pieces = expand(band)
-        for pair in range(PAIRS):
-            low, high = pair - HALO, pair - HALO + HALF
+        for pair in range(HALF):
             for t in range(TILES):
-                left = level_tile(stage, (slot, low), t) if low >= 0 else zero
-                right = level_tile(stage, (slot, high), t) if high < COLS else zero
-                both = jnp.concatenate([left, right], axis=1)
-                c[band + HALO, pair, 8 * t : 8 * t + 8] = both
-            if pair % 4 == 3:
+                both = [level_tile(stage, (band, col), t) for col in (pair, pair + HALF)]
+                both = jnp.concatenate(both, axis=1)
+                c[band + HALO, SPILL + pair, 8 * t : 8 * t + 8] = both
+            if pieces is not None and pair % 3 == 2:
                 next(pieces)()
-
-        @pl.when(band + RING < BANDS)
-        def _():
-            fetch(band + RING).start()
-
-        return carry
-
-    lax.fori_loop(0, BANDS, load, 0)
-    for piece in expand(BANDS):
-        piece()
+        c[band + HALO, 0:SPILL] = jnp.zeros((SPILL, LEVP, 128), F32)
+
+    def load_and_expand(band, carry):
+        load(band, expand(band))
+        return carry
+
+    def load_only(band, carry):
+        load(band, None)
+        return carry
+
+    lax.fori_loop(0, PAIRS // 2, load_and_expand, 0)
+    lax.fori_loop(PAIRS // 2, BANDS, load_only, 0)
 
     def clear(band, carry):
         c[band] = jnp.zeros((PAIRS, LEVP, 128), F32)
@@ -439,23 +490,22 @@
     lax.fori_loop(0, HALO, clear, 0)
 
     def save(band):
-        return pltpu.make_async_copy(c.at[band, pl.ds(HALO, HALF)], out.at[band], out_sem.at[band])
+        return pltpu.make_async_copy(c.at[band, pl.ds(SPILL, HALF)], out.at[band], out_sem.at[band])
 
     for step in range(1, STEPS + 1):
-        first, last = step, PAIRS - step
-        count = last - first
 
         def gain(band, carry):
-            for pair in range(PAIRS):
-                c[band + HALO, pair, 0:1] = c[band + HALO, pair, 0:1] + flux[band, pair : pair + 1]
+            for pair in range(HALF):
+                at = SPILL + pair
+                c[band + HALO, at, 0:1] = c[band + HALO, at, 0:1] + flux[band, pair : pair + 1]
             return carry
 
         lax.fori_loop(0, BANDS, gain, 0)
-        fs[first:last] = jnp.zeros((count, LEVP, 128), F32)
+        fs[...] = jnp.zeros((PAIRS, LEVP, 128), F32)
 
         def rows(at, carry):
             band = HALO - step + 2 * at
-            two_rows(band, range(first, last), c, u, v, m, fs, line0, line1)
+            block_rows(step, band, c, u, v, m, fs, line0, line1, last)
             if step == STEPS:
                 save(band).start()
                 save(band + 1).start()
@@ -489,10 +539,11 @@
             line,
             line,
             line,
+            pltpu.VMEM((2, LEVP, 128), F32),
             pltpu.VMEM((3, 4, LEVP, 128), F32),
             pltpu.VMEM((LEVP, 128), F32),
-            pltpu.VMEM((RING, COLS, LEVS, PROBES), F32),
-            pltpu.SemaphoreType.DMA((RING,)),
+            pltpu.VMEM((BANDS, COLS, LEVS, PROBES), F32),
+            pltpu.SemaphoreType.DMA((BANDS,)),
             pltpu.SemaphoreType.DMA((TALL,)),
         ],
         compiler_params=params(62),

time: 110 us -> 108 us (0.982)
  Pallas kernels: 59.2 us -> 57.5 us
    pallas_call x1, Pallas kernels: 29.8 us -> 28.1 us  [transport(): pl.pallas_call(transport_kernel, in_specs=[whole(pltpu.SMEM), whole(pl.AN...]
  transfers between devices with their start and end apart: 18 -> 18, of which waited for: 7 -> 7; matrix products, arithmetic and copies ran while one was open for 1% -> 1% of each run, Pallas kernels for 36% -> 35%
where the time goes in v5:
time: 108 us
  Pallas kernels  57.5 us (53%)
  starting transfers between devices  34.4 us (32%)
  waiting for transfers between devices  11.7 us (11%)
  between operations  1.53 us (1%)
  local copies, waits for them, and re-layouts  1.29 us (1%)
  other arithmetic  1.12 us (1%)
    pallas_call x1, Pallas kernels, transport(): pl.pallas_call(transport_kernel, in_specs=[whole(pltpu.SMEM), whole(pl.AN...  28.1 us
    ppermute x10, starting transfers between devices, all_sum(): lax.ppermute(x, ('lon', 'lat'), [(i, i ^ m) for i in range(size)])  19.7 us
    ppermute x8, starting transfers between devices, swap(): lax.ppermute(x, axis, [(i, j) for i, j in enumerate(partner) if 0 <= j <...  14.7 us
    pallas_call x1, Pallas kernels, strips(): pl.pallas_call(strips_kernel, in_specs=[whole(pltpu.SMEM), whole(pltpu.SM...  13.9 us
    ppermute x10, waiting for transfers between devices, all_sum(): lax.ppermute(x, ('lon', 'lat'), [(i, i ^ m) for i in range(size)])  11.7 us
    pallas_call x1, Pallas kernels, pack_edges(): pl.pallas_call(edges_kernel, grid_spec=pltpu.PrefetchScalarGridSpec(num_s...  5.3 us
    pallas_call x1, Pallas kernels, margins(): pl.pallas_call(margins_kernel, in_specs=[whole(pltpu.SMEM)] + [whole()] *...  4.49 us
    pallas_call x1, Pallas kernels, factor_of(): pl.pallas_call(lambda *refs: factor_kernel(root, *refs), in_specs=[whole(...  3 us
  transfers between devices with their start and end apart: 18, of which 7 were waited for; matrix products, arithmetic and copies ran while one was open for 1% of the time, Pallas kernels for 35%

profile of v5, /device:TPU:0, one launch (start us, length us, event | category | flops | bytes accessed | tf_op | source)
XLA Modules:
  0.0 107.6 jit_solution(16287084801422547221)
XLA Ops:
  0.6 2.1 %pack_lat.1 = (f32[248,128]{1,0:T(8,128)}, f32[248,128]{1,0:T(8,128)}, f32[3,5,8,128]{3,2,1,0:T(8,128)}, f32[3,5,8,128]{3,2,1,0:T(8,128)}) custom-call(s32[1]{0:T(128)} %bitcast.odd, f32[12,36,47]{2,1,0:T(8,128)} %u.3, f32[12,36,47]{2,1,0:T(8,128)} %v.3, f32[12,36,47]{2,1,0:T(8,128)} %mix.3, s32[8,128]{1,0:T(8,128)} %bitcast.7), custom_call_target="tpu_custom_call" | custom-call | tf_op jit(solution)/shard_map/pack_lat/pallas_call | solution.py:93
  2.7 0.7 collective-permute-start
  3.4 0.0 copy-start.8
  3.4 3.1 %collective-permute-start.1 = (f32[248,128]{1,0:T(8,128)}, f32[248,128]{1,0:T(8,128)S(1)}, u32[]{:S(2)}, u32[]{:S(2)}) collective-permute-start(f32[248,128]{1,0:T(8,128)} %get-tuple-element.34), channel_id=1, source_target_pairs={{0,1},{1,0},{2,3},{3,2},{4,5},{5,4},{6,7},{7,6},{8,9},{9,8},{10,11... | collective-permute-start | bytes 380936 | tf_op jit(solution)/shard_map/ppermute | solution.py:43
  6.5 5.3 %pack_edges.1 = (f32[12,2,48,128]{3,2,1,0:T(8,128)}, f32[12,2,48,128]{3,2,1,0:T(8,128)}, f32[12,18,128]{2,1,0:T(8,128)}, f32[3,12,48,128]{3,2,1,0:T(8,128)}) custom-call(s32[1]{0:T(128)} %bitcast.odd, f32[12,36,47,64]{3,2,1,0:T(8,128)} %conc.1, f32[12,36,47,64]{3,2,1,0:T(8,128)} %conc.1, f32[12,36,64]{2,1,0:T(8,128)} %flux.1, f32[12,36,47]{2,1,0:T(8,128)} %u.3, ...), custom_call_target="tpu_custom_call" | custom-call | tf_op jit(solution)/shard_map/pack_edges/pallas_call | solution.py:198
  11.8 0.0 collective-permute-done.far
  11.8 0.0 collective-permute-done.1.near
  11.9 0.1 pack_lon.1
  12.0 5.0 %collective-permute-start.2 = (f32[3,5,8,128]{3,2,1,0:T(8,128)S(1)}, f32[3,5,8,128]{3,2,1,0:T(8,128)S(1)}, u32[]{:S(2)}, u32[]{:S(2)}) collective-permute-start(f32[3,5,8,128]{3,2,1,0:T(8,128)S(1)} %get-tuple-element.46), channel_id=1, source_target_pairs={{0,112},{16,32},{32,16},{48,64},{64,48},{80,96},{96,80},{112,0},{1... | collective-permute-start | bytes 184328 | tf_op jit(solution)/shard_map/ppermute | solution.py:43
  17.0 0.0 collective-permute-start.3
  17.0 4.5 %margins.1 = (f32[3,8,48,128]{3,2,1,0:T(8,128)}, s32[24,128]{1,0:T(8,128)}, f32[3,512,128]{2,1,0:T(8,128)}) custom-call(s32[1]{0:T(128)} %bitcast.odd, f32[248,128]{1,0:T(8,128)} %copy-done, f32[248,128]{1,0:T(8,128)} %copy-done.1, s32[8,128]{1,0:T(8,128)} %bitcast.8), custom_call_target="tpu_custom_call" | custom-call | tf_op jit(solution)/shard_map/margins/pallas_call | solution.py:267
  21.5 0.0 collective-permute-done.2.far
  21.5 0.0 collective-permute-done.3.near
  21.6 2.3 %collective-permute-start.4 = (f32[12,2,48,128]{3,2,1,0:T(8,128)}, f32[12,2,48,128]{3,2,1,0:T(8,128)S(1)}, u32[]{:S(2)}, u32[]{:S(2)}) collective-permute-start(f32[12,2,48,128]{3,2,1,0:T(8,128)} %get-tuple-element.48), channel_id=1, source_target_pairs={{0,112},{16,32},{32,16},{48,64},{64,48},{80,96},{96,80},{112,0},{1... | collective-permute-start | bytes 1769480 | tf_op jit(solution)/shard_map/ppermute | solution.py:43
  23.8 0.0 collective-permute-start.5
  24.5 28.1 %transport.1 = (f32[20,18,48,128]{3,2,1,0:T(8,128)}, bf16[3,960,128]{2,1,0:T(8,128)(2,1)}) custom-call(s32[1]{0:T(128)} %bitcast.odd, f32[12,36,47,64]{3,2,1,0:T(8,128)} %conc.1, f32[12,18,128]{2,1,0:T(8,128)} %get-tuple-element.50.flux, f32[3,12,48,128]{3,2,1,0:T(8,128)} %get-tuple-element.51.own, f32[3,8,48,128]{3,2,1,0:T(8,128)} %get-tuple-element.52.beyond, ...), custom_call_target="tpu_custom_call" | custom-call | tf_op jit(solution)/shard_map/transport/pallas_call | solution.py:526
  52.7 0.0 collective-permute-done.4.edge_far
  52.7 0.0 collective-permute-done.5.edge_near
  52.7 0.8 copy-done.4
  53.5 0.2 copy-done.5
  53.7 13.9 %strips.1 = (f32[512,128]{1,0:T(8,128)}, f32[512,128]{1,0:T(8,128)}, f32[512,128]{1,0:T(8,128)}) custom-call(s32[1]{0:T(128)} %bitcast.odd, s32[24,128]{1,0:T(8,128)} %get-tuple-element.35.codes, f32[3,512,128]{2,1,0:T(8,128)} %get-tuple-element.36.turned, f32[12,2,48,128]{3,2,1,0:T(8,128)} %copy-done.4, f32[12,2,48,128]{3,2,1,0:T(8,128)} %copy-done.5, ...), custom_call_target="tpu_custom_call" | custom-call | tf_op jit(solution)/shard_map/strips/pallas_call | solution.py:663
  67.6 0.7 collective-permute-start.6
  68.2 3.0 %collective-permute-start.7 = (f32[512,128]{1,0:T(8,128)}, f32[512,128]{1,0:T(8,128)S(1)}, u32[]{:S(2)}, u32[]{:S(2)}) collective-permute-start(f32[512,128]{1,0:T(8,128)} %get-tuple-element.59), channel_id=1, source_target_pairs={{0,1},{1,0},{2,3},{3,2},{4,5},{5,4},{6,7},{7,6},{8,9},{9,8},{10,11... | collective-permute-start | bytes 786440 | tf_op jit(solution)/shard_map/ppermute | solution.py:43
  71.3 0.1 broadcast_in_dim.18
  71.4 0.1 broadcast_in_dim.9
  71.5 1.1 %pad_maximum_fusion = (f32[512,128]{1,0:T(8,128)S(1)}, f32[512,128]{1,0:T(8,128)S(1)}) fusion(f32[512,64]{1,0:T(8,128)S(1)} %broadcast_in_dim.18, f32[512,64]{1,0:T(8,128)S(1)} %broadcast_in_dim.9, f32[512,128]{1,0:T(8,128)} %get-tuple-element.57), kind=kLoop, calls=%fused_computation | loop fusion | flops 131072 | bytes 1048576 | tf_op jit(solution)/shard_map/concatenate | solution.py:813
  72.6 0.0 collective-permute-done.6.far
  72.6 0.0 collective-permute-done.7.near
  72.6 0.6 gram.1
  73.2 2.8 %collective-permute-start.8 = (f32[32,128]{1,0:T(8,128)S(1)}, f32[32,128]{1,0:T(8,128)S(1)}, u32[]{:S(2)}, u32[]{:S(2)}) collective-permute-start(f32[32,128]{1,0:T(8,128)S(1)} %get-tuple-element.60), channel_id=1, source_target_pairs={{0,1},{1,0},{2,3},{3,2},{4,5},{5,4},{6,7},{7,6},{8,9},{9,8},{10,11... | collective-permute-start | bytes 49160 | tf_op jit(solution)/shard_map/ppermute | solution.py:51
  76.0 0.8 collective-permute-done.8
  76.9 3.6 %collective-permute-start.10 = (f32[32,128]{1,0:T(8,128)S(1)}, f32[32,128]{1,0:T(8,128)S(1)}, u32[]{:S(2)}, u32[]{:S(2)}) collective-permute-start(f32[32,128]{1,0:T(8,128)S(1)} %add.43), channel_id=1, source_target_pairs={{0,4},{1,5},{2,6},{3,7},{4,0},{5,1},{6,2},{7,3},{8,12},{9,13},{10,... | collective-permute-start | bytes 49160 | tf_op jit(solution)/shard_map/ppermute | solution.py:51
  80.5 3.1 %collective-permute-start.11 = (f32[32,128]{1,0:T(8,128)S(1)}, f32[32,128]{1,0:T(8,128)S(1)}, u32[]{:S(2)}, u32[]{:S(2)}) collective-permute-start(f32[32,128]{1,0:T(8,128)S(1)} %add.43), channel_id=1, source_target_pairs={{0,6},{1,7},{2,4},{3,5},{4,2},{5,3},{6,0},{7,1},{8,14},{9,15},{10,... | collective-permute-start | bytes 49160 | tf_op jit(solution)/shard_map/ppermute | solution.py:51
  83.5 0.8 collective-permute-start.9
  84.3 1.1 collective-permute-done.11
  85.4 1.9 %collective-permute-done.9 = f32[32,128]{1,0:T(8,128)S(1)} collective-permute-done((f32[32,128]{1,0:T(8,128)S(1)}, f32[32,128]{1,0:T(8,128)S(1)}, u32[]{:S(2)}, u32[]{:S(2)}) %collective-permute-start.9) | collective-permute-done | bytes 16416 | tf_op jit(solution)/shard_map/ppermute | solution.py:51
  87.3 1.4 %collective-permute-start.12 = (f32[32,128]{1,0:T(8,128)S(1)}, f32[32,128]{1,0:T(8,128)S(1)}, u32[]{:S(2)}, u32[]{:S(2)}) collective-permute-start(f32[32,128]{1,0:T(8,128)S(1)} %add_add_fusion.2), channel_id=1, source_target_pairs={{0,32},{1,33},{2,34},{3,35},{4,36},{5,37},{6,38},{7,39},{8,40},{9,... | collective-permute-start | bytes 49160 | tf_op jit(solution)/shard_map/ppermute | solution.py:51
  88.7 2.7 %collective-permute-start.13 = (f32[32,128]{1,0:T(8,128)S(1)}, f32[32,128]{1,0:T(8,128)S(1)}, u32[]{:S(2)}, u32[]{:S(2)}) collective-permute-start(f32[32,128]{1,0:T(8,128)S(1)} %add_add_fusion.2), channel_id=1, source_target_pairs={{0,64},{1,65},{2,66},{3,67},{4,68},{5,69},{6,70},{7,71},{8,72},{9,... | collective-permute-start | bytes 49160 | tf_op jit(solution)/shard_map/ppermute | solution.py:51
  91.3 0.6 collective-permute-start.14
  92.0 0.0 collective-permute-done.12
  92.0 1.9 %collective-permute-done.13 = f32[32,128]{1,0:T(8,128)S(1)} collective-permute-done((f32[32,128]{1,0:T(8,128)S(1)}, f32[32,128]{1,0:T(8,128)S(1)}, u32[]{:S(2)}, u32[]{:S(2)}) %collective-permute-start.13) | collective-permute-done | bytes 16416 | tf_op jit(solution)/shard_map/ppermute | solution.py:51
  93.9 2.4 %collective-permute-done.14 = f32[32,128]{1,0:T(8,128)S(1)} collective-permute-done((f32[32,128]{1,0:T(8,128)S(1)}, f32[32,128]{1,0:T(8,128)S(1)}, u32[]{:S(2)}, u32[]{:S(2)}) %collective-permute-start.14) | collective-permute-done | bytes 16416 | tf_op jit(solution)/shard_map/ppermute | solution.py:51
  96.3 0.3 collective-permute-start.15
  96.6 3.0 %collective-permute-start.16 = (f32[32,128]{1,0:T(8,128)S(1)}, f32[32,128]{1,0:T(8,128)S(1)}, u32[]{:S(2)}, u32[]{:S(2)}) collective-permute-start(f32[32,128]{1,0:T(8,128)S(1)} %add_add_fusion.1), channel_id=1, source_target_pairs={{0,8},{1,9},{2,10},{3,11},{4,12},{5,13},{6,14},{7,15},{8,0},{9,1},... | collective-permute-start | bytes 49160 | tf_op jit(solution)/shard_map/ppermute | solution.py:51
  99.6 1.4 %collective-permute-start.17 = (f32[32,128]{1,0:T(8,128)S(1)}, f32[32,128]{1,0:T(8,128)S(1)}, u32[]{:S(2)}, u32[]{:S(2)}) collective-permute-start(f32[32,128]{1,0:T(8,128)S(1)} %add_add_fusion.1), channel_id=1, source_target_pairs={{0,24},{1,25},{2,26},{3,27},{4,28},{5,29},{6,30},{7,31},{8,16},{9,... | collective-permute-start | bytes 49160 | tf_op jit(solution)/shard_map/ppermute | solution.py:51
  101.0 0.8 collective-permute-done.16
  101.8 2.7 %collective-permute-done.17 = f32[32,128]{1,0:T(8,128)S(1)} collective-permute-done((f32[32,128]{1,0:T(8,128)S(1)}, f32[32,128]{1,0:T(8,128)S(1)}, u32[]{:S(2)}, u32[]{:S(2)}) %collective-permute-start.17) | collective-permute-done | bytes 16416 | tf_op jit(solution)/shard_map/ppermute | solution.py:51
  104.6 3.0 %factor.1 = (f32[64,1024]{1,0:T(8,128)}, f32[64,64]{1,0:T(8,128)}) custom-call(f32[32,128]{1,0:T(8,128)S(1)} %add_add_fusion.refs_0_, f32[512,128]{1,0:T(8,128)S(1)} %get-tuple-element.61.refs_1_), custom_call_target="tpu_custom_call" | custom-call | tf_op jit(solution)/shard_map/factor/pallas_call | solution.py:770
  (23 shorter events, 0.1 us)
Async XLA Ops:
  2.7 9.1 %collective-permute-start = (f32[248,128]{1,0:T(8,128)}, f32[248,128]{1,0:T(8,128)S(1)}, u32[]{:S(2)}, u32[]{:S(2)}) collective-permute-start(f32[248,128]{1,0:T(8,128)} %get-tuple-element.33), channel_id=1, source_target_pairs={{1,2},{2,1},{3,4},{4,3},{5,6},{6,5},{7,8},{8,7},{9,10},{10,9},{11,... | collective-permute-start | bytes 380936 | tf_op jit(solution)/shard_map/ppermute | solution.py:43
  3.4 8.4 %copy-start.2 = (f32[3,5,8,128]{3,2,1,0:T(8,128)S(1)}, f32[3,5,8,128]{3,2,1,0:T(8,128)}, u32[]{:S(2)}) copy-start(f32[3,5,8,128]{3,2,1,0:T(8,128)} %get-tuple-element.44.west) | copy-start | bytes 184324
  3.4 8.4 %copy-start.3 = (f32[3,5,8,128]{3,2,1,0:T(8,128)S(1)}, f32[3,5,8,128]{3,2,1,0:T(8,128)}, u32[]{:S(2)}) copy-start(f32[3,5,8,128]{3,2,1,0:T(8,128)} %get-tuple-element.45.east) | copy-start | bytes 184324
  3.4 21.1 %copy-start.8 = (f32[1024]{0:T(1024)S(1)}, f32[1024]{0:T(1024)}, u32[]{:S(2)}) copy-start(f32[1024]{0:T(1024)} %param.14) | copy-start | bytes 12292
  3.4 8.4 %collective-permute-start.1 = (f32[248,128]{1,0:T(8,128)}, f32[248,128]{1,0:T(8,128)S(1)}, u32[]{:S(2)}, u32[]{:S(2)}) collective-permute-start(f32[248,128]{1,0:T(8,128)} %get-tuple-element.34), channel_id=1, source_target_pairs={{0,1},{1,0},{2,3},{3,2},{4,5},{5,4},{6,7},{7,6},{8,9},{9,8},{10,11... | collective-permute-start | bytes 380936 | tf_op jit(solution)/shard_map/ppermute | solution.py:43
  11.8 5.2 %copy-start = (f32[248,128]{1,0:T(8,128)}, f32[248,128]{1,0:T(8,128)S(1)}, u32[]{:S(2)}) copy-start(f32[248,128]{1,0:T(8,128)S(1)} %collective-permute-done.far) | copy-start | bytes 380932
  11.9 5.2 %copy-start.1 = (f32[248,128]{1,0:T(8,128)}, f32[248,128]{1,0:T(8,128)S(1)}, u32[]{:S(2)}) copy-start(f32[248,128]{1,0:T(8,128)S(1)} %collective-permute-done.1.near) | copy-start | bytes 380932
  12.0 9.6 %collective-permute-start.2 = (f32[3,5,8,128]{3,2,1,0:T(8,128)S(1)}, f32[3,5,8,128]{3,2,1,0:T(8,128)S(1)}, u32[]{:S(2)}, u32[]{:S(2)}) collective-permute-start(f32[3,5,8,128]{3,2,1,0:T(8,128)S(1)} %get-tuple-element.46), channel_id=1, source_target_pairs={{0,112},{16,32},{32,16},{48,64},{64,48},{80,96},{96,80},{112,0},{1... | collective-permute-start | bytes 184328 | tf_op jit(solution)/shard_map/ppermute | solution.py:43
  17.0 4.5 %collective-permute-start.3 = (f32[3,5,8,128]{3,2,1,0:T(8,128)S(1)}, f32[3,5,8,128]{3,2,1,0:T(8,128)S(1)}, u32[]{:S(2)}, u32[]{:S(2)}) collective-permute-start(f32[3,5,8,128]{3,2,1,0:T(8,128)S(1)} %get-tuple-element.47), channel_id=1, source_target_pairs={{0,16},{16,0},{32,48},{48,32},{64,80},{80,64},{96,112},{112,96},{1... | collective-permute-start | bytes 184328 | tf_op jit(solution)/shard_map/ppermute | solution.py:43
  21.5 3.0 %copy-start.6 = (f32[3,5,8,128]{3,2,1,0:T(8,128)}, f32[3,5,8,128]{3,2,1,0:T(8,128)S(1)}, u32[]{:S(2)}) copy-start(f32[3,5,8,128]{3,2,1,0:T(8,128)S(1)} %collective-permute-done.2.far) | copy-start | bytes 184324
  21.5 3.0 %copy-start.7 = (f32[3,5,8,128]{3,2,1,0:T(8,128)}, f32[3,5,8,128]{3,2,1,0:T(8,128)S(1)}, u32[]{:S(2)}) copy-start(f32[3,5,8,128]{3,2,1,0:T(8,128)S(1)} %collective-permute-done.3.near) | copy-start | bytes 184324
  21.6 31.1 %collective-permute-start.4 = (f32[12,2,48,128]{3,2,1,0:T(8,128)}, f32[12,2,48,128]{3,2,1,0:T(8,128)S(1)}, u32[]{:S(2)}, u32[]{:S(2)}) collective-permute-start(f32[12,2,48,128]{3,2,1,0:T(8,128)} %get-tuple-element.48), channel_id=1, source_target_pairs={{0,112},{16,32},{32,16},{48,64},{64,48},{80,96},{96,80},{112,0},{1... | collective-permute-start | bytes 1769480 | tf_op jit(solution)/shard_map/ppermute | solution.py:43
  23.8 28.9 %collective-permute-start.5 = (f32[12,2,48,128]{3,2,1,0:T(8,128)}, f32[12,2,48,128]{3,2,1,0:T(8,128)S(1)}, u32[]{:S(2)}, u32[]{:S(2)}) collective-permute-start(f32[12,2,48,128]{3,2,1,0:T(8,128)} %get-tuple-element.49), channel_id=1, source_target_pairs={{0,16},{16,0},{32,48},{48,32},{64,80},{80,64},{96,112},{112,96},{1... | collective-permute-start | bytes 1769480 | tf_op jit(solution)/shard_map/ppermute | solution.py:43
  52.7 0.8 copy-start.4
  52.7 1.0 copy-start.5
  67.6 5.1 %collective-permute-start.6 = (f32[512,128]{1,0:T(8,128)}, f32[512,128]{1,0:T(8,128)S(1)}, u32[]{:S(2)}, u32[]{:S(2)}) collective-permute-start(f32[512,128]{1,0:T(8,128)} %get-tuple-element.58), channel_id=1, source_target_pairs={{1,2},{2,1},{3,4},{4,3},{5,6},{6,5},{7,8},{8,7},{9,10},{10,9},{11,... | collective-permute-start | bytes 786440 | tf_op jit(solution)/shard_map/ppermute | solution.py:43
  68.2 4.4 %collective-permute-start.7 = (f32[512,128]{1,0:T(8,128)}, f32[512,128]{1,0:T(8,128)S(1)}, u32[]{:S(2)}, u32[]{:S(2)}) collective-permute-start(f32[512,128]{1,0:T(8,128)} %get-tuple-element.59), channel_id=1, source_target_pairs={{0,1},{1,0},{2,3},{3,2},{4,5},{5,4},{6,7},{7,6},{8,9},{9,8},{10,11... | collective-permute-start | bytes 786440 | tf_op jit(solution)/shard_map/ppermute | solution.py:43
  73.2 3.7 %collective-permute-start.8 = (f32[32,128]{1,0:T(8,128)S(1)}, f32[32,128]{1,0:T(8,128)S(1)}, u32[]{:S(2)}, u32[]{:S(2)}) collective-permute-start(f32[32,128]{1,0:T(8,128)S(1)} %get-tuple-element.60), channel_id=1, source_target_pairs={{0,1},{1,0},{2,3},{3,2},{4,5},{5,4},{6,7},{7,6},{8,9},{9,8},{10,11... | collective-permute-start | bytes 49160 | tf_op jit(solution)/shard_map/ppermute | solution.py:51
  76.9 7.5 %collective-permute-start.10 = (f32[32,128]{1,0:T(8,128)S(1)}, f32[32,128]{1,0:T(8,128)S(1)}, u32[]{:S(2)}, u32[]{:S(2)}) collective-permute-start(f32[32,128]{1,0:T(8,128)S(1)} %add.43), channel_id=1, source_target_pairs={{0,4},{1,5},{2,6},{3,7},{4,0},{5,1},{6,2},{7,3},{8,12},{9,13},{10,... | collective-permute-start | bytes 49160 | tf_op jit(solution)/shard_map/ppermute | solution.py:51
  80.5 4.9 %collective-permute-start.11 = (f32[32,128]{1,0:T(8,128)S(1)}, f32[32,128]{1,0:T(8,128)S(1)}, u32[]{:S(2)}, u32[]{:S(2)}) collective-permute-start(f32[32,128]{1,0:T(8,128)S(1)} %add.43), channel_id=1, source_target_pairs={{0,6},{1,7},{2,4},{3,5},{4,2},{5,3},{6,0},{7,1},{8,14},{9,15},{10,... | collective-permute-start | bytes 49160 | tf_op jit(solution)/shard_map/ppermute | solution.py:51
  83.5 3.7 %collective-permute-start.9 = (f32[32,128]{1,0:T(8,128)S(1)}, f32[32,128]{1,0:T(8,128)S(1)}, u32[]{:S(2)}, u32[]{:S(2)}) collective-permute-start(f32[32,128]{1,0:T(8,128)S(1)} %add.43), channel_id=1, source_target_pairs={{0,2},{1,3},{2,0},{3,1},{4,6},{5,7},{6,4},{7,5},{8,10},{9,11},{10,... | collective-permute-start | bytes 49160 | tf_op jit(solution)/shard_map/ppermute | solution.py:51
  87.3 4.7 %collective-permute-start.12 = (f32[32,128]{1,0:T(8,128)S(1)}, f32[32,128]{1,0:T(8,128)S(1)}, u32[]{:S(2)}, u32[]{:S(2)}) collective-permute-start(f32[32,128]{1,0:T(8,128)S(1)} %add_add_fusion.2), channel_id=1, source_target_pairs={{0,32},{1,33},{2,34},{3,35},{4,36},{5,37},{6,38},{7,39},{8,40},{9,... | collective-permute-start | bytes 49160 | tf_op jit(solution)/shard_map/ppermute | solution.py:51
  88.7 5.2 %collective-permute-start.13 = (f32[32,128]{1,0:T(8,128)S(1)}, f32[32,128]{1,0:T(8,128)S(1)}, u32[]{:S(2)}, u32[]{:S(2)}) collective-permute-start(f32[32,128]{1,0:T(8,128)S(1)} %add_add_fusion.2), channel_id=1, source_target_pairs={{0,64},{1,65},{2,66},{3,67},{4,68},{5,69},{6,70},{7,71},{8,72},{9,... | collective-permute-start | bytes 49160 | tf_op jit(solution)/shard_map/ppermute | solution.py:51
  91.3 4.9 %collective-permute-start.14 = (f32[32,128]{1,0:T(8,128)S(1)}, f32[32,128]{1,0:T(8,128)S(1)}, u32[]{:S(2)}, u32[]{:S(2)}) collective-permute-start(f32[32,128]{1,0:T(8,128)S(1)} %add_add_fusion.2), channel_id=1, source_target_pairs={{0,96},{1,97},{2,98},{3,99},{4,100},{5,101},{6,102},{7,103},{8,104... | collective-permute-start | bytes 49160 | tf_op jit(solution)/shard_map/ppermute | solution.py:51
  96.3 4.7 %collective-permute-start.15 = (f32[32,128]{1,0:T(8,128)S(1)}, f32[32,128]{1,0:T(8,128)S(1)}, u32[]{:S(2)}, u32[]{:S(2)}) collective-permute-start(f32[32,128]{1,0:T(8,128)S(1)} %add_add_fusion.1), channel_id=1, source_target_pairs={{0,16},{1,17},{2,18},{3,19},{4,20},{5,21},{6,22},{7,23},{8,24},{9,... | collective-permute-start | bytes 49160 | tf_op jit(solution)/shard_map/ppermute | solution.py:51
  96.6 5.2 %collective-permute-start.16 = (f32[32,128]{1,0:T(8,128)S(1)}, f32[32,128]{1,0:T(8,128)S(1)}, u32[]{:S(2)}, u32[]{:S(2)}) collective-permute-start(f32[32,128]{1,0:T(8,128)S(1)} %add_add_fusion.1), channel_id=1, source_target_pairs={{0,8},{1,9},{2,10},{3,11},{4,12},{5,13},{6,14},{7,15},{8,0},{9,1},... | collective-permute-start | bytes 49160 | tf_op jit(solution)/shard_map/ppermute | solution.py:51
  99.6 4.9 %collective-permute-start.17 = (f32[32,128]{1,0:T(8,128)S(1)}, f32[32,128]{1,0:T(8,128)S(1)}, u32[]{:S(2)}, u32[]{:S(2)}) collective-permute-start(f32[32,128]{1,0:T(8,128)S(1)} %add_add_fusion.1), channel_id=1, source_target_pairs={{0,24},{1,25},{2,26},{3,27},{4,28},{5,29},{6,30},{7,31},{8,16},{9,... | collective-permute-start | bytes 49160 | tf_op jit(solution)/shard_map/ppermute | solution.py:51

commit v6 on v5

--- a/solution.py
+++ b/solution.py
@@ -494,13 +494,14 @@
 
     for step in range(1, STEPS + 1):
 
-        def gain(band, carry):
-            for pair in range(HALF):
-                at = SPILL + pair
-                c[band + HALO, at, 0:1] = c[band + HALO, at, 0:1] + flux[band, pair : pair + 1]
+        def gain(at, carry):
+            for band in range(3):
+                for pair in range(HALF):
+                    spot = 3 * at + band + HALO, SPILL + pair, slice(0, 1)
+                    c[spot] = c[spot] + flux[3 * at + band, pair : pair + 1]
             return carry
 
-        lax.fori_loop(0, BANDS, gain, 0)
+        lax.fori_loop(0, BANDS // 3, gain, 0)
         fs[...] = jnp.zeros((PAIRS, LEVP, 128), F32)
 
         def rows(at, carry):
@@ -558,26 +559,12 @@
     fetch = pltpu.make_async_copy(field, full.at[pl.ds(0, FIELD_ROWS)], sem)
     fetch.start()
 
-    def expand(tile, carry):
-        faces = selector(tile, lambda k: k, lambda k: WIDE - k, -1.0)
-        cells = selector(tile, lambda k: k, lambda k: WIDE - 1 - k)
-        for which, ref in enumerate((u, v, m)):
-            spread(ref, split.at[which], cells if which else faces, tile)
-        return carry
-
-    lax.fori_loop(0, HALO, expand, 0)
-
-    def clear(band, carry):
-        c[band] = jnp.zeros((2 * HALO, LEVP, 128), F32)
-        return carry
-
-    lax.fori_loop(0, TALL, clear, 0)
     lower = lax.broadcasted_iota(jnp.int32, (LEVP, 128), 1) < PROBES
     inside = lax.broadcasted_iota(jnp.int32, (8, 128), 0) < 7
     low_lanes = lax.broadcasted_iota(jnp.int32, (8, 128), 1) < PROBES
     west_near = near_west(odd) == 1
 
-    def place(band, carry):
+    def place(band):
         for k in range(2):
             for tile in range(TILES):
                 rows = pl.ds(tile, 8, stride=TILES)
@@ -591,9 +578,21 @@
                         gain[band, at, 0:1] = value[7:8]
                         value = jnp.where(inside, value, 0.0)
                     c[band + HALO, at, 8 * tile : 8 * tile + 8] = value
+
+    def expand(tile, carry):
+        faces = selector(tile, lambda k: k, lambda k: WIDE - k, -1.0)
+        cells = selector(tile, lambda k: k, lambda k: WIDE - 1 - k)
+        none = jnp.zeros((HALO, LEVP, 128), F32)
+        for which, ref in enumerate((u, v, m)):
+            spread(ref, split.at[which], cells if which else faces, tile)
+            place(3 * tile + which)
+        for k in range(TALL // 4):
+            c[tile * (TALL // 4) + k, HALO:] = none
+        c[tile, 0:HALO] = none
+        c[tile + HALO + BANDS, 0:HALO] = none
         return carry
 
-    lax.fori_loop(0, BANDS, place, 0)
+    lax.fori_loop(0, HALO, expand, 0)
 
     full[ZERO_ROW : ZERO_ROW + 8] = jnp.zeros((8, 128), F32)
 

time: 108 us -> 107 us (level)
  Pallas kernels: 57.5 us -> 56.2 us
    pallas_call x1, Pallas kernels: 13.9 us -> 12.7 us  [strips(): pl.pallas_call(strips_kernel, in_specs=[whole(pltpu.SMEM), whole(pltpu.SM...]
  transfers between devices with their start and end apart: 18 -> 18, of which waited for: 7 -> 7; matrix products, arithmetic and copies ran while one was open for 1% -> 1% of each run, Pallas kernels for 35% -> 36%
where the time goes in v6:
time: 107 us; the launch traced here: 106 us
  Pallas kernels  56.2 us (53%)
  starting transfers between devices  34.4 us (32%)
  waiting for transfers between devices  11.7 us (11%)
  between operations  1.53 us (1%)
  local copies, waits for them, and re-layouts  1.29 us (1%)
  other arithmetic  1.12 us (1%)
    pallas_call x1, Pallas kernels, transport(): pl.pallas_call(transport_kernel, in_specs=[whole(pltpu.SMEM), whole(pl.AN...  27.9 us
    ppermute x10, starting transfers between devices, all_sum(): lax.ppermute(x, ('lon', 'lat'), [(i, i ^ m) for i in range(size)])  19.7 us
    ppermute x8, starting transfers between devices, swap(): lax.ppermute(x, axis, [(i, j) for i, j in enumerate(partner) if 0 <= j <...  14.7 us
    pallas_call x1, Pallas kernels, strips(): pl.pallas_call(strips_kernel, in_specs=[whole(pltpu.SMEM), whole(pltpu.SM...  12.7 us
    ppermute x10, waiting for transfers between devices, all_sum(): lax.ppermute(x, ('lon', 'lat'), [(i, i ^ m) for i in range(size)])  11.7 us
    pallas_call x1, Pallas kernels, pack_edges(): pl.pallas_call(edges_kernel, grid_spec=pltpu.PrefetchScalarGridSpec(num_s...  5.3 us
    pallas_call x1, Pallas kernels, margins(): pl.pallas_call(margins_kernel, in_specs=[whole(pltpu.SMEM)] + [whole()] *...  4.49 us
    pallas_call x1, Pallas kernels, factor_of(): pl.pallas_call(lambda *refs: factor_kernel(root, *refs), in_specs=[whole(...  3 us
  transfers between devices with their start and end apart: 18, of which 7 were waited for; matrix products, arithmetic and copies ran while one was open for 1% of the time, Pallas kernels for 36%

profile of v6, /device:TPU:0, one launch (start us, length us, event | category | flops | bytes accessed | tf_op | source)
XLA Modules:
  0.0 106.2 jit_solution(9398650573481367046)
XLA Ops:
  0.6 2.1 %pack_lat.1 = (f32[248,128]{1,0:T(8,128)}, f32[248,128]{1,0:T(8,128)}, f32[3,5,8,128]{3,2,1,0:T(8,128)}, f32[3,5,8,128]{3,2,1,0:T(8,128)}) custom-call(s32[1]{0:T(128)} %bitcast.odd, f32[12,36,47]{2,1,0:T(8,128)} %u.3, f32[12,36,47]{2,1,0:T(8,128)} %v.3, f32[12,36,47]{2,1,0:T(8,128)} %mix.3, s32[8,128]{1,0:T(8,128)} %bitcast.7), custom_call_target="tpu_custom_call" | custom-call | tf_op jit(solution)/shard_map/pack_lat/pallas_call | solution.py:93
  2.7 0.7 collective-permute-start
  3.4 0.0 copy-start.8
  3.4 3.1 %collective-permute-start.1 = (f32[248,128]{1,0:T(8,128)}, f32[248,128]{1,0:T(8,128)S(1)}, u32[]{:S(2)}, u32[]{:S(2)}) collective-permute-start(f32[248,128]{1,0:T(8,128)} %get-tuple-element.34), channel_id=1, source_target_pairs={{0,1},{1,0},{2,3},{3,2},{4,5},{5,4},{6,7},{7,6},{8,9},{9,8},{10,11... | collective-permute-start | bytes 380936 | tf_op jit(solution)/shard_map/ppermute | solution.py:43
  6.5 5.3 %pack_edges.1 = (f32[12,2,48,128]{3,2,1,0:T(8,128)}, f32[12,2,48,128]{3,2,1,0:T(8,128)}, f32[12,18,128]{2,1,0:T(8,128)}, f32[3,12,48,128]{3,2,1,0:T(8,128)}) custom-call(s32[1]{0:T(128)} %bitcast.odd, f32[12,36,47,64]{3,2,1,0:T(8,128)} %conc.1, f32[12,36,47,64]{3,2,1,0:T(8,128)} %conc.1, f32[12,36,64]{2,1,0:T(8,128)} %flux.1, f32[12,36,47]{2,1,0:T(8,128)} %u.3, ...), custom_call_target="tpu_custom_call" | custom-call | tf_op jit(solution)/shard_map/pack_edges/pallas_call | solution.py:198
  11.8 0.0 collective-permute-done.far
  11.8 0.0 collective-permute-done.1.near
  11.9 0.1 pack_lon.1
  12.0 5.0 %collective-permute-start.2 = (f32[3,5,8,128]{3,2,1,0:T(8,128)S(1)}, f32[3,5,8,128]{3,2,1,0:T(8,128)S(1)}, u32[]{:S(2)}, u32[]{:S(2)}) collective-permute-start(f32[3,5,8,128]{3,2,1,0:T(8,128)S(1)} %get-tuple-element.46), channel_id=1, source_target_pairs={{0,112},{16,32},{32,16},{48,64},{64,48},{80,96},{96,80},{112,0},{1... | collective-permute-start | bytes 184328 | tf_op jit(solution)/shard_map/ppermute | solution.py:43
  17.0 0.0 collective-permute-start.3
  17.0 4.5 %margins.1 = (f32[3,8,48,128]{3,2,1,0:T(8,128)}, s32[24,128]{1,0:T(8,128)}, f32[3,512,128]{2,1,0:T(8,128)}) custom-call(s32[1]{0:T(128)} %bitcast.odd, f32[248,128]{1,0:T(8,128)} %copy-done, f32[248,128]{1,0:T(8,128)} %copy-done.1, s32[8,128]{1,0:T(8,128)} %bitcast.8), custom_call_target="tpu_custom_call" | custom-call | tf_op jit(solution)/shard_map/margins/pallas_call | solution.py:267
  21.5 0.0 collective-permute-done.2.far
  21.5 0.0 collective-permute-done.3.near
  21.6 2.3 %collective-permute-start.4 = (f32[12,2,48,128]{3,2,1,0:T(8,128)}, f32[12,2,48,128]{3,2,1,0:T(8,128)S(1)}, u32[]{:S(2)}, u32[]{:S(2)}) collective-permute-start(f32[12,2,48,128]{3,2,1,0:T(8,128)} %get-tuple-element.48), channel_id=1, source_target_pairs={{0,112},{16,32},{32,16},{48,64},{64,48},{80,96},{96,80},{112,0},{1... | collective-permute-start | bytes 1769480 | tf_op jit(solution)/shard_map/ppermute | solution.py:43
  23.8 0.0 collective-permute-start.5
  24.5 27.9 %transport.1 = (f32[20,18,48,128]{3,2,1,0:T(8,128)}, bf16[3,960,128]{2,1,0:T(8,128)(2,1)}) custom-call(s32[1]{0:T(128)} %bitcast.odd, f32[12,36,47,64]{3,2,1,0:T(8,128)} %conc.1, f32[12,18,128]{2,1,0:T(8,128)} %get-tuple-element.50.flux, f32[3,12,48,128]{3,2,1,0:T(8,128)} %get-tuple-element.51.own, f32[3,8,48,128]{3,2,1,0:T(8,128)} %get-tuple-element.52.beyond, ...), custom_call_target="tpu_custom_call" | custom-call | tf_op jit(solution)/shard_map/transport/pallas_call | solution.py:527
  52.5 0.0 collective-permute-done.4.edge_far
  52.5 0.0 collective-permute-done.5.edge_near
  52.5 0.8 copy-done.4
  53.3 0.2 copy-done.5
  53.5 12.7 %strips.1 = (f32[512,128]{1,0:T(8,128)}, f32[512,128]{1,0:T(8,128)}, f32[512,128]{1,0:T(8,128)}) custom-call(s32[1]{0:T(128)} %bitcast.odd, s32[24,128]{1,0:T(8,128)} %get-tuple-element.35.codes, f32[3,512,128]{2,1,0:T(8,128)} %get-tuple-element.36.turned, f32[12,2,48,128]{3,2,1,0:T(8,128)} %copy-done.4, f32[12,2,48,128]{3,2,1,0:T(8,128)} %copy-done.5, ...), custom_call_target="tpu_custom_call" | custom-call | tf_op jit(solution)/shard_map/strips/pallas_call | solution.py:662
  66.2 0.7 collective-permute-start.6
  66.9 3.0 %collective-permute-start.7 = (f32[512,128]{1,0:T(8,128)}, f32[512,128]{1,0:T(8,128)S(1)}, u32[]{:S(2)}, u32[]{:S(2)}) collective-permute-start(f32[512,128]{1,0:T(8,128)} %get-tuple-element.59), channel_id=1, source_target_pairs={{0,1},{1,0},{2,3},{3,2},{4,5},{5,4},{6,7},{7,6},{8,9},{9,8},{10,11... | collective-permute-start | bytes 786440 | tf_op jit(solution)/shard_map/ppermute | solution.py:43
  69.9 0.1 broadcast_in_dim.18
  70.0 0.1 broadcast_in_dim.9
  70.1 1.1 %pad_maximum_fusion = (f32[512,128]{1,0:T(8,128)S(1)}, f32[512,128]{1,0:T(8,128)S(1)}) fusion(f32[512,64]{1,0:T(8,128)S(1)} %broadcast_in_dim.18, f32[512,64]{1,0:T(8,128)S(1)} %broadcast_in_dim.9, f32[512,128]{1,0:T(8,128)} %get-tuple-element.57), kind=kLoop, calls=%fused_computation | loop fusion | flops 131072 | bytes 1048576 | tf_op jit(solution)/shard_map/concatenate | solution.py:812
  71.2 0.0 collective-permute-done.6.far
  71.2 0.0 collective-permute-done.7.near
  71.2 0.6 gram.1
  71.8 2.8 %collective-permute-start.8 = (f32[32,128]{1,0:T(8,128)S(1)}, f32[32,128]{1,0:T(8,128)S(1)}, u32[]{:S(2)}, u32[]{:S(2)}) collective-permute-start(f32[32,128]{1,0:T(8,128)S(1)} %get-tuple-element.60), channel_id=1, source_target_pairs={{0,1},{1,0},{2,3},{3,2},{4,5},{5,4},{6,7},{7,6},{8,9},{9,8},{10,11... | collective-permute-start | bytes 49160 | tf_op jit(solution)/shard_map/ppermute | solution.py:51
  74.6 0.8 collective-permute-done.8
  75.5 3.6 %collective-permute-start.10 = (f32[32,128]{1,0:T(8,128)S(1)}, f32[32,128]{1,0:T(8,128)S(1)}, u32[]{:S(2)}, u32[]{:S(2)}) collective-permute-start(f32[32,128]{1,0:T(8,128)S(1)} %add.43), channel_id=1, source_target_pairs={{0,4},{1,5},{2,6},{3,7},{4,0},{5,1},{6,2},{7,3},{8,12},{9,13},{10,... | collective-permute-start | bytes 49160 | tf_op jit(solution)/shard_map/ppermute | solution.py:51
  79.1 3.1 %collective-permute-start.11 = (f32[32,128]{1,0:T(8,128)S(1)}, f32[32,128]{1,0:T(8,128)S(1)}, u32[]{:S(2)}, u32[]{:S(2)}) collective-permute-start(f32[32,128]{1,0:T(8,128)S(1)} %add.43), channel_id=1, source_target_pairs={{0,6},{1,7},{2,4},{3,5},{4,2},{5,3},{6,0},{7,1},{8,14},{9,15},{10,... | collective-permute-start | bytes 49160 | tf_op jit(solution)/shard_map/ppermute | solution.py:51
  82.2 0.8 collective-permute-start.9
  83.0 1.1 %collective-permute-done.11 = f32[32,128]{1,0:T(8,128)S(1)} collective-permute-done((f32[32,128]{1,0:T(8,128)S(1)}, f32[32,128]{1,0:T(8,128)S(1)}, u32[]{:S(2)}, u32[]{:S(2)}) %collective-permute-start.11) | collective-permute-done | bytes 16416 | tf_op jit(solution)/shard_map/ppermute | solution.py:51
  84.0 1.9 %collective-permute-done.9 = f32[32,128]{1,0:T(8,128)S(1)} collective-permute-done((f32[32,128]{1,0:T(8,128)S(1)}, f32[32,128]{1,0:T(8,128)S(1)}, u32[]{:S(2)}, u32[]{:S(2)}) %collective-permute-start.9) | collective-permute-done | bytes 16416 | tf_op jit(solution)/shard_map/ppermute | solution.py:51
  85.9 1.4 %collective-permute-start.12 = (f32[32,128]{1,0:T(8,128)S(1)}, f32[32,128]{1,0:T(8,128)S(1)}, u32[]{:S(2)}, u32[]{:S(2)}) collective-permute-start(f32[32,128]{1,0:T(8,128)S(1)} %add_add_fusion.2), channel_id=1, source_target_pairs={{0,32},{1,33},{2,34},{3,35},{4,36},{5,37},{6,38},{7,39},{8,40},{9,... | collective-permute-start | bytes 49160 | tf_op jit(solution)/shard_map/ppermute | solution.py:51
  87.3 2.7 %collective-permute-start.13 = (f32[32,128]{1,0:T(8,128)S(1)}, f32[32,128]{1,0:T(8,128)S(1)}, u32[]{:S(2)}, u32[]{:S(2)}) collective-permute-start(f32[32,128]{1,0:T(8,128)S(1)} %add_add_fusion.2), channel_id=1, source_target_pairs={{0,64},{1,65},{2,66},{3,67},{4,68},{5,69},{6,70},{7,71},{8,72},{9,... | collective-permute-start | bytes 49160 | tf_op jit(solution)/shard_map/ppermute | solution.py:51
  90.0 0.6 collective-permute-start.14
  90.6 0.0 collective-permute-done.12
  90.6 1.9 %collective-permute-done.13 = f32[32,128]{1,0:T(8,128)S(1)} collective-permute-done((f32[32,128]{1,0:T(8,128)S(1)}, f32[32,128]{1,0:T(8,128)S(1)}, u32[]{:S(2)}, u32[]{:S(2)}) %collective-permute-start.13) | collective-permute-done | bytes 16416 | tf_op jit(solution)/shard_map/ppermute | solution.py:51
  92.5 2.4 %collective-permute-done.14 = f32[32,128]{1,0:T(8,128)S(1)} collective-permute-done((f32[32,128]{1,0:T(8,128)S(1)}, f32[32,128]{1,0:T(8,128)S(1)}, u32[]{:S(2)}, u32[]{:S(2)}) %collective-permute-start.14) | collective-permute-done | bytes 16416 | tf_op jit(solution)/shard_map/ppermute | solution.py:51
  94.9 0.3 collective-permute-start.15
  95.2 3.0 %collective-permute-start.16 = (f32[32,128]{1,0:T(8,128)S(1)}, f32[32,128]{1,0:T(8,128)S(1)}, u32[]{:S(2)}, u32[]{:S(2)}) collective-permute-start(f32[32,128]{1,0:T(8,128)S(1)} %add_add_fusion.1), channel_id=1, source_target_pairs={{0,8},{1,9},{2,10},{3,11},{4,12},{5,13},{6,14},{7,15},{8,0},{9,1},... | collective-permute-start | bytes 49160 | tf_op jit(solution)/shard_map/ppermute | solution.py:51
  98.2 1.4 %collective-permute-start.17 = (f32[32,128]{1,0:T(8,128)S(1)}, f32[32,128]{1,0:T(8,128)S(1)}, u32[]{:S(2)}, u32[]{:S(2)}) collective-permute-start(f32[32,128]{1,0:T(8,128)S(1)} %add_add_fusion.1), channel_id=1, source_target_pairs={{0,24},{1,25},{2,26},{3,27},{4,28},{5,29},{6,30},{7,31},{8,16},{9,... | collective-permute-start | bytes 49160 | tf_op jit(solution)/shard_map/ppermute | solution.py:51
  99.6 0.8 collective-permute-done.16
  100.5 2.7 %collective-permute-done.17 = f32[32,128]{1,0:T(8,128)S(1)} collective-permute-done((f32[32,128]{1,0:T(8,128)S(1)}, f32[32,128]{1,0:T(8,128)S(1)}, u32[]{:S(2)}, u32[]{:S(2)}) %collective-permute-start.17) | collective-permute-done | bytes 16416 | tf_op jit(solution)/shard_map/ppermute | solution.py:51
  103.2 3.0 %factor.1 = (f32[64,1024]{1,0:T(8,128)}, f32[64,64]{1,0:T(8,128)}) custom-call(f32[32,128]{1,0:T(8,128)S(1)} %add_add_fusion.refs_0_, f32[512,128]{1,0:T(8,128)S(1)} %get-tuple-element.61.refs_1_), custom_call_target="tpu_custom_call" | custom-call | tf_op jit(solution)/shard_map/factor/pallas_call | solution.py:769
  (23 shorter events, 0.1 us)
Async XLA Ops:
  2.7 9.1 %collective-permute-start = (f32[248,128]{1,0:T(8,128)}, f32[248,128]{1,0:T(8,128)S(1)}, u32[]{:S(2)}, u32[]{:S(2)}) collective-permute-start(f32[248,128]{1,0:T(8,128)} %get-tuple-element.33), channel_id=1, source_target_pairs={{1,2},{2,1},{3,4},{4,3},{5,6},{6,5},{7,8},{8,7},{9,10},{10,9},{11,... | collective-permute-start | bytes 380936 | tf_op jit(solution)/shard_map/ppermute | solution.py:43
  3.4 8.4 %copy-start.2 = (f32[3,5,8,128]{3,2,1,0:T(8,128)S(1)}, f32[3,5,8,128]{3,2,1,0:T(8,128)}, u32[]{:S(2)}) copy-start(f32[3,5,8,128]{3,2,1,0:T(8,128)} %get-tuple-element.44.west) | copy-start | bytes 184324
  3.4 8.4 %copy-start.3 = (f32[3,5,8,128]{3,2,1,0:T(8,128)S(1)}, f32[3,5,8,128]{3,2,1,0:T(8,128)}, u32[]{:S(2)}) copy-start(f32[3,5,8,128]{3,2,1,0:T(8,128)} %get-tuple-element.45.east) | copy-start | bytes 184324
  3.4 21.1 %copy-start.8 = (f32[1024]{0:T(1024)S(1)}, f32[1024]{0:T(1024)}, u32[]{:S(2)}) copy-start(f32[1024]{0:T(1024)} %param.14) | copy-start | bytes 12292
  3.4 8.4 %collective-permute-start.1 = (f32[248,128]{1,0:T(8,128)}, f32[248,128]{1,0:T(8,128)S(1)}, u32[]{:S(2)}, u32[]{:S(2)}) collective-permute-start(f32[248,128]{1,0:T(8,128)} %get-tuple-element.34), channel_id=1, source_target_pairs={{0,1},{1,0},{2,3},{3,2},{4,5},{5,4},{6,7},{7,6},{8,9},{9,8},{10,11... | collective-permute-start | bytes 380936 | tf_op jit(solution)/shard_map/ppermute | solution.py:43
  11.8 5.2 %copy-start = (f32[248,128]{1,0:T(8,128)}, f32[248,128]{1,0:T(8,128)S(1)}, u32[]{:S(2)}) copy-start(f32[248,128]{1,0:T(8,128)S(1)} %collective-permute-done.far) | copy-start | bytes 380932
  11.9 5.2 %copy-start.1 = (f32[248,128]{1,0:T(8,128)}, f32[248,128]{1,0:T(8,128)S(1)}, u32[]{:S(2)}) copy-start(f32[248,128]{1,0:T(8,128)S(1)} %collective-permute-done.1.near) | copy-start | bytes 380932
  12.0 9.6 %collective-permute-start.2 = (f32[3,5,8,128]{3,2,1,0:T(8,128)S(1)}, f32[3,5,8,128]{3,2,1,0:T(8,128)S(1)}, u32[]{:S(2)}, u32[]{:S(2)}) collective-permute-start(f32[3,5,8,128]{3,2,1,0:T(8,128)S(1)} %get-tuple-element.46), channel_id=1, source_target_pairs={{0,112},{16,32},{32,16},{48,64},{64,48},{80,96},{96,80},{112,0},{1... | collective-permute-start | bytes 184328 | tf_op jit(solution)/shard_map/ppermute | solution.py:43
  17.0 4.5 %collective-permute-start.3 = (f32[3,5,8,128]{3,2,1,0:T(8,128)S(1)}, f32[3,5,8,128]{3,2,1,0:T(8,128)S(1)}, u32[]{:S(2)}, u32[]{:S(2)}) collective-permute-start(f32[3,5,8,128]{3,2,1,0:T(8,128)S(1)} %get-tuple-element.47), channel_id=1, source_target_pairs={{0,16},{16,0},{32,48},{48,32},{64,80},{80,64},{96,112},{112,96},{1... | collective-permute-start | bytes 184328 | tf_op jit(solution)/shard_map/ppermute | solution.py:43
  21.5 3.0 %copy-start.6 = (f32[3,5,8,128]{3,2,1,0:T(8,128)}, f32[3,5,8,128]{3,2,1,0:T(8,128)S(1)}, u32[]{:S(2)}) copy-start(f32[3,5,8,128]{3,2,1,0:T(8,128)S(1)} %collective-permute-done.2.far) | copy-start | bytes 184324
  21.5 3.0 %copy-start.7 = (f32[3,5,8,128]{3,2,1,0:T(8,128)}, f32[3,5,8,128]{3,2,1,0:T(8,128)S(1)}, u32[]{:S(2)}) copy-start(f32[3,5,8,128]{3,2,1,0:T(8,128)S(1)} %collective-permute-done.3.near) | copy-start | bytes 184324
  21.6 30.9 %collective-permute-start.4 = (f32[12,2,48,128]{3,2,1,0:T(8,128)}, f32[12,2,48,128]{3,2,1,0:T(8,128)S(1)}, u32[]{:S(2)}, u32[]{:S(2)}) collective-permute-start(f32[12,2,48,128]{3,2,1,0:T(8,128)} %get-tuple-element.48), channel_id=1, source_target_pairs={{0,112},{16,32},{32,16},{48,64},{64,48},{80,96},{96,80},{112,0},{1... | collective-permute-start | bytes 1769480 | tf_op jit(solution)/shard_map/ppermute | solution.py:43
  23.8 28.7 %collective-permute-start.5 = (f32[12,2,48,128]{3,2,1,0:T(8,128)}, f32[12,2,48,128]{3,2,1,0:T(8,128)S(1)}, u32[]{:S(2)}, u32[]{:S(2)}) collective-permute-start(f32[12,2,48,128]{3,2,1,0:T(8,128)} %get-tuple-element.49), channel_id=1, source_target_pairs={{0,16},{16,0},{32,48},{48,32},{64,80},{80,64},{96,112},{112,96},{1... | collective-permute-start | bytes 1769480 | tf_op jit(solution)/shard_map/ppermute | solution.py:43
  52.5 0.8 copy-start.4
  52.5 1.0 copy-start.5
  66.2 5.1 %collective-permute-start.6 = (f32[512,128]{1,0:T(8,128)}, f32[512,128]{1,0:T(8,128)S(1)}, u32[]{:S(2)}, u32[]{:S(2)}) collective-permute-start(f32[512,128]{1,0:T(8,128)} %get-tuple-element.58), channel_id=1, source_target_pairs={{1,2},{2,1},{3,4},{4,3},{5,6},{6,5},{7,8},{8,7},{9,10},{10,9},{11,... | collective-permute-start | bytes 786440 | tf_op jit(solution)/shard_map/ppermute | solution.py:43
  66.9 4.4 %collective-permute-start.7 = (f32[512,128]{1,0:T(8,128)}, f32[512,128]{1,0:T(8,128)S(1)}, u32[]{:S(2)}, u32[]{:S(2)}) collective-permute-start(f32[512,128]{1,0:T(8,128)} %get-tuple-element.59), channel_id=1, source_target_pairs={{0,1},{1,0},{2,3},{3,2},{4,5},{5,4},{6,7},{7,6},{8,9},{9,8},{10,11... | collective-permute-start | bytes 786440 | tf_op jit(solution)/shard_map/ppermute | solution.py:43
  71.8 3.7 %collective-permute-start.8 = (f32[32,128]{1,0:T(8,128)S(1)}, f32[32,128]{1,0:T(8,128)S(1)}, u32[]{:S(2)}, u32[]{:S(2)}) collective-permute-start(f32[32,128]{1,0:T(8,128)S(1)} %get-tuple-element.60), channel_id=1, source_target_pairs={{0,1},{1,0},{2,3},{3,2},{4,5},{5,4},{6,7},{7,6},{8,9},{9,8},{10,11... | collective-permute-start | bytes 49160 | tf_op jit(solution)/shard_map/ppermute | solution.py:51
  75.5 7.5 %collective-permute-start.10 = (f32[32,128]{1,0:T(8,128)S(1)}, f32[32,128]{1,0:T(8,128)S(1)}, u32[]{:S(2)}, u32[]{:S(2)}) collective-permute-start(f32[32,128]{1,0:T(8,128)S(1)} %add.43), channel_id=1, source_target_pairs={{0,4},{1,5},{2,6},{3,7},{4,0},{5,1},{6,2},{7,3},{8,12},{9,13},{10,... | collective-permute-start | bytes 49160 | tf_op jit(solution)/shard_map/ppermute | solution.py:51
  79.1 4.9 %collective-permute-start.11 = (f32[32,128]{1,0:T(8,128)S(1)}, f32[32,128]{1,0:T(8,128)S(1)}, u32[]{:S(2)}, u32[]{:S(2)}) collective-permute-start(f32[32,128]{1,0:T(8,128)S(1)} %add.43), channel_id=1, source_target_pairs={{0,6},{1,7},{2,4},{3,5},{4,2},{5,3},{6,0},{7,1},{8,14},{9,15},{10,... | collective-permute-start | bytes 49160 | tf_op jit(solution)/shard_map/ppermute | solution.py:51
  82.2 3.7 %collective-permute-start.9 = (f32[32,128]{1,0:T(8,128)S(1)}, f32[32,128]{1,0:T(8,128)S(1)}, u32[]{:S(2)}, u32[]{:S(2)}) collective-permute-start(f32[32,128]{1,0:T(8,128)S(1)} %add.43), channel_id=1, source_target_pairs={{0,2},{1,3},{2,0},{3,1},{4,6},{5,7},{6,4},{7,5},{8,10},{9,11},{10,... | collective-permute-start | bytes 49160 | tf_op jit(solution)/shard_map/ppermute | solution.py:51
  85.9 4.7 %collective-permute-start.12 = (f32[32,128]{1,0:T(8,128)S(1)}, f32[32,128]{1,0:T(8,128)S(1)}, u32[]{:S(2)}, u32[]{:S(2)}) collective-permute-start(f32[32,128]{1,0:T(8,128)S(1)} %add_add_fusion.2), channel_id=1, source_target_pairs={{0,32},{1,33},{2,34},{3,35},{4,36},{5,37},{6,38},{7,39},{8,40},{9,... | collective-permute-start | bytes 49160 | tf_op jit(solution)/shard_map/ppermute | solution.py:51
  87.3 5.2 %collective-permute-start.13 = (f32[32,128]{1,0:T(8,128)S(1)}, f32[32,128]{1,0:T(8,128)S(1)}, u32[]{:S(2)}, u32[]{:S(2)}) collective-permute-start(f32[32,128]{1,0:T(8,128)S(1)} %add_add_fusion.2), channel_id=1, source_target_pairs={{0,64},{1,65},{2,66},{3,67},{4,68},{5,69},{6,70},{7,71},{8,72},{9,... | collective-permute-start | bytes 49160 | tf_op jit(solution)/shard_map/ppermute | solution.py:51
  90.0 4.9 %collective-permute-start.14 = (f32[32,128]{1,0:T(8,128)S(1)}, f32[32,128]{1,0:T(8,128)S(1)}, u32[]{:S(2)}, u32[]{:S(2)}) collective-permute-start(f32[32,128]{1,0:T(8,128)S(1)} %add_add_fusion.2), channel_id=1, source_target_pairs={{0,96},{1,97},{2,98},{3,99},{4,100},{5,101},{6,102},{7,103},{8,104... | collective-permute-start | bytes 49160 | tf_op jit(solution)/shard_map/ppermute | solution.py:51
  94.9 4.7 %collective-permute-start.15 = (f32[32,128]{1,0:T(8,128)S(1)}, f32[32,128]{1,0:T(8,128)S(1)}, u32[]{:S(2)}, u32[]{:S(2)}) collective-permute-start(f32[32,128]{1,0:T(8,128)S(1)} %add_add_fusion.1), channel_id=1, source_target_pairs={{0,16},{1,17},{2,18},{3,19},{4,20},{5,21},{6,22},{7,23},{8,24},{9,... | collective-permute-start | bytes 49160 | tf_op jit(solution)/shard_map/ppermute | solution.py:51
  95.2 5.2 %collective-permute-start.16 = (f32[32,128]{1,0:T(8,128)S(1)}, f32[32,128]{1,0:T(8,128)S(1)}, u32[]{:S(2)}, u32[]{:S(2)}) collective-permute-start(f32[32,128]{1,0:T(8,128)S(1)} %add_add_fusion.1), channel_id=1, source_target_pairs={{0,8},{1,9},{2,10},{3,11},{4,12},{5,13},{6,14},{7,15},{8,0},{9,1},... | collective-permute-start | bytes 49160 | tf_op jit(solution)/shard_map/ppermute | solution.py:51
  98.2 4.9 %collective-permute-start.17 = (f32[32,128]{1,0:T(8,128)S(1)}, f32[32,128]{1,0:T(8,128)S(1)}, u32[]{:S(2)}, u32[]{:S(2)}) collective-permute-start(f32[32,128]{1,0:T(8,128)S(1)} %add_add_fusion.1), channel_id=1, source_target_pairs={{0,24},{1,25},{2,26},{3,27},{4,28},{5,29},{6,30},{7,31},{8,16},{9,... | collective-permute-start | bytes 49160 | tf_op jit(solution)/shard_map/ppermute | solution.py:51

commit v7 on v6

--- a/solution.py
+++ b/solution.py
@@ -46,7 +46,7 @@
 def all_sum(x):
     lats = lax.axis_size("lat")
     size = lats * lax.axis_size("lon")
-    for bits in ((1,), (2, 4), (2 * lats, 4 * lats), (lats, 8)):
+    for bits in ((2, 4), (2 * lats, 4 * lats), (lats, 8), (1,)):
         masks = [bits[0]] if len(bits) == 1 else [bits[0], bits[1], bits[0] | bits[1]]
         terms = [lax.ppermute(x, ("lon", "lat"), [(i, i ^ m) for i in range(size)]) for m in masks]
         for term in terms:

time: 107 us -> 109 us (1.019)
  waiting for transfers between devices: 11.7 us -> 13.1 us
    ppermute x10, waiting for transfers between devices: 11.7 us -> 13.1 us  [all_sum(): lax.ppermute(x, ('lon', 'lat'), [(i, i ^ m) for i in range(size)])]
  transfers between devices with their start and end apart: 18 -> 18, of which waited for: 7 -> 8; matrix products, arithmetic and copies ran while one was open for 1% -> 1% of each run, Pallas kernels for 36% -> 35%
where the time goes in v7:
time: 109 us; the launch traced here: 107 us
  Pallas kernels  56.2 us (52%)
  starting transfers between devices  34.2 us (31%)
  waiting for transfers between devices  13.1 us (12%)
  between operations  1.53 us (1%)
  local copies, waits for them, and re-layouts  1.29 us (1%)
  other arithmetic  1.12 us (1%)
    pallas_call x1, Pallas kernels, transport(): pl.pallas_call(transport_kernel, in_specs=[whole(pltpu.SMEM), whole(pl.AN...  27.9 us
    ppermute x10, starting transfers between devices, all_sum(): lax.ppermute(x, ('lon', 'lat'), [(i, i ^ m) for i in range(size)])  19.5 us
    ppermute x8, starting transfers between devices, swap(): lax.ppermute(x, axis, [(i, j) for i, j in enumerate(partner) if 0 <= j <...  14.7 us
    ppermute x10, waiting for transfers between devices, all_sum(): lax.ppermute(x, ('lon', 'lat'), [(i, i ^ m) for i in range(size)])  13.1 us
    pallas_call x1, Pallas kernels, strips(): pl.pallas_call(strips_kernel, in_specs=[whole(pltpu.SMEM), whole(pltpu.SM...  12.7 us
    pallas_call x1, Pallas kernels, pack_edges(): pl.pallas_call(edges_kernel, grid_spec=pltpu.PrefetchScalarGridSpec(num_s...  5.3 us
    pallas_call x1, Pallas kernels, margins(): pl.pallas_call(margins_kernel, in_specs=[whole(pltpu.SMEM)] + [whole()] *...  4.49 us
    pallas_call x1, Pallas kernels, factor_of(): pl.pallas_call(lambda *refs: factor_kernel(root, *refs), in_specs=[whole(...  3 us
  transfers between devices with their start and end apart: 18, of which 8 were waited for; matrix products, arithmetic and copies ran while one was open for 1% of the time, Pallas kernels for 35%

profile of v7, /device:TPU:0, one launch (start us, length us, event | category | flops | bytes accessed | tf_op | source)
XLA Modules:
  0.0 107.4 jit_solution(2353173303786348151)
XLA Ops:
  0.6 2.1 %pack_lat.1 = (f32[248,128]{1,0:T(8,128)}, f32[248,128]{1,0:T(8,128)}, f32[3,5,8,128]{3,2,1,0:T(8,128)}, f32[3,5,8,128]{3,2,1,0:T(8,128)}) custom-call(s32[1]{0:T(128)} %bitcast.odd, f32[12,36,47]{2,1,0:T(8,128)} %u.3, f32[12,36,47]{2,1,0:T(8,128)} %v.3, f32[12,36,47]{2,1,0:T(8,128)} %mix.3, s32[8,128]{1,0:T(8,128)} %bitcast.7), custom_call_target="tpu_custom_call" | custom-call | tf_op jit(solution)/shard_map/pack_lat/pallas_call | solution.py:93
  2.7 0.7 collective-permute-start
  3.4 0.0 copy-start.8
  3.4 3.1 %collective-permute-start.1 = (f32[248,128]{1,0:T(8,128)}, f32[248,128]{1,0:T(8,128)S(1)}, u32[]{:S(2)}, u32[]{:S(2)}) collective-permute-start(f32[248,128]{1,0:T(8,128)} %get-tuple-element.34), channel_id=1, source_target_pairs={{0,1},{1,0},{2,3},{3,2},{4,5},{5,4},{6,7},{7,6},{8,9},{9,8},{10,11... | collective-permute-start | bytes 380936 | tf_op jit(solution)/shard_map/ppermute | solution.py:43
  6.5 5.3 %pack_edges.1 = (f32[12,2,48,128]{3,2,1,0:T(8,128)}, f32[12,2,48,128]{3,2,1,0:T(8,128)}, f32[12,18,128]{2,1,0:T(8,128)}, f32[3,12,48,128]{3,2,1,0:T(8,128)}) custom-call(s32[1]{0:T(128)} %bitcast.odd, f32[12,36,47,64]{3,2,1,0:T(8,128)} %conc.1, f32[12,36,47,64]{3,2,1,0:T(8,128)} %conc.1, f32[12,36,64]{2,1,0:T(8,128)} %flux.1, f32[12,36,47]{2,1,0:T(8,128)} %u.3, ...), custom_call_target="tpu_custom_call" | custom-call | tf_op jit(solution)/shard_map/pack_edges/pallas_call | solution.py:198
  11.8 0.0 collective-permute-done.far
  11.8 0.0 collective-permute-done.1.near
  11.9 0.1 pack_lon.1
  12.0 5.0 %collective-permute-start.2 = (f32[3,5,8,128]{3,2,1,0:T(8,128)S(1)}, f32[3,5,8,128]{3,2,1,0:T(8,128)S(1)}, u32[]{:S(2)}, u32[]{:S(2)}) collective-permute-start(f32[3,5,8,128]{3,2,1,0:T(8,128)S(1)} %get-tuple-element.46), channel_id=1, source_target_pairs={{0,112},{16,32},{32,16},{48,64},{64,48},{80,96},{96,80},{112,0},{1... | collective-permute-start | bytes 184328 | tf_op jit(solution)/shard_map/ppermute | solution.py:43
  17.0 0.0 collective-permute-start.3
  17.0 4.5 %margins.1 = (f32[3,8,48,128]{3,2,1,0:T(8,128)}, s32[24,128]{1,0:T(8,128)}, f32[3,512,128]{2,1,0:T(8,128)}) custom-call(s32[1]{0:T(128)} %bitcast.odd, f32[248,128]{1,0:T(8,128)} %copy-done, f32[248,128]{1,0:T(8,128)} %copy-done.1, s32[8,128]{1,0:T(8,128)} %bitcast.8), custom_call_target="tpu_custom_call" | custom-call | tf_op jit(solution)/shard_map/margins/pallas_call | solution.py:267
  21.5 0.0 collective-permute-done.2.far
  21.5 0.0 collective-permute-done.3.near
  21.6 2.3 %collective-permute-start.4 = (f32[12,2,48,128]{3,2,1,0:T(8,128)}, f32[12,2,48,128]{3,2,1,0:T(8,128)S(1)}, u32[]{:S(2)}, u32[]{:S(2)}) collective-permute-start(f32[12,2,48,128]{3,2,1,0:T(8,128)} %get-tuple-element.48), channel_id=1, source_target_pairs={{0,112},{16,32},{32,16},{48,64},{64,48},{80,96},{96,80},{112,0},{1... | collective-permute-start | bytes 1769480 | tf_op jit(solution)/shard_map/ppermute | solution.py:43
  23.8 0.0 collective-permute-start.5
  24.5 27.9 %transport.1 = (f32[20,18,48,128]{3,2,1,0:T(8,128)}, bf16[3,960,128]{2,1,0:T(8,128)(2,1)}) custom-call(s32[1]{0:T(128)} %bitcast.odd, f32[12,36,47,64]{3,2,1,0:T(8,128)} %conc.1, f32[12,18,128]{2,1,0:T(8,128)} %get-tuple-element.50.flux, f32[3,12,48,128]{3,2,1,0:T(8,128)} %get-tuple-element.51.own, f32[3,8,48,128]{3,2,1,0:T(8,128)} %get-tuple-element.52.beyond, ...), custom_call_target="tpu_custom_call" | custom-call | tf_op jit(solution)/shard_map/transport/pallas_call | solution.py:527
  52.5 0.0 collective-permute-done.4.edge_far
  52.5 0.0 collective-permute-done.5.edge_near
  52.5 0.8 copy-done.4
  53.3 0.2 copy-done.5
  53.5 12.7 %strips.1 = (f32[512,128]{1,0:T(8,128)}, f32[512,128]{1,0:T(8,128)}, f32[512,128]{1,0:T(8,128)}) custom-call(s32[1]{0:T(128)} %bitcast.odd, s32[24,128]{1,0:T(8,128)} %get-tuple-element.35.codes, f32[3,512,128]{2,1,0:T(8,128)} %get-tuple-element.36.turned, f32[12,2,48,128]{3,2,1,0:T(8,128)} %copy-done.4, f32[12,2,48,128]{3,2,1,0:T(8,128)} %copy-done.5, ...), custom_call_target="tpu_custom_call" | custom-call | tf_op jit(solution)/shard_map/strips/pallas_call | solution.py:662
  66.2 0.7 collective-permute-start.6
  66.9 3.0 %collective-permute-start.7 = (f32[512,128]{1,0:T(8,128)}, f32[512,128]{1,0:T(8,128)S(1)}, u32[]{:S(2)}, u32[]{:S(2)}) collective-permute-start(f32[512,128]{1,0:T(8,128)} %get-tuple-element.59), channel_id=1, source_target_pairs={{0,1},{1,0},{2,3},{3,2},{4,5},{5,4},{6,7},{7,6},{8,9},{9,8},{10,11... | collective-permute-start | bytes 786440 | tf_op jit(solution)/shard_map/ppermute | solution.py:43
  69.9 0.1 broadcast_in_dim.18
  70.0 0.1 broadcast_in_dim.9
  70.1 1.1 %pad_maximum_fusion = (f32[512,128]{1,0:T(8,128)S(1)}, f32[512,128]{1,0:T(8,128)S(1)}) fusion(f32[512,64]{1,0:T(8,128)S(1)} %broadcast_in_dim.18, f32[512,64]{1,0:T(8,128)S(1)} %broadcast_in_dim.9, f32[512,128]{1,0:T(8,128)} %get-tuple-element.57), kind=kLoop, calls=%fused_computation | loop fusion | flops 131072 | bytes 1048576 | tf_op jit(solution)/shard_map/concatenate | solution.py:812
  71.2 0.0 collective-permute-done.6.far
  71.2 0.0 collective-permute-done.7.near
  71.3 0.6 gram.1
  71.8 6.6 %collective-permute-start.10 = (f32[32,128]{1,0:T(8,128)S(1)}, f32[32,128]{1,0:T(8,128)S(1)}, u32[]{:S(2)}, u32[]{:S(2)}) collective-permute-start(f32[32,128]{1,0:T(8,128)S(1)} %get-tuple-element.60), channel_id=1, source_target_pairs={{0,6},{1,7},{2,4},{3,5},{4,2},{5,3},{6,0},{7,1},{8,14},{9,15},{10,... | collective-permute-start | bytes 49160 | tf_op jit(solution)/shard_map/ppermute | solution.py:51
  78.4 0.0 collective-permute-start.8
  78.4 1.6 %collective-permute-start.9 = (f32[32,128]{1,0:T(8,128)S(1)}, f32[32,128]{1,0:T(8,128)S(1)}, u32[]{:S(2)}, u32[]{:S(2)}) collective-permute-start(f32[32,128]{1,0:T(8,128)S(1)} %get-tuple-element.60), channel_id=1, source_target_pairs={{0,4},{1,5},{2,6},{3,7},{4,0},{5,1},{6,2},{7,3},{8,12},{9,13},{10,... | collective-permute-start | bytes 49160 | tf_op jit(solution)/shard_map/ppermute | solution.py:51
  80.0 0.2 collective-permute-done.10
  80.1 2.0 %collective-permute-done.8 = f32[32,128]{1,0:T(8,128)S(1)} collective-permute-done((f32[32,128]{1,0:T(8,128)S(1)}, f32[32,128]{1,0:T(8,128)S(1)}, u32[]{:S(2)}, u32[]{:S(2)}) %collective-permute-start.8) | collective-permute-done | bytes 16416 | tf_op jit(solution)/shard_map/ppermute | solution.py:51
  82.1 1.6 %collective-permute-done.9 = f32[32,128]{1,0:T(8,128)S(1)} collective-permute-done((f32[32,128]{1,0:T(8,128)S(1)}, f32[32,128]{1,0:T(8,128)S(1)}, u32[]{:S(2)}, u32[]{:S(2)}) %collective-permute-start.9) | collective-permute-done | bytes 16416 | tf_op jit(solution)/shard_map/ppermute | solution.py:51
  83.7 1.5 %collective-permute-start.11 = (f32[32,128]{1,0:T(8,128)S(1)}, f32[32,128]{1,0:T(8,128)S(1)}, u32[]{:S(2)}, u32[]{:S(2)}) collective-permute-start(f32[32,128]{1,0:T(8,128)S(1)} %add_add_fusion.2), channel_id=1, source_target_pairs={{0,32},{1,33},{2,34},{3,35},{4,36},{5,37},{6,38},{7,39},{8,40},{9,... | collective-permute-start | bytes 49160 | tf_op jit(solution)/shard_map/ppermute | solution.py:51
  85.3 1.9 %collective-permute-start.12 = (f32[32,128]{1,0:T(8,128)S(1)}, f32[32,128]{1,0:T(8,128)S(1)}, u32[]{:S(2)}, u32[]{:S(2)}) collective-permute-start(f32[32,128]{1,0:T(8,128)S(1)} %add_add_fusion.2), channel_id=1, source_target_pairs={{0,64},{1,65},{2,66},{3,67},{4,68},{5,69},{6,70},{7,71},{8,72},{9,... | collective-permute-start | bytes 49160 | tf_op jit(solution)/shard_map/ppermute | solution.py:51
  87.1 1.3 %collective-permute-start.13 = (f32[32,128]{1,0:T(8,128)S(1)}, f32[32,128]{1,0:T(8,128)S(1)}, u32[]{:S(2)}, u32[]{:S(2)}) collective-permute-start(f32[32,128]{1,0:T(8,128)S(1)} %add_add_fusion.2), channel_id=1, source_target_pairs={{0,96},{1,97},{2,98},{3,99},{4,100},{5,101},{6,102},{7,103},{8,104... | collective-permute-start | bytes 49160 | tf_op jit(solution)/shard_map/ppermute | solution.py:51
  88.4 0.0 collective-permute-done.11
  88.4 2.2 %collective-permute-done.12 = f32[32,128]{1,0:T(8,128)S(1)} collective-permute-done((f32[32,128]{1,0:T(8,128)S(1)}, f32[32,128]{1,0:T(8,128)S(1)}, u32[]{:S(2)}, u32[]{:S(2)}) %collective-permute-start.12) | collective-permute-done | bytes 16416 | tf_op jit(solution)/shard_map/ppermute | solution.py:51
  90.6 1.5 %collective-permute-done.13 = f32[32,128]{1,0:T(8,128)S(1)} collective-permute-done((f32[32,128]{1,0:T(8,128)S(1)}, f32[32,128]{1,0:T(8,128)S(1)}, u32[]{:S(2)}, u32[]{:S(2)}) %collective-permute-start.13) | collective-permute-done | bytes 16416 | tf_op jit(solution)/shard_map/ppermute | solution.py:51
  92.1 0.3 collective-permute-start.14
  92.4 5.9 %collective-permute-start.15 = (f32[32,128]{1,0:T(8,128)S(1)}, f32[32,128]{1,0:T(8,128)S(1)}, u32[]{:S(2)}, u32[]{:S(2)}) collective-permute-start(f32[32,128]{1,0:T(8,128)S(1)} %add_add_fusion.1), channel_id=1, source_target_pairs={{0,8},{1,9},{2,10},{3,11},{4,12},{5,13},{6,14},{7,15},{8,0},{9,1},... | collective-permute-start | bytes 49160 | tf_op jit(solution)/shard_map/ppermute | solution.py:51
  98.3 0.5 collective-permute-start.16
  98.7 1.3 %collective-permute-done.15 = f32[32,128]{1,0:T(8,128)S(1)} collective-permute-done((f32[32,128]{1,0:T(8,128)S(1)}, f32[32,128]{1,0:T(8,128)S(1)}, u32[]{:S(2)}, u32[]{:S(2)}) %collective-permute-start.15) | collective-permute-done | bytes 16416 | tf_op jit(solution)/shard_map/ppermute | solution.py:51
  100.1 3.1 %collective-permute-done.16 = f32[32,128]{1,0:T(8,128)S(1)} collective-permute-done((f32[32,128]{1,0:T(8,128)S(1)}, f32[32,128]{1,0:T(8,128)S(1)}, u32[]{:S(2)}, u32[]{:S(2)}) %collective-permute-start.16) | collective-permute-done | bytes 16416 | tf_op jit(solution)/shard_map/ppermute | solution.py:51
  103.2 1.2 %collective-permute-done.17 = f32[32,128]{1,0:T(8,128)S(1)} collective-permute-done((f32[32,128]{1,0:T(8,128)S(1)}, f32[32,128]{1,0:T(8,128)S(1)}, u32[]{:S(2)}, u32[]{:S(2)}) %collective-permute-start.17) | collective-permute-done | bytes 16416 | tf_op jit(solution)/shard_map/ppermute | solution.py:51
  104.4 3.0 %factor.1 = (f32[64,1024]{1,0:T(8,128)}, f32[64,64]{1,0:T(8,128)}) custom-call(f32[32,128]{1,0:T(8,128)S(1)} %add.52.refs_0_, f32[512,128]{1,0:T(8,128)S(1)} %get-tuple-element.61.refs_1_), custom_call_target="tpu_custom_call" | custom-call | tf_op jit(solution)/shard_map/factor/pallas_call | solution.py:769
  (23 shorter events, 0.1 us)
Async XLA Ops:
  2.7 9.1 %collective-permute-start = (f32[248,128]{1,0:T(8,128)}, f32[248,128]{1,0:T(8,128)S(1)}, u32[]{:S(2)}, u32[]{:S(2)}) collective-permute-start(f32[248,128]{1,0:T(8,128)} %get-tuple-element.33), channel_id=1, source_target_pairs={{1,2},{2,1},{3,4},{4,3},{5,6},{6,5},{7,8},{8,7},{9,10},{10,9},{11,... | collective-permute-start | bytes 380936 | tf_op jit(solution)/shard_map/ppermute | solution.py:43
  3.4 8.4 %copy-start.2 = (f32[3,5,8,128]{3,2,1,0:T(8,128)S(1)}, f32[3,5,8,128]{3,2,1,0:T(8,128)}, u32[]{:S(2)}) copy-start(f32[3,5,8,128]{3,2,1,0:T(8,128)} %get-tuple-element.44.west) | copy-start | bytes 184324
  3.4 8.4 %copy-start.3 = (f32[3,5,8,128]{3,2,1,0:T(8,128)S(1)}, f32[3,5,8,128]{3,2,1,0:T(8,128)}, u32[]{:S(2)}) copy-start(f32[3,5,8,128]{3,2,1,0:T(8,128)} %get-tuple-element.45.east) | copy-start | bytes 184324
  3.4 21.1 %copy-start.8 = (f32[1024]{0:T(1024)S(1)}, f32[1024]{0:T(1024)}, u32[]{:S(2)}) copy-start(f32[1024]{0:T(1024)} %param.14) | copy-start | bytes 12292
  3.4 8.4 %collective-permute-start.1 = (f32[248,128]{1,0:T(8,128)}, f32[248,128]{1,0:T(8,128)S(1)}, u32[]{:S(2)}, u32[]{:S(2)}) collective-permute-start(f32[248,128]{1,0:T(8,128)} %get-tuple-element.34), channel_id=1, source_target_pairs={{0,1},{1,0},{2,3},{3,2},{4,5},{5,4},{6,7},{7,6},{8,9},{9,8},{10,11... | collective-permute-start | bytes 380936 | tf_op jit(solution)/shard_map/ppermute | solution.py:43
  11.8 5.2 %copy-start = (f32[248,128]{1,0:T(8,128)}, f32[248,128]{1,0:T(8,128)S(1)}, u32[]{:S(2)}) copy-start(f32[248,128]{1,0:T(8,128)S(1)} %collective-permute-done.far) | copy-start | bytes 380932
  11.9 5.2 %copy-start.1 = (f32[248,128]{1,0:T(8,128)}, f32[248,128]{1,0:T(8,128)S(1)}, u32[]{:S(2)}) copy-start(f32[248,128]{1,0:T(8,128)S(1)} %collective-permute-done.1.near) | copy-start | bytes 380932
  12.0 9.6 %collective-permute-start.2 = (f32[3,5,8,128]{3,2,1,0:T(8,128)S(1)}, f32[3,5,8,128]{3,2,1,0:T(8,128)S(1)}, u32[]{:S(2)}, u32[]{:S(2)}) collective-permute-start(f32[3,5,8,128]{3,2,1,0:T(8,128)S(1)} %get-tuple-element.46), channel_id=1, source_target_pairs={{0,112},{16,32},{32,16},{48,64},{64,48},{80,96},{96,80},{112,0},{1... | collective-permute-start | bytes 184328 | tf_op jit(solution)/shard_map/ppermute | solution.py:43
  17.0 4.5 %collective-permute-start.3 = (f32[3,5,8,128]{3,2,1,0:T(8,128)S(1)}, f32[3,5,8,128]{3,2,1,0:T(8,128)S(1)}, u32[]{:S(2)}, u32[]{:S(2)}) collective-permute-start(f32[3,5,8,128]{3,2,1,0:T(8,128)S(1)} %get-tuple-element.47), channel_id=1, source_target_pairs={{0,16},{16,0},{32,48},{48,32},{64,80},{80,64},{96,112},{112,96},{1... | collective-permute-start | bytes 184328 | tf_op jit(solution)/shard_map/ppermute | solution.py:43
  21.5 3.0 %copy-start.6 = (f32[3,5,8,128]{3,2,1,0:T(8,128)}, f32[3,5,8,128]{3,2,1,0:T(8,128)S(1)}, u32[]{:S(2)}) copy-start(f32[3,5,8,128]{3,2,1,0:T(8,128)S(1)} %collective-permute-done.2.far) | copy-start | bytes 184324
  21.5 3.0 %copy-start.7 = (f32[3,5,8,128]{3,2,1,0:T(8,128)}, f32[3,5,8,128]{3,2,1,0:T(8,128)S(1)}, u32[]{:S(2)}) copy-start(f32[3,5,8,128]{3,2,1,0:T(8,128)S(1)} %collective-permute-done.3.near) | copy-start | bytes 184324
  21.6 30.9 %collective-permute-start.4 = (f32[12,2,48,128]{3,2,1,0:T(8,128)}, f32[12,2,48,128]{3,2,1,0:T(8,128)S(1)}, u32[]{:S(2)}, u32[]{:S(2)}) collective-permute-start(f32[12,2,48,128]{3,2,1,0:T(8,128)} %get-tuple-element.48), channel_id=1, source_target_pairs={{0,112},{16,32},{32,16},{48,64},{64,48},{80,96},{96,80},{112,0},{1... | collective-permute-start | bytes 1769480 | tf_op jit(solution)/shard_map/ppermute | solution.py:43
  23.8 28.7 %collective-permute-start.5 = (f32[12,2,48,128]{3,2,1,0:T(8,128)}, f32[12,2,48,128]{3,2,1,0:T(8,128)S(1)}, u32[]{:S(2)}, u32[]{:S(2)}) collective-permute-start(f32[12,2,48,128]{3,2,1,0:T(8,128)} %get-tuple-element.49), channel_id=1, source_target_pairs={{0,16},{16,0},{32,48},{48,32},{64,80},{80,64},{96,112},{112,96},{1... | collective-permute-start | bytes 1769480 | tf_op jit(solution)/shard_map/ppermute | solution.py:43
  52.5 0.8 copy-start.4
  52.5 1.0 copy-start.5
  66.2 5.1 %collective-permute-start.6 = (f32[512,128]{1,0:T(8,128)}, f32[512,128]{1,0:T(8,128)S(1)}, u32[]{:S(2)}, u32[]{:S(2)}) collective-permute-start(f32[512,128]{1,0:T(8,128)} %get-tuple-element.58), channel_id=1, source_target_pairs={{1,2},{2,1},{3,4},{4,3},{5,6},{6,5},{7,8},{8,7},{9,10},{10,9},{11,... | collective-permute-start | bytes 786440 | tf_op jit(solution)/shard_map/ppermute | solution.py:43
  66.9 4.4 %collective-permute-start.7 = (f32[512,128]{1,0:T(8,128)}, f32[512,128]{1,0:T(8,128)S(1)}, u32[]{:S(2)}, u32[]{:S(2)}) collective-permute-start(f32[512,128]{1,0:T(8,128)} %get-tuple-element.59), channel_id=1, source_target_pairs={{0,1},{1,0},{2,3},{3,2},{4,5},{5,4},{6,7},{7,6},{8,9},{9,8},{10,11... | collective-permute-start | bytes 786440 | tf_op jit(solution)/shard_map/ppermute | solution.py:43
  71.8 8.3 %collective-permute-start.10 = (f32[32,128]{1,0:T(8,128)S(1)}, f32[32,128]{1,0:T(8,128)S(1)}, u32[]{:S(2)}, u32[]{:S(2)}) collective-permute-start(f32[32,128]{1,0:T(8,128)S(1)} %get-tuple-element.60), channel_id=1, source_target_pairs={{0,6},{1,7},{2,4},{3,5},{4,2},{5,3},{6,0},{7,1},{8,14},{9,15},{10,... | collective-permute-start | bytes 49160 | tf_op jit(solution)/shard_map/ppermute | solution.py:51
  78.4 3.7 %collective-permute-start.8 = (f32[32,128]{1,0:T(8,128)S(1)}, f32[32,128]{1,0:T(8,128)S(1)}, u32[]{:S(2)}, u32[]{:S(2)}) collective-permute-start(f32[32,128]{1,0:T(8,128)S(1)} %get-tuple-element.60), channel_id=1, source_target_pairs={{0,2},{1,3},{2,0},{3,1},{4,6},{5,7},{6,4},{7,5},{8,10},{9,11},{10,... | collective-permute-start | bytes 49160 | tf_op jit(solution)/shard_map/ppermute | solution.py:51
  78.4 5.3 %collective-permute-start.9 = (f32[32,128]{1,0:T(8,128)S(1)}, f32[32,128]{1,0:T(8,128)S(1)}, u32[]{:S(2)}, u32[]{:S(2)}) collective-permute-start(f32[32,128]{1,0:T(8,128)S(1)} %get-tuple-element.60), channel_id=1, source_target_pairs={{0,4},{1,5},{2,6},{3,7},{4,0},{5,1},{6,2},{7,3},{8,12},{9,13},{10,... | collective-permute-start | bytes 49160 | tf_op jit(solution)/shard_map/ppermute | solution.py:51
  83.7 4.7 %collective-permute-start.11 = (f32[32,128]{1,0:T(8,128)S(1)}, f32[32,128]{1,0:T(8,128)S(1)}, u32[]{:S(2)}, u32[]{:S(2)}) collective-permute-start(f32[32,128]{1,0:T(8,128)S(1)} %add_add_fusion.2), channel_id=1, source_target_pairs={{0,32},{1,33},{2,34},{3,35},{4,36},{5,37},{6,38},{7,39},{8,40},{9,... | collective-permute-start | bytes 49160 | tf_op jit(solution)/shard_map/ppermute | solution.py:51
  85.3 5.3 %collective-permute-start.12 = (f32[32,128]{1,0:T(8,128)S(1)}, f32[32,128]{1,0:T(8,128)S(1)}, u32[]{:S(2)}, u32[]{:S(2)}) collective-permute-start(f32[32,128]{1,0:T(8,128)S(1)} %add_add_fusion.2), channel_id=1, source_target_pairs={{0,64},{1,65},{2,66},{3,67},{4,68},{5,69},{6,70},{7,71},{8,72},{9,... | collective-permute-start | bytes 49160 | tf_op jit(solution)/shard_map/ppermute | solution.py:51
  87.1 4.9 %collective-permute-start.13 = (f32[32,128]{1,0:T(8,128)S(1)}, f32[32,128]{1,0:T(8,128)S(1)}, u32[]{:S(2)}, u32[]{:S(2)}) collective-permute-start(f32[32,128]{1,0:T(8,128)S(1)} %add_add_fusion.2), channel_id=1, source_target_pairs={{0,96},{1,97},{2,98},{3,99},{4,100},{5,101},{6,102},{7,103},{8,104... | collective-permute-start | bytes 49160 | tf_op jit(solution)/shard_map/ppermute | solution.py:51
  92.1 6.6 %collective-permute-start.14 = (f32[32,128]{1,0:T(8,128)S(1)}, f32[32,128]{1,0:T(8,128)S(1)}, u32[]{:S(2)}, u32[]{:S(2)}) collective-permute-start(f32[32,128]{1,0:T(8,128)S(1)} %add_add_fusion.1), channel_id=1, source_target_pairs={{0,16},{1,17},{2,18},{3,19},{4,20},{5,21},{6,22},{7,23},{8,24},{9,... | collective-permute-start | bytes 49160 | tf_op jit(solution)/shard_map/ppermute | solution.py:51
  92.4 7.7 %collective-permute-start.15 = (f32[32,128]{1,0:T(8,128)S(1)}, f32[32,128]{1,0:T(8,128)S(1)}, u32[]{:S(2)}, u32[]{:S(2)}) collective-permute-start(f32[32,128]{1,0:T(8,128)S(1)} %add_add_fusion.1), channel_id=1, source_target_pairs={{0,8},{1,9},{2,10},{3,11},{4,12},{5,13},{6,14},{7,15},{8,0},{9,1},... | collective-permute-start | bytes 49160 | tf_op jit(solution)/shard_map/ppermute | solution.py:51
  98.3 4.9 %collective-permute-start.16 = (f32[32,128]{1,0:T(8,128)S(1)}, f32[32,128]{1,0:T(8,128)S(1)}, u32[]{:S(2)}, u32[]{:S(2)}) collective-permute-start(f32[32,128]{1,0:T(8,128)S(1)} %add_add_fusion.1), channel_id=1, source_target_pairs={{0,24},{1,25},{2,26},{3,27},{4,28},{5,29},{6,30},{7,31},{8,16},{9,... | collective-permute-start | bytes 49160 | tf_op jit(solution)/shard_map/ppermute | solution.py:51
  103.2 1.2 %collective-permute-start.17 = (f32[32,128]{1,0:T(8,128)S(1)}, f32[32,128]{1,0:T(8,128)S(1)}, u32[]{:S(2)}, u32[]{:S(2)}) collective-permute-start(f32[32,128]{1,0:T(8,128)S(1)} %add_add_fusion), channel_id=1, source_target_pairs={{0,1},{1,0},{2,3},{3,2},{4,5},{5,4},{6,7},{7,6},{8,9},{9,8},{10,11... | collective-permute-start | bytes 49160 | tf_op jit(solution)/shard_map/ppermute | solution.py:51
